TPU v7x, 32 devices: a whole 2x2x4 slice. The times are simulated.
32 devices in a mesh: groups: 2 (over y), section: 8 (over z, x), tensor: 2 (over core).
Axes of the slice: x: 2, y: 2, z: 4, core: 2. Of those that a mesh axis runs over, the one named last changes fastest.
Arguments:
- text_embed: bfloat16 [4096, 8192], P(('groups', 'section'), 'tensor'), parts along dimension 0, may hold values from -6 to 6
- image_embed: bfloat16 [4096, 8192], P(('groups', 'section'), 'tensor'), parts along dimension 0, may hold values from -6 to 6
- image_count: int32 [16], P(('groups', 'section')), parts along dimension 0, may hold values from 64 to 256, as said below
- prompt_len: int32 [16], P(('groups', 'section')), parts along dimension 0, may hold values from 64 to 256, as said below
- embed_target: int32 [4096], P(('groups', 'section')), parts along dimension 0, may hold values from -1 to 2047, as said below
- kv_weight: bfloat16 [8192, 1024], P('section', 'tensor'), may hold values from -0.0625 to 0.0625
- kv_bias: float32 [1024], P('tensor'), may hold values from -3 to 3
- norm_gain: float32 [8192], replicated, may hold values from 0.25 to 1.75
- queries: bfloat16 [16, 4096], P(('groups', 'section'), 'tensor'), parts along dimension 0, may hold values from -240 to 240
- old_pool: bfloat16 [768, 4, 1024], P(('groups', 'section'), None, 'tensor'), parts along dimension 0, may hold values from -6 to 6
- pool_owner: int32 [768], P(('groups', 'section')), parts along dimension 0, may hold values from -1 to 7, as said below
- pool_fill: int32 [768], P(('groups', 'section')), parts along dimension 0, may hold values from 0 to 4, as said below
- block_owner: int32 [1024], P(('groups', 'section')), parts along dimension 0, may hold values from -1 to 7, as said below
Outputs:
- decode_out: bfloat16 [16, 4096], P(('groups', 'section'), 'tensor'), parts along dimension 0
- fresh_cache: bfloat16 [4096, 1024], P(('groups', 'section'), 'tensor'), parts along dimension 0
There are 2 independent parts, one for each index of `groups`. A program takes and returns all parts, laid end to end along the dimension named above; an argument that names none is the same for every part. Nothing has to cross between parts.
Inputs may be any that keep to these rules, and one draw needn't show every extreme that they name: `image_count`: some prefill index has 256 image tokens. `prompt_len`: at least the index's image_count; some index reaches 256. `embed_target`: prefill index times 256 plus position, or -1 for an unused row; every position below its index's image_count is named by exactly one encode row; at most 32 rows of one encode index name one prefill index, and some pairs reach 32 in every draw. `block_owner`: -1 exactly for blocks wholly at or past prompt_len; at most 8 blocks of one prefill index go to one decode index, reached in every draw. `pool_owner`: -1 for an unused block. `pool_fill`: 0 exactly for unused blocks, 1 or more for used ones.
All inputs are finite; a program needn't handle non-finite values.
Results may differ from a plain program's by a relative error of at most 0.012.
The roundings to bfloat16 on the way count: a program that leaves them out, or rounds other values in their place, can miss the bound.
Values may be sent and summed in bfloat16 or wider, within the bound.
No kernel may reach another device: no remote copies, remote signals or barrier semaphores. Data moves between devices by JAX's collectives and lax.ppermute only.
A program may use at most 64 MiB of HBM per device.

v0:
```python
import jax
import jax.numpy as jnp
from jax import lax
from jax.sharding import PartitionSpec as P

HQ = 32
KVH = 4
HD = 128


def normalize(rows, norm_gain):
    values = rows.astype(jnp.float32)
    factor = lax.rsqrt(jnp.mean(values * values, axis=-1, keepdims=True) + 1e-06)
    return (values * factor * norm_gain[None, :]).astype(jnp.bfloat16)


def project(normed, kv_weight, kv_bias):
    whole_weight = lax.all_gather(kv_weight, "section", axis=0, tiled=True)
    summed = jnp.dot(normed, whole_weight, preferred_element_type=jnp.float32)
    return (summed + kv_bias[None, :]).astype(jnp.bfloat16)


def ranks_by_target(targets, valid, sections):
    hits = (
        (targets[:, None] == jnp.arange(sections, dtype=jnp.int32)[None, :]) & valid[:, None]
    ).astype(jnp.int32)
    return jnp.sum(hits * (jnp.cumsum(hits, axis=0) - 1), axis=1)


def shards(
    text_embed,
    image_embed,
    image_count,
    prompt_len,
    embed_target,
    kv_weight,
    kv_bias,
    norm_gain,
    queries,
    old_pool,
    pool_owner,
    pool_fill,
    block_owner,
):
    sections = lax.axis_size("section")
    rows = text_embed.shape[0]
    per_pair = rows // sections
    valid = embed_target >= 0
    destination = jnp.where(valid, embed_target // rows, 0)
    slot_rank = ranks_by_target(destination, valid, sections)
    send_slot = jnp.where(valid, destination * per_pair + slot_rank, sections * per_pair)
    send_position = (
        jnp.full((sections * per_pair,), -1, jnp.int32)
        .at[send_slot]
        .set(embed_target % rows, mode="drop")
    )
    image_limit = image_count[0]
    outgoing = (
        jnp.zeros((sections * per_pair, image_embed.shape[1]), jnp.bfloat16)
        .at[send_slot]
        .set(image_embed, mode="drop")
    )
    arrived, arrived_position = (
        lax.all_to_all(
            outgoing.reshape(sections, per_pair, -1),
            "section",
            split_axis=0,
            concat_axis=0,
            tiled=True,
        ),
        lax.all_to_all(
            send_position.reshape(sections, per_pair),
            "section",
            split_axis=0,
            concat_axis=0,
            tiled=True,
        ),
    )
    width = arrived.shape[-1]
    landing = arrived_position.reshape(-1)
    landing = jnp.where(landing >= 0, landing, rows)
    placed = (
        jnp.zeros((rows, width), arrived.dtype)
        .at[landing]
        .set(arrived.reshape(-1, width), mode="drop")
    )
    filled = jnp.zeros((rows,), jnp.bool_).at[landing].set(True, mode="drop")
    keep = filled & (jnp.arange(rows, dtype=jnp.int32) < image_limit)
    placed, keep = (placed, keep)
    assembled = jnp.where(keep[:, None], placed, text_embed)
    whole = lax.all_gather(assembled, "tensor", axis=1, tiled=True)
    key_value = project(normalize(whole, norm_gain), kv_weight, kv_bias)
    width = key_value.shape[1]
    block_rows = old_pool.shape[1]
    blocks_count = block_owner.shape[0]
    per_link = (blocks_count + sections - 1) // sections
    live = block_owner >= 0
    target_index = jnp.where(live, block_owner, 0)
    block_rank = ranks_by_target(target_index, live, sections)
    link_slot = jnp.where(live, target_index * per_link + block_rank, sections * per_link)
    block_data = key_value.reshape(blocks_count, block_rows * width)
    valid_rows = jnp.clip(
        prompt_len[0] - jnp.arange(blocks_count, dtype=jnp.int32) * block_rows, 0, block_rows
    )
    out_blocks = (
        jnp.zeros((sections * per_link, block_rows * width), jnp.bfloat16)
        .at[link_slot]
        .set(block_data, mode="drop")
    )
    out_valid = (
        jnp.zeros((sections * per_link,), jnp.int32).at[link_slot].set(valid_rows, mode="drop")
    )
    fresh, fresh_valid = (
        lax.all_to_all(
            out_blocks.reshape(sections, per_link, -1),
            "section",
            split_axis=0,
            concat_axis=0,
            tiled=True,
        ),
        lax.all_to_all(
            out_valid.reshape(sections, per_link),
            "section",
            split_axis=0,
            concat_axis=0,
            tiled=True,
        ),
    )
    fresh_rows = fresh.reshape(sections * per_link * block_rows, width)
    heads_local = width // (2 * HD)
    group = HQ // KVH
    scale = HD ** (-0.5)
    every_query = lax.all_gather(queries, "section", axis=0, tiled=True)
    query_heads = every_query.reshape(sections, heads_local, group, HD)
    fresh_keys = fresh_rows.reshape(sections, per_link * block_rows, heads_local, 2, HD)
    fresh_scores = (
        jnp.einsum(
            "phgd,pkhd->phgk",
            query_heads,
            fresh_keys[:, :, :, 0, :],
            preferred_element_type=jnp.float32,
        )
        * scale
    )
    row_in_block = jnp.arange(per_link * block_rows, dtype=jnp.int32) % block_rows
    fresh_mask = row_in_block[None, :] < jnp.repeat(fresh_valid, block_rows, axis=1)
    fresh_scores = jnp.where(fresh_mask[:, None, None, :], fresh_scores, -jnp.inf)
    pool_count = old_pool.shape[0]
    safe_owner = jnp.where(pool_owner >= 0, pool_owner, 0)
    block_query = query_heads[safe_owner]
    pool_keys = old_pool.reshape(pool_count, block_rows, heads_local, 2, HD)
    old_scores = (
        jnp.einsum(
            "bhgd,bkhd->bhgk",
            block_query,
            pool_keys[:, :, :, 0, :],
            preferred_element_type=jnp.float32,
        )
        * scale
    )
    old_mask = (jnp.arange(block_rows, dtype=jnp.int32)[None, :] < pool_fill[:, None]) & (
        pool_owner >= 0
    )[:, None]
    old_scores = jnp.where(old_mask[:, None, None, :], old_scores, -jnp.inf)
    onehot = pool_owner[None, :] == jnp.arange(sections, dtype=jnp.int32)[:, None]
    block_top = jnp.max(old_scores, axis=-1)
    old_top = jnp.max(jnp.where(onehot[:, :, None, None], block_top[None], -jnp.inf), axis=1)
    top = jnp.maximum(jnp.maximum(jnp.max(fresh_scores, axis=-1), old_top), -1e30)
    fresh_expo = jnp.exp(fresh_scores - top[..., None])
    old_expo = jnp.exp(old_scores - top[safe_owner][..., None])
    selector = onehot.astype(jnp.float32)
    total = jnp.sum(fresh_expo, axis=-1) + jnp.einsum(
        "rb,bhg->rhg", selector, jnp.sum(old_expo, axis=-1), precision=lax.Precision.HIGHEST
    )
    fresh_acc = jnp.einsum(
        "phgk,pkhd->phgd",
        fresh_expo.astype(jnp.bfloat16),
        fresh_keys[:, :, :, 1, :],
        preferred_element_type=jnp.float32,
    )
    block_acc = jnp.einsum(
        "bhgk,bkhd->bhgd",
        old_expo.astype(jnp.bfloat16),
        pool_keys[:, :, :, 1, :],
        preferred_element_type=jnp.float32,
    )
    acc = fresh_acc + jnp.einsum(
        "rb,bhgd->rhgd", selector, block_acc, precision=lax.Precision.HIGHEST
    )
    best = lax.pmax(top, "section")
    factor = jnp.exp(top - best)
    own_total, own_acc = (
        lax.psum_scatter(total * factor, "section", scatter_dimension=0, tiled=True),
        lax.psum_scatter(acc * factor[..., None], "section", scatter_dimension=0, tiled=True),
    )
    result = own_acc / own_total[..., None]
    return (result.astype(jnp.bfloat16).reshape(1, -1), fresh_rows)


def solution(mesh):
    return jax.shard_map(
        shards,
        mesh=mesh,
        in_specs=(
            P(("groups", "section"), "tensor"),
            P(("groups", "section"), "tensor"),
            P(("groups", "section")),
            P(("groups", "section")),
            P(("groups", "section")),
            P("section", "tensor"),
            P("tensor"),
            P(),
            P(("groups", "section"), "tensor"),
            P(("groups", "section"), None, "tensor"),
            P(("groups", "section")),
            P(("groups", "section")),
            P(("groups", "section")),
        ),
        out_specs=(P(("groups", "section"), "tensor"), P(("groups", "section"), "tensor")),
        check_vma=False,
    )
```

profile of v0, /device:TPU:0, one launch (start us, length us, event | category | flops | bytes accessed | tf_op | source)
XLA Modules:
  0.0 339.5 jit_solution(16879232226946857925)
XLA Ops:
  8.8 1.4 scatter_custom_fusion.1
  10.9 7.3 %all-to-all-start.1 = ((s32[8,1,32]{2,1,0:T(1,128)}), s32[8,1,32]{2,1,0:T(1,128)S(1)}, u32[]{:S(2)}, u32[]{:S(2)}) async-start(s32[8,1,32]{2,1,0:T(1,128)} %all_to_all.23), calls=%async_computation.1 | async-start | bytes 8192 | tf_op jit(solution)/shard_map/all_to_all | solution.py:71
  18.1 6.0 %scatter_custom_fusion.3 = bf16[256,4096]{1,0:T(8,128)(2,1)} fusion(s32[256]{0:T(256)S(1)} %compare_select_fusion.2, bf16[256,4096]{1,0:T(8,128)(2,1)} %param.14, bf16[]{:T(256)} %constant.77.clone.1), kind=kCustom, calls=%fused_computation.30 | custom fusion | bytes 2097664 | tf_op jit(solution)/shard_map/scatter | solution.py:61
  24.5 5.6 %all-to-all-start.2 = ((bf16[8,32,4096]{2,1,0:T(8,128)(2,1)}), bf16[8,32,4096]{2,1,0:T(8,128)(2,1)S(1)}, u32[]{:S(2)}, u32[]{:S(2)}) async-start(bf16[8,32,4096]{2,1,0:T(8,128)(2,1)} %bitcast.10), calls=%async_computation.2 | async-start | bytes 4194304 | tf_op jit(solution)/shard_map/all_to_all | solution.py:64
  32.1 1.5 scatter_custom_fusion.2
  33.6 44.2 %all-to-all-done.2 = bf16[8,32,4096]{2,1,0:T(8,128)(2,1)S(1)} async-done(((bf16[8,32,4096]{2,1,0:T(8,128)(2,1)}), bf16[8,32,4096]{2,1,0:T(8,128)(2,1)S(1)}, u32[]{:S(2)}, u32[]{:S(2)}) %all-to-all-start.2) | async-done | bytes 2097184 | tf_op jit(solution)/shard_map/all_to_all | solution.py:64
  77.8 1.3 copy-done
  79.2 5.1 %scatter_custom_fusion.4 = bf16[256,4096]{1,0:T(8,128)(2,1)S(1)} fusion(s32[256]{0:T(256)S(1)} %bitcast.77, bf16[256,4096]{1,0:T(8,128)(2,1)} %bitcast.65, bf16[]{:T(256)} %constant.77.clone.1), kind=kCustom, calls=%fused_computation.28 | custom fusion | bytes 2097664 | tf_op jit(solution)/shard_map/scatter | solution.py:85
  84.2 3.2 broadcast_select_fusion
  89.4 0.8 scatter_custom_fusion
  90.8 3.6 %all-to-all-start = ((s32[8,1,8]{2,1,0:T(1,128)}), s32[8,1,8]{2,1,0:T(1,128)S(1)}, u32[]{:S(2)}, u32[]{:S(2)}) async-start(s32[8,1,8]{2,1,0:T(1,128)} %bitcast.1), calls=%async_computation | async-start | bytes 8192 | tf_op jit(solution)/shard_map/all_to_all | solution.py:121
  94.5 31.6 %all-gather = bf16[8,1,2048]{2,1,0:T(2,128)(2,1)S(1)} all-gather(bf16[1,1,2048]{2,1,0:T(2,128)(2,1)S(1)} %bitcast.73), channel_id=1, replica_groups=mesh['groups'=2,'section'=8,'tensor'=2] {'section'}, dimensions={0}, use_global_device_ids=true | all-gather | bytes 36864 | tf_op jit(solution)/shard_map/all_gather | solution.py:133
  127.8 3.1 fusion
  130.9 97.9 %all-gather.6.cloned.1.call-done = bf16[8192,512]{1,0:T(8,128)(2,1)} async-done(((bf16[1024,512]{1,0:T(8,128)(2,1)}), bf16[8192,512]{1,0:T(8,128)(2,1)}) %all-gather.6.cloned.1.call-update) | async-done | bytes 8388624 | tf_op jit(solution)/shard_map/all_gather | solution.py:18
  228.8 7.0 %fusion.10 = bf16[256,512]{1,0:T(8,128)(2,1)S(1)} fusion(bf16[8192,512]{1,0:T(8,128)(2,1)} %all-gather.6.cloned.1.call-done, bf16[256,8192]{1,0:T(8,128)(2,1)} %all-gather.4.cloned.1.call-done, f32[8192]{0:T(1024)S(1)} %copy-done.5, f32[256]{0:T(256)S(1)} %add_rsqrt_fusion, f32[512]{0:T(512)S(1)} %copy-done.6), kind=kOutput, calls=%fused_computation.18 | convolution fusion | flops 2156134400 | bytes 12880896 | tf_op jit(solution)/shard_map/dot_general | solution.py:19
  236.0 1.7 scatter_custom_fusion.5
  237.7 3.4 %all-to-all-start.3 = ((bf16[8,8,2048]{2,1,0:T(8,128)(2,1)}), bf16[8,8,2048]{2,1,0:T(8,128)(2,1)S(1)}, u32[]{:S(2)}, u32[]{:S(2)}) async-start(bf16[8,8,2048]{2,1,0:T(8,128)(2,1)} %bitcast.12), calls=%async_computation.3 | async-start | bytes 524288 | tf_op jit(solution)/shard_map/all_to_all | solution.py:114
  242.2 7.6 %all-to-all-done.3 = bf16[8,8,2048]{2,1,0:T(8,128)(2,1)S(1)} async-done(((bf16[8,8,2048]{2,1,0:T(8,128)(2,1)}), bf16[8,8,2048]{2,1,0:T(8,128)(2,1)S(1)}, u32[]{:S(2)}, u32[]{:S(2)}) %all-to-all-start.3) | async-done | bytes 262176 | tf_op jit(solution)/shard_map/all_to_all | solution.py:114
  250.7 19.6 %pmax.7 = f32[8,2,8]{2,0,1:T(8,128)S(1)} all-reduce(f32[8,2,8]{2,0,1:T(8,128)S(1)} %fusion.41), channel_id=1, replica_groups=mesh['groups'=2,'section'=8,'tensor'=2] {'section'}, use_global_device_ids=true, to_apply=%region_15.16 | all-reduce | flops 128 | bytes 1024 | tf_op jit(solution)/shard_map/pmax | solution.py:190
  272.0 0.8 fusion.14
  273.1 0.9 reshape.201
  273.9 17.4 %all-reduce = f32[8,2,8]{2,1,0:T(2,128)S(1)} all-reduce(f32[8,2,8]{2,1,0:T(2,128)S(1)} %copy.116), channel_id=3, replica_groups=mesh['groups'=2,'section'=8,'tensor'=2] {'section'}, use_global_device_ids=true, to_apply=%region_19.20.clone | all-reduce | flops 128 | bytes 1024
  291.9 39.6 %reduce-scatter.2.cloned.1.call-done = f32[1,2,8,128]{3,2,1,0:T(8,128)} async-done(((f32[8,2,8,128]{3,2,1,0:T(8,128)}), f32[1,2,8,128]{3,2,1,0:T(8,128)}) %reduce-scatter.2.cloned.1.call-update) | async-done | bytes 8208 | tf_op jit(solution)/shard_map/reduce_scatter | solution.py:194
  331.6 0.8 fusion.45
  (87 shorter events, 12.7 us)
Async XLA Ops:
  10.9 13.6 %all-to-all-start.1 = ((s32[8,1,32]{2,1,0:T(1,128)}), s32[8,1,32]{2,1,0:T(1,128)S(1)}, u32[]{:S(2)}, u32[]{:S(2)}) async-start(s32[8,1,32]{2,1,0:T(1,128)} %all_to_all.23), calls=%async_computation.1 | async-start | bytes 8192 | tf_op jit(solution)/shard_map/all_to_all | solution.py:71
  24.5 53.3 %all-to-all-start.2 = ((bf16[8,32,4096]{2,1,0:T(8,128)(2,1)}), bf16[8,32,4096]{2,1,0:T(8,128)(2,1)S(1)}, u32[]{:S(2)}, u32[]{:S(2)}) async-start(bf16[8,32,4096]{2,1,0:T(8,128)(2,1)} %bitcast.10), calls=%async_computation.2 | async-start | bytes 4194304 | tf_op jit(solution)/shard_map/all_to_all | solution.py:64
  30.1 97.6 %all-gather.4.cloned.1.call-start = ((), (), s32[]{:S(2)}) async-start(), calls=%async_computation.5 | async-start | bytes 6291456 | tf_op jit(solution)/shard_map/all_gather | solution.py:91
  77.8 1.4 copy-start
  87.5 0.8 copy-start.7
  87.5 7.0 %copy-start.2 = (bf16[1,2048]{1,0:T(2,128)(2,1)S(1)}, bf16[1,2048]{1,0:T(2,128)(2,1)}, u32[]{:S(2)}) copy-start(bf16[1,2048]{1,0:T(2,128)(2,1)} %param.21) | copy-start | bytes 12292
  87.5 38.7 %copy-start.1 = (bf16[48,4,512]{2,1,0:T(4,128)(2,1)S(1)}, bf16[48,4,512]{2,1,0:T(4,128)(2,1)}, u32[]{:S(2)}) copy-start(bf16[48,4,512]{2,1,0:T(4,128)(2,1)} %param.22) | copy-start | bytes 589828
  87.5 38.8 %copy-start.3 = (s32[48]{0:T(128)S(1)}, s32[48]{0:T(128)}, u32[]{:S(2)}) copy-start(s32[48]{0:T(128)} %param.23) | copy-start | bytes 580
  87.5 39.5 %copy-start.4 = (s32[48]{0:T(128)S(1)}, s32[48]{0:T(128)}, u32[]{:S(2)}) copy-start(s32[48]{0:T(128)} %param.24) | copy-start | bytes 580
  87.5 141.3 %all-gather.6.cloned.1.call-start = ((), (), s32[]{:S(2)}) async-start(), calls=%async_computation.6 | async-start | bytes 9437184 | tf_op jit(solution)/shard_map/all_gather | solution.py:18
  90.8 146.9 %all-to-all-start = ((s32[8,1,8]{2,1,0:T(1,128)}), s32[8,1,8]{2,1,0:T(1,128)S(1)}, u32[]{:S(2)}, u32[]{:S(2)}) async-start(s32[8,1,8]{2,1,0:T(1,128)} %bitcast.1), calls=%async_computation | async-start | bytes 8192 | tf_op jit(solution)/shard_map/all_to_all | solution.py:121
  127.7 101.1 %copy-start.5 = (f32[8192]{0:T(1024)S(1)}, f32[8192]{0:T(1024)}, u32[]{:S(2)}) copy-start(f32[8192]{0:T(1024)} %param.20) | copy-start | bytes 98308
  127.7 101.1 %copy-start.6 = (f32[512]{0:T(512)S(1)}, f32[512]{0:T(512)}, u32[]{:S(2)}) copy-start(f32[512]{0:T(512)} %param.19) | copy-start | bytes 6148
  130.9 110.4 %copy-start.8 = (u32[32]{0:T(128)S(1)}, u32[32]{0:T(128)}, u32[]{:S(2)}) copy-start(u32[32]{0:T(128)} %constant.95) | copy-start | bytes 388
  237.7 12.2 %all-to-all-start.3 = ((bf16[8,8,2048]{2,1,0:T(8,128)(2,1)}), bf16[8,8,2048]{2,1,0:T(8,128)(2,1)S(1)}, u32[]{:S(2)}, u32[]{:S(2)}) async-start(bf16[8,8,2048]{2,1,0:T(8,128)(2,1)} %bitcast.12), calls=%async_computation.3 | async-start | bytes 524288 | tf_op jit(solution)/shard_map/all_to_all | solution.py:114
  241.1 90.5 %reduce-scatter.2.cloned.1.call-start = ((), (), s32[]{:S(2)}) async-start(), calls=%async_computation.7 | async-start | bytes 73728 | tf_op jit(solution)/shard_map/reduce_scatter | solution.py:194
Sparse Core Ops, SparseCore 0:
  87.6 12.7 all-gather.3
  102.6 126.1 all-gather.5
  273.0 58.4 reduce-scatter.1
where the time goes:
time: 340 us; the launch traced here: 339 us
  waiting for transfers between devices  190 us (56%)
  blocking collectives  68.6 us (20%)
  local copies, waits for them, and re-layouts  25.2 us (7%)
  starting transfers between devices  20 us (6%)
  between operations  15.4 us (5%)
  other arithmetic  10.5 us (3%)
  matrix products  9.29 us (3%)
    all_gather x1, waiting for transfers between devices, project(): whole_weight = lax.all_gather(kv_weight, 'section', axis=0, tiled=True)  97.9 us
    all_to_all x1, waiting for transfers between devices, shards(): lax.all_to_all(outgoing.reshape(sections, per_pair, -1), 'section', split...  44.2 us
    reduce_scatter x1, waiting for transfers between devices, shards(): lax.psum_scatter(acc * factor[..., None], 'section', scatter_dimension=0,...  39.6 us
    all_gather x1, blocking collectives, shards(): every_query = lax.all_gather(queries, 'section', axis=0, tiled=True)  31.6 us
    pmax x1, blocking collectives, shards(): best = lax.pmax(top, 'section')  19.6 us
    unnamed x1, blocking collectives  17.4 us
    all_to_all x1, waiting for transfers between devices, shards(): lax.all_to_all(out_blocks.reshape(sections, per_link, -1), 'section', spl...  7.59 us
    all_to_all x1, starting transfers between devices, shards(): lax.all_to_all(send_position.reshape(sections, per_pair), 'section', spli...  7.25 us
  transfers between devices with their start and end apart: 7, of which 5 were waited for; matrix products, arithmetic and copies ran while one was open for 8% of the time, Pallas kernels for 0%

commit v1 on v0

v1 whole, which is shorter than its diff:
```python
import functools

import jax
import jax.numpy as jnp
import numpy as np
from jax import lax
from jax.experimental import pallas as pl
from jax.experimental.pallas import tpu as pltpu
from jax.sharding import PartitionSpec as P

HQ = 32
KVH = 4
HD = 128
GROUP = HQ // KVH
SCALE = HD ** (-0.5)
LANES = 128
NEG = -1e30
VMEM = 60 * 1024 * 1024


def iota(shape, dim):
    return lax.broadcasted_iota(jnp.int32, shape, dim)


def call(kernel, outs, *args, cost=None, smem=()):
    return pl.pallas_call(
        kernel,
        out_shape=outs,
        in_specs=[
            pl.BlockSpec(memory_space=pltpu.SMEM if i in smem else pltpu.VMEM)
            for i in range(len(args))
        ],
        out_specs=jax.tree.map(lambda _: pl.BlockSpec(memory_space=pltpu.VMEM), outs),
        compiler_params=pltpu.CompilerParams(vmem_limit_bytes=VMEM),
        cost_estimate=cost,
    )(*args)


def cost(flops, nbytes):
    return pl.CostEstimate(flops=int(flops), bytes_accessed=int(nbytes), transcendentals=0)


def rank_before(hits):
    items = hits.shape[1]
    earlier = (iota((items, items), 0) < iota((items, items), 1)).astype(jnp.bfloat16)
    before = jnp.dot(hits.astype(jnp.bfloat16), earlier, preferred_element_type=jnp.float32)
    return jnp.sum(before * hits, axis=0, keepdims=True).astype(jnp.int32)


def prep_kernel(
    sections, cape, capr, image_ref, place_ref, owner_ref, query_ref, out_slot, out_block, out_message
):
    target, place, owner = image_ref[...], place_ref[...], owner_ref[...]
    hits = ((target == iota((sections, target.shape[1]), 0)) & (target >= 0)).astype(jnp.float32)
    rank = rank_before(hits)
    out_slot[...] = jnp.where(target >= 0, target * cape + rank, -1)
    at_rank = (rank == iota((LANES, target.shape[1]), 0)).astype(jnp.bfloat16)
    numbered = (hits * (place + 1).astype(jnp.float32)).astype(jnp.bfloat16)
    positions = lax.dot_general(
        numbered, at_rank, (((1,), (1,)), ((), ())), preferred_element_type=jnp.float32
    )
    positions = (positions - 1.0).astype(jnp.bfloat16)
    query = query_ref[...]
    heads = query.shape[0]
    out_message[:, :heads, :] = jnp.broadcast_to(query[None], (sections,) + query.shape)
    out_message[:, heads:, :] = jnp.broadcast_to(
        positions[:, None, :], (sections, out_message.shape[1] - heads, LANES)
    )
    owner_hits = ((owner == iota((sections, owner.shape[1]), 0)) & (owner >= 0)).astype(jnp.float32)
    out_block[...] = jnp.where(owner >= 0, owner * capr + rank_before(owner_hits), -1)


def norm_kernel(
    blocks, features, swap_width, slot_ref, text, image, text_far, image_far, gain, gain_far, out_ref
):
    half, width = blocks // 2, out_ref.shape[3]
    swap = slot_ref[blocks]
    for kind, (near_ref, far_ref) in enumerate(((text, text_far), (image, image_far))):
        near = near_ref[...].astype(jnp.float32)
        far = far_ref[...].astype(jnp.float32)
        total = jnp.sum(near * near, axis=1, keepdims=True) + jnp.sum(
            far * far, axis=1, keepdims=True
        )
        factor = lax.rsqrt(total * (1.0 / features) + 1e-06)
        for side, (ref, gains) in enumerate(((near_ref, gain), (far_ref, gain_far))):
            for j in range(half):
                at = pl.ds(j * width, width)
                block = ref[:, at].astype(jnp.float32) * factor * gains[:, at]
                block = block.astype(jnp.bfloat16)
                slot = slot_ref[side * half + j]
                out_ref[slot, kind] = block
                if swap_width:
                    turned = (swap > 0) & (slot > 0)

                    @pl.when(turned)
                    def _():
                        out_ref[slot, kind, :, :swap_width] = block[:, width - swap_width :]
                        out_ref[slot, kind, :, width - swap_width :] = block[:, :swap_width]


def normalize(slots, blocks, swap_width, text, image, text_far, image_far, gain, gain_far):
    rows, near = text.shape
    width = 2 * near // blocks
    tile = 32
    rows_spec = pl.BlockSpec((tile, near), lambda i, s: (i, 0))
    gain_spec = pl.BlockSpec((1, near), lambda i, s: (0, 0))
    return pl.pallas_call(
        functools.partial(norm_kernel, blocks, 2 * near, swap_width),
        out_shape=jax.ShapeDtypeStruct((blocks, 2, rows, width), jnp.bfloat16),
        grid_spec=pltpu.PrefetchScalarGridSpec(
            num_scalar_prefetch=1,
            grid=(rows // tile,),
            in_specs=[rows_spec] * 4 + [gain_spec] * 2,
            out_specs=pl.BlockSpec((blocks, 2, tile, width), lambda i, s: (0, 0, i, 0)),
        ),
        compiler_params=pltpu.CompilerParams(vmem_limit_bytes=VMEM),
        cost_estimate=cost(0, 8 * rows * 2 * near),
    )(slots, text, image, text_far, image_far, gain, gain_far)


def pool_kernel(message_ref, pool_ref, owner_ref, out_ref):
    sections, heads = out_ref.shape[0], out_ref.shape[1]
    keys = owner_ref.shape[1]
    owned = owner_ref[...] == iota((sections * GROUP, keys), 0) // GROUP
    for h in range(heads // GROUP):
        query = message_ref[:, h * GROUP : (h + 1) * GROUP, :].astype(jnp.float32)
        query = query.reshape(sections * GROUP, HD).astype(jnp.bfloat16)
        key = pool_ref[:, 2 * h * HD : (2 * h + 1) * HD]
        value = pool_ref[:, (2 * h + 1) * HD : (2 * h + 2) * HD]
        top, total, acc = attend(query, key, value, owned)
        lane = iota((sections * GROUP, LANES), 1)
        state = jnp.where(lane == 0, top, jnp.where(lane == 1, total, 0.0))
        out_ref[:, h * GROUP : (h + 1) * GROUP, :HD] = acc.reshape(sections, GROUP, HD)
        out_ref[:, h * GROUP : (h + 1) * GROUP, HD:] = state.reshape(sections, GROUP, LANES)


def attend(query, key, value, mask):
    scores = (
        lax.dot_general(query, key, (((1,), (1,)), ((), ())), preferred_element_type=jnp.float32)
        * SCALE
    )
    scores = jnp.where(mask, scores, NEG)
    top = jnp.max(scores, axis=1, keepdims=True)
    expo = jnp.where(mask, jnp.exp(scores - top), 0.0)
    total = jnp.sum(expo, axis=1, keepdims=True)
    acc = jnp.dot(expo.astype(jnp.bfloat16), value, preferred_element_type=jnp.float32)
    return top, total, acc


def finish_kernel(acc_ref, bias_ref, slot_ref, text_ref, send_ref):
    rows = text_ref.shape[0]
    text_ref[...] = (acc_ref[:rows] + bias_ref[...]).astype(jnp.bfloat16)
    image = (acc_ref[rows:] + bias_ref[...]).astype(jnp.bfloat16)
    place = (iota((send_ref.shape[0], rows), 0) == slot_ref[...]).astype(jnp.bfloat16)
    send_ref[...] = jnp.dot(place, image, preferred_element_type=jnp.float32).astype(jnp.bfloat16)


def place_kernel(text_ref, arrived_ref, position_ref, slot_ref, count_ref, rows_ref, blocks_ref):
    rows = text_ref.shape[0]
    row = iota((rows, arrived_ref.shape[0]), 0)
    match = (row == position_ref[...]) & (row < count_ref[0])
    filled = jnp.max(match.astype(jnp.float32), axis=1, keepdims=True) > 0.0
    placed = jnp.dot(
        match.astype(jnp.bfloat16), arrived_ref[...], preferred_element_type=jnp.float32
    )
    whole = jnp.where(filled, placed, text_ref[...].astype(jnp.float32)).astype(jnp.bfloat16)
    rows_ref[...] = whole
    slots = (iota((blocks_ref.shape[0], rows), 0) == slot_ref[...]).astype(jnp.bfloat16)
    blocks_ref[...] = jnp.dot(slots, whole, preferred_element_type=jnp.float32).astype(jnp.bfloat16)


def decode_kernel(rows_ref, query_ref, partial_ref, length_ref, out_ref):
    rows = rows_ref.shape[0]
    mask = iota((GROUP, rows), 1) < length_ref[0]
    for h in range(query_ref.shape[0] // GROUP):
        at = slice(h * GROUP, (h + 1) * GROUP)
        key = rows_ref[:, 2 * h * HD : (2 * h + 1) * HD]
        value = rows_ref[:, (2 * h + 1) * HD : (2 * h + 2) * HD]
        top, total, acc = attend(query_ref[at, :], key, value, mask)
        old_acc = partial_ref[:, at, :HD]
        old_top = partial_ref[:, at, HD : HD + 1]
        old_total = partial_ref[:, at, HD + 1 : HD + 2]
        best = jnp.maximum(top, jnp.max(old_top, axis=0))
        fresh_factor = jnp.exp(top - best)
        old_factor = jnp.exp(old_top - best[None])
        total = total * fresh_factor + jnp.sum(old_total * old_factor, axis=0)
        acc = acc * fresh_factor + jnp.sum(old_acc * old_factor, axis=0)
        out_ref[at, :] = (acc / total).astype(jnp.bfloat16)


def ring_order(sections):
    return list(range(0, sections, 2)) + list(range(1, sections, 2))[::-1]


def feature_slots(sections, tensors, ring):
    if not ring:
        return np.array([[[t, 1 - t] for t in range(tensors)] for _ in range(sections)], np.int32)
    order = ring_order(sections)
    table = np.zeros((sections, tensors, sections), np.int32)
    distances = [0] + [s * d for d in range(1, sections // 2) for s in (1, -1)] + [sections // 2]
    for at, section in enumerate(order):
        for slot, distance in enumerate(distances):
            source = order[(at - distance) % sections]
            for t in range(tensors):
                local = (source - t * (sections // tensors)) % sections
                table[section, t, local] = slot
    return table


def ring_project(normed, weight):
    sections = lax.axis_size("section")
    order = ring_order(sections)
    ahead = [(order[i], order[(i + 1) % sections]) for i in range(sections)]
    back = [(b, a) for a, b in ahead]
    depth = weight.shape[0]
    part = depth // 4
    index = lax.axis_index("groups")

    def up(x):
        return lax.ppermute(x, "section", ahead)

    def down(x):
        return lax.ppermute(x, "section", back)

    def across(x):
        return lax.ppermute(x, "groups", [(0, 1), (1, 0)])

    def product(slot, first, last, block):
        return jnp.dot(normed[slot, :, first:last], block, preferred_element_type=jnp.float32)

    own = lax.dynamic_slice_in_dim(weight, index * (depth - part), part, 0)
    middle = weight[part : depth - part]
    acc = product(0, 0, depth, weight)
    up_own, up_middle, down_own, down_middle = own, middle, own, middle
    slot = 1
    for _ in range(1, sections // 2):
        up_own, down_own = up(up_own), down(down_own)
        up_far, down_far = across(up_own), across(down_own)
        up_middle, down_middle = up(up_middle), down(down_middle)
        for near, mid, far in ((up_own, up_middle, up_far), (down_own, down_middle, down_far)):
            acc = acc + product(slot, 0, depth, jnp.concatenate([near, mid, far], 0))
            slot += 1
    last_own = up(up_own)
    last_far = across(last_own)
    eighth = part // 2
    last_middle = jnp.concatenate([up(up_middle[:eighth]), down(down_middle[eighth:])], 0)
    return acc + product(slot, 0, depth, jnp.concatenate([last_own, last_middle, last_far], 0))


def gather_project(normed, weight):
    whole = lax.all_gather(weight, "section", axis=0, tiled=True)
    width = normed.shape[2]
    acc = jnp.dot(normed[0], whole[:width], preferred_element_type=jnp.float32)
    return acc + jnp.dot(normed[1], whole[width:], preferred_element_type=jnp.float32)


def shards(
    text_embed,
    image_embed,
    image_count,
    prompt_len,
    embed_target,
    kv_weight,
    kv_bias,
    norm_gain,
    queries,
    old_pool,
    pool_owner,
    pool_fill,
    block_owner,
):
    sections, tensors = lax.axis_size("section"), lax.axis_size("tensor")
    rows, near = text_embed.shape
    width = kv_weight.shape[1]
    heads = queries.shape[1] // HD
    cape = rows // sections
    block_rows = old_pool.shape[1]
    capr = (block_owner.shape[0] + sections - 1) // sections * block_rows
    ring = (
        sections <= 16
        and sections % (2 * tensors) == 0
        and lax.axis_size("groups") == 2
        and kv_weight.shape[0] % (8 * LANES) == 0
    )
    section, tensor = lax.axis_index("section"), lax.axis_index("tensor")

    def exchange(x):
        return lax.all_to_all(x, "section", split_axis=0, concat_axis=0, tiled=True)

    def beside(x):
        return lax.ppermute(x, "tensor", [(0, 1), (1, 0)])

    table = feature_slots(sections, tensors, ring)
    blocks = table.shape[2]
    turn = lax.axis_index("groups").astype(jnp.int32).reshape(1)
    slots = lax.dynamic_slice(jnp.asarray(table), (section, tensor, 0), (1, 1, blocks))
    slots = jnp.concatenate([slots.reshape(blocks), turn])
    gains = norm_gain.reshape(tensors, near)
    gain = lax.dynamic_slice(gains, (tensor, 0), (1, near))
    gain_far = lax.dynamic_slice(gains, (1 - tensor, 0), (1, near))
    normed = normalize(
        slots,
        blocks,
        kv_weight.shape[0] // 4 if ring else 0,
        text_embed,
        image_embed,
        beside(text_embed),
        beside(image_embed),
        gain,
        gain_far,
    ).reshape(blocks, 2 * rows, -1)

    target = embed_target.reshape(1, rows)
    owner_rows = jnp.repeat(block_owner, block_rows).reshape(1, -1)
    query = queries.reshape(heads, HD)
    image_slot, block_slot, message = call(
        functools.partial(prep_kernel, sections, cape, capr),
        (
            jax.ShapeDtypeStruct((1, rows), jnp.int32),
            jax.ShapeDtypeStruct((1, owner_rows.shape[1]), jnp.int32),
            jax.ShapeDtypeStruct((sections, 2 * heads, LANES), jnp.bfloat16),
        ),
        jnp.where(target >= 0, target // rows, -1),
        target % rows,
        owner_rows,
        query,
    )
    message = exchange(message)
    position = message[:, heads, :cape].astype(jnp.int32).reshape(1, sections * cape)

    pool_rows = old_pool.reshape(-1, width)
    held = jnp.arange(block_rows, dtype=jnp.int32)[None, :] < pool_fill[:, None]
    held_owner = jnp.where(held, pool_owner[:, None], -1).reshape(1, -1)
    partial = exchange(
        call(
            pool_kernel,
            jax.ShapeDtypeStruct((sections, heads, 2 * HD), jnp.float32),
            message,
            pool_rows,
            held_owner,
        )
    )

    acc = (ring_project if ring else gather_project)(normed, kv_weight)
    text_rows, send = call(
        finish_kernel,
        (
            jax.ShapeDtypeStruct((rows, width), jnp.bfloat16),
            jax.ShapeDtypeStruct((sections * cape, width), jnp.bfloat16),
        ),
        acc,
        kv_bias.reshape(1, width),
        image_slot,
    )
    arrived = exchange(send.reshape(sections, cape, width)).reshape(sections * cape, width)
    whole_rows, block_data = call(
        place_kernel,
        (
            jax.ShapeDtypeStruct((rows, width), jnp.bfloat16),
            jax.ShapeDtypeStruct((sections * capr, width), jnp.bfloat16),
        ),
        text_rows,
        arrived,
        position,
        block_slot,
        image_count,
        smem=(4,),
    )
    fresh = exchange(block_data.reshape(sections, capr, width)).reshape(sections * capr, width)
    decoded = call(
        decode_kernel,
        jax.ShapeDtypeStruct((heads, HD), jnp.bfloat16),
        whole_rows,
        query,
        partial,
        prompt_len,
        smem=(3,),
    )
    return decoded.reshape(1, heads * HD), fresh


def solution(mesh):
    return jax.shard_map(
        shards,
        mesh=mesh,
        in_specs=(
            P(("groups", "section"), "tensor"),
            P(("groups", "section"), "tensor"),
            P(("groups", "section")),
            P(("groups", "section")),
            P(("groups", "section")),
            P("section", "tensor"),
            P("tensor"),
            P(),
            P(("groups", "section"), "tensor"),
            P(("groups", "section"), None, "tensor"),
            P(("groups", "section")),
            P(("groups", "section")),
            P(("groups", "section")),
        ),
        out_specs=(P(("groups", "section"), "tensor"), P(("groups", "section"), "tensor")),
        check_vma=False,
    )
```

time: 340 us -> 151 us (0.44)
  waiting for transfers between devices: 190 us -> 49.8 us
  blocking collectives: 68.6 us -> 0 us
  starting transfers between devices: 20 us -> 43.1 us
  Pallas kernels: 0 us -> 21.7 us
  between operations: 15.4 us -> 2.18 us
  local copies, waits for them, and re-layouts: 25.2 us -> 15.5 us
  other arithmetic: 10.5 us -> 3.97 us
  matrix products: 9.29 us -> 13 us
    all_gather x2 -> x0, waiting for transfers between devices: 97.9 us -> none  [the longest x1 97.9 us: project(): whole_weight = lax.all_gather(kv_weight, 'section', axis=0, tiled=True)]
    all_to_all x4, waiting for transfers between devices: 52.2 us -> 12 us  [exchange(): return lax.all_to_all(x, 'section', split_axis=0, concat_axis=0, tiled=True)]
    reduce_scatter x1 -> x0, waiting for transfers between devices: 39.6 us -> none  [shards(): lax.psum_scatter(acc * factor[..., None], 'section', scatter_dimension=0,...]
    ppermute x0 -> x24, waiting for transfers between devices: none -> 37.8 us  [the longest x7 27.1 us: down(): return lax.ppermute(x, 'section', back)]
    all_gather x1 -> x0, blocking collectives: 31.6 us -> none  [shards(): every_query = lax.all_gather(queries, 'section', axis=0, tiled=True)]
    ppermute x0 -> x24, starting transfers between devices: none -> 26.4 us  [the longest x7 12.1 us: down(): return lax.ppermute(x, 'section', back)]
    pallas_call x0 -> x6, Pallas kernels: none -> 21.7 us  [the longest x1 11.1 us: normalize(): pl.pallas_call(functools.partial(norm_kernel, blocks, 2 * near, swap_widt...]
    pmax x1 -> x0, blocking collectives: 19.6 us -> none  [shards(): best = lax.pmax(top, 'section')]
  transfers between devices with their start and end apart: 7 -> 28, of which waited for: 5 -> 9; matrix products, arithmetic and copies ran while one was open for 8% -> 20% of each run, Pallas kernels for 0% -> 15%
where the time goes in v1:
time: 151 us; the launch traced here: 149 us
  waiting for transfers between devices  49.8 us (33%)
  starting transfers between devices  43.1 us (29%)
  Pallas kernels  21.7 us (14%)
  local copies, waits for them, and re-layouts  15.5 us (10%)
  matrix products  13 us (9%)
  other arithmetic  3.97 us (3%)
  between operations  2.18 us (1%)
    ppermute x7, waiting for transfers between devices, down(): return lax.ppermute(x, 'section', back)  27.1 us
    all_to_all x4, starting transfers between devices, exchange(): return lax.all_to_all(x, 'section', split_axis=0, concat_axis=0, tiled=True)  16.7 us
    dot_general x8, matrix products, product(): jnp.dot(normed[slot, :, first:last], block, preferred_element_type=jnp.fl...  13 us
    ppermute x7, starting transfers between devices, down(): return lax.ppermute(x, 'section', back)  12.1 us
    all_to_all x4, waiting for transfers between devices, exchange(): return lax.all_to_all(x, 'section', split_axis=0, concat_axis=0, tiled=True)  12 us
    pallas_call x1, Pallas kernels, normalize(): pl.pallas_call(functools.partial(norm_kernel, blocks, 2 * near, swap_widt...  11.1 us
    ppermute x8, waiting for transfers between devices, up(): return lax.ppermute(x, 'section', ahead)  10.7 us
    pallas_call x5, Pallas kernels, call(): pl.pallas_call(kernel, out_shape=outs, in_specs=[pl.BlockSpec(memory_spac...  10.6 us
  transfers between devices with their start and end apart: 28, of which 9 were waited for; matrix products, arithmetic and copies ran while one was open for 20% of the time, Pallas kernels for 15%

profile of v1, /device:TPU:0, one launch (start us, length us, event | category | flops | bytes accessed | tf_op | source)
XLA Modules:
  0.0 149.3 jit_solution(2336370605090206639)
XLA Ops:
  1.7 3.0 %collective-permute-start.6 = (bf16[512,512]{1,0:T(8,128)(2,1)S(1)}, bf16[512,512]{1,0:T(8,128)(2,1)S(1)}, u32[]{:S(2)}, u32[]{:S(2)}) collective-permute-start(bf16[512,512]{1,0:T(8,128)(2,1)S(1)} %slice.46), channel_id=1, source_target_pairs={{4,0},{8,4},{12,8},{14,12},{10,14},{6,10},{2,6},{0,2},{5,1},{9,5},... | collective-permute-start | bytes 1572872 | tf_op jit(solution)/shard_map/ppermute | solution.py:223
  5.4 11.3 %collective-permute-done.6 = bf16[512,512]{1,0:T(8,128)(2,1)S(1)} collective-permute-done((bf16[512,512]{1,0:T(8,128)(2,1)S(1)}, bf16[512,512]{1,0:T(8,128)(2,1)S(1)}, u32[]{:S(2)}, u32[]{:S(2)}) %collective-permute-start.6) | collective-permute-done | bytes 524320 | tf_op jit(solution)/shard_map/ppermute | solution.py:223
  21.5 8.5 %collective-permute-done.12 = bf16[512,512]{1,0:T(8,128)(2,1)} collective-permute-done((bf16[512,512]{1,0:T(8,128)(2,1)S(1)}, bf16[512,512]{1,0:T(8,128)(2,1)}, u32[]{:S(2)}, u32[]{:S(2)}) %collective-permute-start.12) | collective-permute-done | bytes 524320 | tf_op jit(solution)/shard_map/ppermute | solution.py:223
  39.3 3.9 %all-to-all-start.1 = ((bf16[8,32,128]{2,1,0:T(8,128)(2,1)}), bf16[8,32,128]{2,1,0:T(8,128)(2,1)S(1)}, u32[]{:S(2)}, u32[]{:S(2)}) async-start(bf16[8,32,128]{2,1,0:T(8,128)(2,1)} %get-tuple-element.12), calls=%async_computation.1 | async-start | bytes 131072 | tf_op jit(solution)/shard_map/all_to_all | solution.py:288
  43.9 4.9 %collective-permute-done.5 = bf16[256,512]{1,0:T(8,128)(2,1)} collective-permute-done((bf16[256,512]{1,0:T(8,128)(2,1)S(1)}, bf16[256,512]{1,0:T(8,128)(2,1)}, u32[]{:S(2)}, u32[]{:S(2)}) %collective-permute-start.5) | collective-permute-done | bytes 262176 | tf_op jit(solution)/shard_map/ppermute | solution.py:223
  50.8 1.8 %collective-permute-start.15 = (bf16[512,512]{1,0:T(8,128)(2,1)S(1)}, bf16[512,512]{1,0:T(8,128)(2,1)S(1)}, u32[]{:S(2)}, u32[]{:S(2)}) collective-permute-start(bf16[512,512]{1,0:T(8,128)(2,1)S(1)} %collective-permute-done.9), channel_id=1, source_target_pairs={{0,4},{4,8},{8,12},{12,14},{14,10},{10,6},{6,2},{2,0},{1,5},{5,9},... | collective-permute-start | bytes 1572872 | tf_op jit(solution)/shard_map/ppermute | solution.py:220
  55.5 10.5 %collective-permute-done.15 = bf16[512,512]{1,0:T(8,128)(2,1)S(1)} collective-permute-done((bf16[512,512]{1,0:T(8,128)(2,1)S(1)}, bf16[512,512]{1,0:T(8,128)(2,1)S(1)}, u32[]{:S(2)}, u32[]{:S(2)}) %collective-permute-start.15) | collective-permute-done | bytes 524320 | tf_op jit(solution)/shard_map/ppermute | solution.py:220
  71.4 11.1 %shard_map.149 = bf16[8,2,256,1024]{3,2,1,0:T(8,128)(2,1)} custom-call(s32[9]{0:T(128)} %pad_add_fusion.slot_ref, bf16[256,4096]{1,0:T(8,128)(2,1)} %text.1, bf16[256,4096]{1,0:T(8,128)(2,1)} %image.1, bf16[256,4096]{1,0:T(8,128)(2,1)} %copy-done, bf16[256,4096]{1,0:T(8,128)(2,1)} %collective-permute-done.1.image_far, f32[1,4096]{1,0:T(1,128)} %get-tuple-element.25.gain, ...), custom_call_target="tpu_custom_call" | custom-call | bytes 16777216 | tf_op jit(solution)/shard_map/pallas_call | solution.py:107
  82.5 4.1 %fusion.51 = (bf16[1,2,256,1024]{3,2,1,0:T(8,128)(2,1)S(1)}, bf16[1,2,256,1024]{3,2,1,0:T(8,128)(2,1)S(1)}, bf16[1,2,256,1024]{3,2,1,0:T(8,128)(2,1)S(1)}, bf16[...) fusion(bf16[8,2,256,1024]{3,2,1,0:T(8,128)(2,1)} %shard_map.149), kind=kLoop, calls=%fused_computation.72 | loop fusion | bytes 16777216 | tf_op jit(solution)/shard_map/slice | solution.py:229
  89.5 1.9 %convolution_add_fusion.4 = f32[512,512]{1,0:T(8,128)S(1)} fusion(f32[512,512]{1,0:T(8,128)S(1)} %fusion.52, bf16[512,1024]{1,0:T(8,128)(2,1)S(1)} %bitcast.39, bf16[256,512]{1,0:T(8,128)(2,1)} %collective-permute-done.4, bf16[512,512]{1,0:T(8,128)(2,1)} %collective-permute-done.3, bf16[256,512]{1,0:T(8,128)(2,1)S(1)} %copy-done.11), kind=kOutput, calls=%fused_computation.6 | convolution fusion | flops 540278784 | bytes 4194304 | tf_op jit(solution)/shard_map/dot_general | solution.py:229
  92.2 2.4 %collective-permute-done.17 = bf16[256,512]{1,0:T(8,128)(2,1)S(1)} collective-permute-done((bf16[256,512]{1,0:T(8,128)(2,1)}, bf16[256,512]{1,0:T(8,128)(2,1)S(1)}, u32[]{:S(2)}, u32[]{:S(2)}) %collective-permute-start.17) | collective-permute-done | bytes 262176 | tf_op jit(solution)/shard_map/ppermute | solution.py:223
  98.4 2.0 %collective-permute-start.22 = (bf16[384,512]{1,0:T(8,128)(2,1)S(1)}, bf16[384,512]{1,0:T(8,128)(2,1)S(1)}, u32[]{:S(2)}, u32[]{:S(2)}) collective-permute-start(bf16[384,512]{1,0:T(8,128)(2,1)S(1)} %slice.65), channel_id=1, source_target_pairs={{4,0},{8,4},{12,8},{14,12},{10,14},{6,10},{2,6},{0,2},{5,1},{9,5},... | collective-permute-start | bytes 1179656 | tf_op jit(solution)/shard_map/ppermute | solution.py:223
  100.5 1.9 %fusion.17 = f32[512,512]{1,0:T(8,128)S(1)} fusion(bf16[512,1024]{1,0:T(8,128)(2,1)S(1)} %bitcast.37, bf16[256,512]{1,0:T(8,128)(2,1)} %collective-permute-done.13, bf16[512,512]{1,0:T(8,128)(2,1)} %collective-permute-done.12, bf16[256,512]{1,0:T(8,128)(2,1)} %collective-permute-done.11), kind=kOutput, calls=%fused_computation.22 | convolution fusion | flops 540016640 | bytes 3145728 | tf_op jit(solution)/shard_map/dot_general | solution.py:229
  104.1 1.7 %fusion.28 = f32[512,512]{1,0:T(8,128)S(1)} fusion(bf16[512,1024]{1,0:T(8,128)(2,1)S(1)} %bitcast.36, bf16[256,512]{1,0:T(8,128)(2,1)S(1)} %collective-permute-done.19, bf16[512,512]{1,0:T(8,128)(2,1)} %collective-permute-done.18, bf16[256,512]{1,0:T(8,128)(2,1)S(1)} %collective-permute-done.17), kind=kOutput, calls=%fused_computation.33 | convolution fusion | flops 540016640 | bytes 3145728 | tf_op jit(solution)/shard_map/dot_general | solution.py:229
  109.4 2.3 %shard_map.151 = (bf16[256,512]{1,0:T(8,128)(2,1)}, bf16[256,512]{1,0:T(8,128)(2,1)}) custom-call(f32[512,512]{1,0:T(8,128)} %convolution_add_fusion.acc_ref, f32[1,512]{1,0:T(1,128)} %bitcast.51, s32[1,256]{1,0:T(1,128)} %get-tuple-element.9.slot_ref), custom_call_target="tpu_custom_call" | custom-call | tf_op jit(solution)/shard_map/pallas_call | solution.py:26
  111.6 6.1 %all-to-all-start = ((bf16[8,32,512]{2,1,0:T(8,128)(2,1)}), bf16[8,32,512]{2,1,0:T(8,128)(2,1)S(1)}, u32[]{:S(2)}, u32[]{:S(2)}) async-start(bf16[8,32,512]{2,1,0:T(8,128)(2,1)} %bitcast.44), calls=%async_computation | async-start | bytes 524288 | tf_op jit(solution)/shard_map/all_to_all | solution.py:288
  119.2 2.2 %shard_map.153 = f32[8,16,256]{2,1,0:T(8,128)} custom-call(bf16[8,32,128]{2,1,0:T(8,128)(2,1)} %copy-done.4, bf16[192,512]{1,0:T(8,128)(2,1)} %reshape.140.pool_ref, s32[1,192]{1,0:T(1,128)} %select_n.58.owner_ref), custom_call_target="tpu_custom_call" | custom-call | tf_op jit(solution)/shard_map/pallas_call | solution.py:26
  121.4 5.0 %all-to-all-done = bf16[8,32,512]{2,1,0:T(8,128)(2,1)S(1)} async-done(((bf16[8,32,512]{2,1,0:T(8,128)(2,1)}), bf16[8,32,512]{2,1,0:T(8,128)(2,1)S(1)}, u32[]{:S(2)}, u32[]{:S(2)}) %all-to-all-start) | async-done | bytes 262176 | tf_op jit(solution)/shard_map/all_to_all | solution.py:288
  126.4 3.4 %all-to-all-start.2 = ((f32[8,16,256]{2,1,0:T(8,128)}), f32[8,16,256]{2,1,0:T(8,128)S(1)}, u32[]{:S(2)}, u32[]{:S(2)}) async-start(f32[8,16,256]{2,1,0:T(8,128)} %shard_map.153), calls=%async_computation.2 | async-start | bytes 262144 | tf_op jit(solution)/shard_map/all_to_all | solution.py:288
  131.8 2.2 %shard_map.152 = (bf16[256,512]{1,0:T(8,128)(2,1)}, bf16[256,512]{1,0:T(8,128)(2,1)}) custom-call(bf16[256,512]{1,0:T(8,128)(2,1)} %get-tuple-element.10.text_ref, bf16[256,512]{1,0:T(8,128)(2,1)} %bitcast.41, s32[1,256]{1,0:T(1,128)} %reshape.144.position_ref, s32[1,256]{1,0:T(1,128)} %get-tuple-element.13.slot_ref, s32[1]{0:T(128)S(6)} %copy.20.count_ref), custom_call_target="tpu_custom_call" | custom-call | tf_op jit(solution)/shard_map/pallas_call | solution.py:26
  134.0 3.1 %all-to-all-done.2.partial_ref = f32[8,16,256]{2,1,0:T(8,128)S(1)} async-done(((f32[8,16,256]{2,1,0:T(8,128)}), f32[8,16,256]{2,1,0:T(8,128)S(1)}, u32[]{:S(2)}, u32[]{:S(2)}) %all-to-all-start.2) | async-done | bytes 131104 | tf_op jit(solution)/shard_map/all_to_all | solution.py:288
  137.1 3.4 %all-to-all-start.3 = ((bf16[8,32,512]{2,1,0:T(8,128)(2,1)}), bf16[8,32,512]{2,1,0:T(8,128)(2,1)S(1)}, u32[]{:S(2)}, u32[]{:S(2)}) async-start(bf16[8,32,512]{2,1,0:T(8,128)(2,1)} %bitcast.43), calls=%async_computation.3 | async-start | bytes 524288 | tf_op jit(solution)/shard_map/all_to_all | solution.py:288
  141.1 2.3 %shard_map.154 = bf16[16,128]{1,0:T(8,128)(2,1)} custom-call(bf16[256,512]{1,0:T(8,128)(2,1)} %get-tuple-element.14.rows_ref, bf16[16,128]{1,0:T(8,128)(2,1)} %bitcast.46, f32[8,16,256]{2,1,0:T(8,128)} %copy-done.3, s32[1]{0:T(128)S(6)} %copy.21.length_ref), custom_call_target="tpu_custom_call" | custom-call | tf_op jit(solution)/shard_map/pallas_call | solution.py:26
  144.7 3.9 %all-to-all-done.3 = bf16[8,32,512]{2,1,0:T(8,128)(2,1)S(1)} async-done(((bf16[8,32,512]{2,1,0:T(8,128)(2,1)}), bf16[8,32,512]{2,1,0:T(8,128)(2,1)S(1)}, u32[]{:S(2)}, u32[]{:S(2)}) %all-to-all-start.3) | async-done | bytes 262176 | tf_op jit(solution)/shard_map/all_to_all | solution.py:288
  (90 shorter events, 44.3 us)
Async XLA Ops:
  1.7 15.0 %collective-permute-start.6 = (bf16[512,512]{1,0:T(8,128)(2,1)S(1)}, bf16[512,512]{1,0:T(8,128)(2,1)S(1)}, u32[]{:S(2)}, u32[]{:S(2)}) collective-permute-start(bf16[512,512]{1,0:T(8,128)(2,1)S(1)} %slice.46), channel_id=1, source_target_pairs={{4,0},{8,4},{12,8},{14,12},{10,14},{6,10},{2,6},{0,2},{5,1},{9,5},... | collective-permute-start | bytes 1572872 | tf_op jit(solution)/shard_map/ppermute | solution.py:223
  4.7 64.9 %collective-permute-start = (bf16[256,4096]{1,0:T(8,128)(2,1)}, bf16[256,4096]{1,0:T(8,128)(2,1)S(1)}, u32[]{:S(2)}, u32[]{:S(2)}) collective-permute-start(bf16[256,4096]{1,0:T(8,128)(2,1)} %text.1), channel_id=1, source_target_pairs={{0,1},{1,0},{2,3},{3,2},{4,5},{5,4},{6,7},{7,6},{8,9},{9,8},{10,11... | collective-permute-start | bytes 6291464 | tf_op jit(solution)/shard_map/ppermute | solution.py:291
  4.7 65.4 %collective-permute-start.1 = (bf16[256,4096]{1,0:T(8,128)(2,1)}, bf16[256,4096]{1,0:T(8,128)(2,1)}, u32[]{:S(2)}, u32[]{:S(2)}) collective-permute-start(bf16[256,4096]{1,0:T(8,128)(2,1)} %image.1), channel_id=1, source_target_pairs={{0,1},{1,0},{2,3},{3,2},{4,5},{5,4},{6,7},{7,6},{8,9},{9,8},{10,11... | collective-permute-start | bytes 6291464 | tf_op jit(solution)/shard_map/ppermute | solution.py:291
  5.2 14.6 %collective-permute-start.3 = (bf16[512,512]{1,0:T(8,128)(2,1)S(1)}, bf16[512,512]{1,0:T(8,128)(2,1)}, u32[]{:S(2)}, u32[]{:S(2)}) collective-permute-start(bf16[512,512]{1,0:T(8,128)(2,1)S(1)} %slice.46), channel_id=1, source_target_pairs={{0,4},{4,8},{8,12},{12,14},{14,10},{10,6},{6,2},{2,0},{1,5},{5,9},... | collective-permute-start | bytes 1572872 | tf_op jit(solution)/shard_map/ppermute | solution.py:220
  16.7 13.3 %collective-permute-start.12 = (bf16[512,512]{1,0:T(8,128)(2,1)S(1)}, bf16[512,512]{1,0:T(8,128)(2,1)}, u32[]{:S(2)}, u32[]{:S(2)}) collective-permute-start(bf16[512,512]{1,0:T(8,128)(2,1)S(1)} %collective-permute-done.6), channel_id=1, source_target_pairs={{4,0},{8,4},{12,8},{14,12},{10,14},{6,10},{2,6},{0,2},{5,1},{9,5},... | collective-permute-start | bytes 1572872 | tf_op jit(solution)/shard_map/ppermute | solution.py:223
  19.3 12.0 %collective-permute-start.2 = (bf16[256,512]{1,0:T(8,128)(2,1)S(1)}, bf16[256,512]{1,0:T(8,128)(2,1)S(1)}, u32[]{:S(2)}, u32[]{:S(2)}) collective-permute-start(bf16[256,512]{1,0:T(8,128)(2,1)S(1)} %constant_dynamic-slice_fusion), channel_id=1, source_target_pairs={{0,4},{4,8},{8,12},{12,14},{14,10},{10,6},{6,2},{2,0},{1,5},{5,9},... | collective-permute-start | bytes 786440 | tf_op jit(solution)/shard_map/ppermute | solution.py:220
  19.8 30.0 %collective-permute-start.9 = (bf16[512,512]{1,0:T(8,128)(2,1)}, bf16[512,512]{1,0:T(8,128)(2,1)S(1)}, u32[]{:S(2)}, u32[]{:S(2)}) collective-permute-start(bf16[512,512]{1,0:T(8,128)(2,1)} %collective-permute-done.3), channel_id=1, source_target_pairs={{0,4},{4,8},{8,12},{12,14},{14,10},{10,6},{6,2},{2,0},{1,5},{5,9},... | collective-permute-start | bytes 1572872 | tf_op jit(solution)/shard_map/ppermute | solution.py:220
  30.0 20.8 %collective-permute-start.18 = (bf16[512,512]{1,0:T(8,128)(2,1)}, bf16[512,512]{1,0:T(8,128)(2,1)}, u32[]{:S(2)}, u32[]{:S(2)}) collective-permute-start(bf16[512,512]{1,0:T(8,128)(2,1)} %collective-permute-done.12), channel_id=1, source_target_pairs={{4,0},{8,4},{12,8},{14,12},{10,14},{6,10},{2,6},{0,2},{5,1},{9,5},... | collective-permute-start | bytes 1572872 | tf_op jit(solution)/shard_map/ppermute | solution.py:223
  32.1 16.7 %collective-permute-start.5 = (bf16[256,512]{1,0:T(8,128)(2,1)S(1)}, bf16[256,512]{1,0:T(8,128)(2,1)}, u32[]{:S(2)}, u32[]{:S(2)}) collective-permute-start(bf16[256,512]{1,0:T(8,128)(2,1)S(1)} %constant_dynamic-slice_fusion), channel_id=1, source_target_pairs={{4,0},{8,4},{12,8},{14,12},{10,14},{6,10},{2,6},{0,2},{5,1},{9,5},... | collective-permute-start | bytes 786440 | tf_op jit(solution)/shard_map/ppermute | solution.py:223
  39.3 72.3 %all-to-all-start.1 = ((bf16[8,32,128]{2,1,0:T(8,128)(2,1)}), bf16[8,32,128]{2,1,0:T(8,128)(2,1)S(1)}, u32[]{:S(2)}, u32[]{:S(2)}) async-start(bf16[8,32,128]{2,1,0:T(8,128)(2,1)} %get-tuple-element.12), calls=%async_computation.1 | async-start | bytes 131072 | tf_op jit(solution)/shard_map/all_to_all | solution.py:288
  48.8 18.7 %collective-permute-start.11 = (bf16[256,512]{1,0:T(8,128)(2,1)}, bf16[256,512]{1,0:T(8,128)(2,1)}, u32[]{:S(2)}, u32[]{:S(2)}) collective-permute-start(bf16[256,512]{1,0:T(8,128)(2,1)} %collective-permute-done.5), channel_id=1, source_target_pairs={{4,0},{8,4},{12,8},{14,12},{10,14},{6,10},{2,6},{0,2},{5,1},{9,5},... | collective-permute-start | bytes 786440 | tf_op jit(solution)/shard_map/ppermute | solution.py:223
  49.8 18.3 %collective-permute-start.8 = (bf16[256,512]{1,0:T(8,128)(2,1)}, bf16[256,512]{1,0:T(8,128)(2,1)S(1)}, u32[]{:S(2)}, u32[]{:S(2)}) collective-permute-start(bf16[256,512]{1,0:T(8,128)(2,1)} %copy-done.10), channel_id=1, source_target_pairs={{0,4},{4,8},{8,12},{12,14},{14,10},{10,6},{6,2},{2,0},{1,5},{5,9},... | collective-permute-start | bytes 786440 | tf_op jit(solution)/shard_map/ppermute | solution.py:220
  50.8 15.1 %collective-permute-start.15 = (bf16[512,512]{1,0:T(8,128)(2,1)S(1)}, bf16[512,512]{1,0:T(8,128)(2,1)S(1)}, u32[]{:S(2)}, u32[]{:S(2)}) collective-permute-start(bf16[512,512]{1,0:T(8,128)(2,1)S(1)} %collective-permute-done.9), channel_id=1, source_target_pairs={{0,4},{4,8},{8,12},{12,14},{14,10},{10,6},{6,2},{2,0},{1,5},{5,9},... | collective-permute-start | bytes 1572872 | tf_op jit(solution)/shard_map/ppermute | solution.py:220
  66.0 21.4 %collective-permute-start.4 = (bf16[256,512]{1,0:T(8,128)(2,1)}, bf16[256,512]{1,0:T(8,128)(2,1)}, u32[]{:S(2)}, u32[]{:S(2)}) collective-permute-start(bf16[256,512]{1,0:T(8,128)(2,1)} %copy-done.10), channel_id=1, source_target_pairs={{0,16},{16,0},{1,17},{17,1},{2,18},{18,2},{3,19},{19,3},{4,20},{20... | collective-permute-start | bytes 786440 | tf_op jit(solution)/shard_map/ppermute | solution.py:226
  67.5 23.8 %collective-permute-start.7 = (bf16[256,512]{1,0:T(8,128)(2,1)}, bf16[256,512]{1,0:T(8,128)(2,1)}, u32[]{:S(2)}, u32[]{:S(2)}) collective-permute-start(bf16[256,512]{1,0:T(8,128)(2,1)} %collective-permute-done.5), channel_id=1, source_target_pairs={{0,16},{16,0},{1,17},{17,1},{2,18},{18,2},{3,19},{19,3},{4,20},{20... | collective-permute-start | bytes 786440 | tf_op jit(solution)/shard_map/ppermute | solution.py:226
  68.1 34.3 %collective-permute-start.10 = (bf16[256,512]{1,0:T(8,128)(2,1)S(1)}, bf16[256,512]{1,0:T(8,128)(2,1)}, u32[]{:S(2)}, u32[]{:S(2)}) collective-permute-start(bf16[256,512]{1,0:T(8,128)(2,1)S(1)} %collective-permute-done.8), channel_id=1, source_target_pairs={{0,16},{16,0},{1,17},{17,1},{2,18},{18,2},{3,19},{19,3},{4,20},{20... | collective-permute-start | bytes 786440 | tf_op jit(solution)/shard_map/ppermute | solution.py:226
  69.6 19.3 %collective-permute-start.14 = (bf16[256,512]{1,0:T(8,128)(2,1)S(1)}, bf16[256,512]{1,0:T(8,128)(2,1)}, u32[]{:S(2)}, u32[]{:S(2)}) collective-permute-start(bf16[256,512]{1,0:T(8,128)(2,1)S(1)} %collective-permute-done.8), channel_id=1, source_target_pairs={{0,4},{4,8},{8,12},{12,14},{14,10},{10,6},{6,2},{2,0},{1,5},{5,9},... | collective-permute-start | bytes 786440 | tf_op jit(solution)/shard_map/ppermute | solution.py:220
  70.1 28.3 %collective-permute-start.13 = (bf16[256,512]{1,0:T(8,128)(2,1)}, bf16[256,512]{1,0:T(8,128)(2,1)}, u32[]{:S(2)}, u32[]{:S(2)}) collective-permute-start(bf16[256,512]{1,0:T(8,128)(2,1)} %collective-permute-done.11), channel_id=1, source_target_pairs={{0,16},{16,0},{1,17},{17,1},{2,18},{18,2},{3,19},{19,3},{4,20},{20... | collective-permute-start | bytes 786440 | tf_op jit(solution)/shard_map/ppermute | solution.py:226
  91.4 14.5 %collective-permute-start.16 = (bf16[256,512]{1,0:T(8,128)(2,1)}, bf16[256,512]{1,0:T(8,128)(2,1)S(1)}, u32[]{:S(2)}, u32[]{:S(2)}) collective-permute-start(bf16[256,512]{1,0:T(8,128)(2,1)} %collective-permute-done.14), channel_id=1, source_target_pairs={{0,16},{16,0},{1,17},{17,1},{2,18},{18,2},{3,19},{19,3},{4,20},{20... | collective-permute-start | bytes 786440 | tf_op jit(solution)/shard_map/ppermute | solution.py:226
  94.6 9.5 %collective-permute-start.19 = (bf16[256,512]{1,0:T(8,128)(2,1)S(1)}, bf16[256,512]{1,0:T(8,128)(2,1)S(1)}, u32[]{:S(2)}, u32[]{:S(2)}) collective-permute-start(bf16[256,512]{1,0:T(8,128)(2,1)S(1)} %collective-permute-done.17), channel_id=1, source_target_pairs={{0,16},{16,0},{1,17},{17,1},{2,18},{18,2},{3,19},{19,3},{4,20},{20... | collective-permute-start | bytes 786440 | tf_op jit(solution)/shard_map/ppermute | solution.py:226
  95.5 12.1 %collective-permute-start.23 = (bf16[256,512]{1,0:T(8,128)(2,1)S(1)}, bf16[256,512]{1,0:T(8,128)(2,1)S(1)}, u32[]{:S(2)}, u32[]{:S(2)}) collective-permute-start(bf16[256,512]{1,0:T(8,128)(2,1)S(1)} %collective-permute-done.20), channel_id=1, source_target_pairs={{0,16},{16,0},{1,17},{17,1},{2,18},{18,2},{3,19},{19,3},{4,20},{20... | collective-permute-start | bytes 786440 | tf_op jit(solution)/shard_map/ppermute | solution.py:226
  111.6 14.8 %all-to-all-start = ((bf16[8,32,512]{2,1,0:T(8,128)(2,1)}), bf16[8,32,512]{2,1,0:T(8,128)(2,1)S(1)}, u32[]{:S(2)}, u32[]{:S(2)}) async-start(bf16[8,32,512]{2,1,0:T(8,128)(2,1)} %bitcast.44), calls=%async_computation | async-start | bytes 524288 | tf_op jit(solution)/shard_map/all_to_all | solution.py:288
  126.4 10.7 %all-to-all-start.2 = ((f32[8,16,256]{2,1,0:T(8,128)}), f32[8,16,256]{2,1,0:T(8,128)S(1)}, u32[]{:S(2)}, u32[]{:S(2)}) async-start(f32[8,16,256]{2,1,0:T(8,128)} %shard_map.153), calls=%async_computation.2 | async-start | bytes 262144 | tf_op jit(solution)/shard_map/all_to_all | solution.py:288
  137.1 11.6 %all-to-all-start.3 = ((bf16[8,32,512]{2,1,0:T(8,128)(2,1)}), bf16[8,32,512]{2,1,0:T(8,128)(2,1)S(1)}, u32[]{:S(2)}, u32[]{:S(2)}) async-start(bf16[8,32,512]{2,1,0:T(8,128)(2,1)} %bitcast.43), calls=%async_computation.3 | async-start | bytes 524288 | tf_op jit(solution)/shard_map/all_to_all | solution.py:288
  (16 other events, 126.7 us)

commit v2 on v1

v2 whole, which is shorter than its diff:
```python
import functools

import jax
import jax.numpy as jnp
import numpy as np
from jax import lax
from jax.experimental import pallas as pl
from jax.experimental.pallas import tpu as pltpu
from jax.sharding import PartitionSpec as P

HQ = 32
KVH = 4
HD = 128
GROUP = HQ // KVH
SCALE = HD ** (-0.5)
LANES = 128
NEG = -1e30
VMEM = 24 * 1024 * 1024


def iota(shape, dim):
    return lax.broadcasted_iota(jnp.int32, shape, dim)


def call(kernel, outs, *args, cost=None, smem=(), aliases=None):
    return pl.pallas_call(
        kernel,
        out_shape=outs,
        in_specs=[
            pl.BlockSpec(memory_space=pltpu.SMEM if i in smem else pltpu.VMEM)
            for i in range(len(args))
        ],
        out_specs=jax.tree.map(lambda _: pl.BlockSpec(memory_space=pltpu.VMEM), outs),
        input_output_aliases=aliases or {},
        compiler_params=pltpu.CompilerParams(vmem_limit_bytes=VMEM),
        cost_estimate=cost,
    )(*args)


def cost(flops, nbytes):
    return pl.CostEstimate(flops=int(flops), bytes_accessed=int(nbytes), transcendentals=0)


def rank_before(hits):
    items = hits.shape[1]
    earlier = (iota((items, items), 0) < iota((items, items), 1)).astype(jnp.bfloat16)
    before = jnp.dot(hits.astype(jnp.bfloat16), earlier, preferred_element_type=jnp.float32)
    return jnp.sum(before * hits, axis=0, keepdims=True).astype(jnp.int32)


def spread(values, items):
    groups = values.shape[1]
    share = items // groups
    same = iota((groups, items), 0) * share
    column = iota((groups, items), 1)
    same = ((column >= same) & (column < same + share)).astype(jnp.bfloat16)
    wide = jnp.broadcast_to(values.astype(jnp.float32), (8, groups)).astype(jnp.bfloat16)
    wide = jnp.dot(wide, same, preferred_element_type=jnp.float32)
    return wide[:1].astype(jnp.int32)


def image_slots(target, sections, cape):
    rows = target.shape[1]
    index = jnp.floor((target.astype(jnp.float32) + 0.5) * (1.0 / rows)).astype(jnp.int32)
    place = target - index * rows
    hits = ((index == iota((sections, rows), 0)) & (target >= 0)).astype(jnp.float32)
    rank = rank_before(hits)
    at_rank = (rank == iota((LANES, rows), 0)).astype(jnp.bfloat16)
    numbered = (hits * (place + 1).astype(jnp.float32)).astype(jnp.bfloat16)
    positions = lax.dot_general(
        numbered, at_rank, (((1,), (1,)), ((), ())), preferred_element_type=jnp.float32
    )
    return jnp.where(target >= 0, index * cape + rank, -1), positions - 1.0


def block_slots(owner, sections, capr, block_rows):
    owner = spread(owner, owner.shape[1] * block_rows)
    hits = ((owner == iota((sections, owner.shape[1]), 0)) & (owner >= 0)).astype(jnp.float32)
    return jnp.where(owner >= 0, owner * capr + rank_before(hits), -1)


def query_group(query_ref, h):
    heads = [
        query_ref[:, j * HD : (j + 1) * HD].astype(jnp.float32)
        for j in range(h * GROUP, (h + 1) * GROUP)
    ]
    return jnp.concatenate(heads, axis=0)


def prep_kernel(
    sections, cape, capr, block_rows, target_ref, owner_ref, query_ref, out_slot, out_block, out_message
):
    out_slot[...], positions = image_slots(target_ref[...], sections, cape)
    heads = query_ref.shape[1] // HD
    query = jnp.concatenate([query_group(query_ref, h) for h in range(heads // GROUP)], axis=0)
    query = query.astype(jnp.bfloat16)
    out_message[:, :heads, :] = jnp.broadcast_to(query[None], (sections,) + query.shape)
    out_message[:, heads:, :] = jnp.broadcast_to(
        positions.astype(jnp.bfloat16)[:, None, :], (sections, out_message.shape[1] - heads, LANES)
    )
    out_block[...] = block_slots(owner_ref[...], sections, capr, block_rows)


def open_kernel(
    sections, cape, capr, block_rows, group_ref, weight_ref, target_ref, owner_ref, query_ref,
    out_own, out_middle, out_slot, out_block
):
    part = out_middle.shape[0] // 2
    turned = pl.multiple_of(group_ref[0] * (weight_ref.shape[0] - part), part)
    out_own[:part] = weight_ref[pl.ds(turned, part), :]
    out_middle[...] = weight_ref[part : 3 * part, :]
    out_slot[...], positions = image_slots(target_ref[...], sections, cape)
    groups = query_ref.shape[1] // (GROUP * HD)
    told = [query_group(query_ref, h) for h in range(groups)]
    told.append(jnp.zeros((GROUP, out_own.shape[1] - groups * HD), jnp.float32))
    told = jnp.concatenate(told, axis=1)
    positions = jnp.concatenate(
        [positions, jnp.zeros((sections, out_own.shape[1] - LANES), jnp.float32)], axis=1
    )
    out_own[part:] = jnp.concatenate([told, positions], axis=0).astype(jnp.bfloat16)
    out_block[...] = block_slots(owner_ref[...], sections, capr, block_rows)


def norm_kernel(blocks, features, half_ref, near_ref, far_ref, gain, gain_far, out_ref, done_ref):
    half, width = blocks // 2, out_ref.shape[2]
    near = near_ref[...].astype(jnp.float32)
    far = far_ref[...].astype(jnp.float32)
    total = jnp.sum(near * near, axis=1, keepdims=True) + jnp.sum(far * far, axis=1, keepdims=True)
    factor = lax.rsqrt(total * (1.0 / features) + 1e-06)
    for side, (ref, gains) in enumerate(((near_ref, gain), (far_ref, gain_far))):
        for j in range(half):
            at = pl.ds(j * width, width)
            block = ref[:, at].astype(jnp.float32) * factor * gains[:, at]
            out_ref[side * half + j] = block.astype(jnp.bfloat16)
    done_ref[...] = jnp.zeros_like(done_ref)


def normalize(blocks, half, near, far, gains):
    rows, features = near.shape
    width = 2 * features // blocks
    tile = 64
    rows_spec = pl.BlockSpec((tile, features), lambda i, h: (i, 0))
    return pl.pallas_call(
        functools.partial(norm_kernel, blocks, 2 * features),
        out_shape=(
            jax.ShapeDtypeStruct((blocks, rows, width), jnp.bfloat16),
            jax.ShapeDtypeStruct((8, LANES), jnp.float32),
        ),
        grid_spec=pltpu.PrefetchScalarGridSpec(
            num_scalar_prefetch=1,
            grid=(rows // tile,),
            in_specs=[
                rows_spec,
                rows_spec,
                pl.BlockSpec((1, features), lambda i, h: (0, h[0])),
                pl.BlockSpec((1, features), lambda i, h: (0, 1 - h[0])),
            ],
            out_specs=(
                pl.BlockSpec((blocks, tile, width), lambda i, h: (0, i, 0)),
                pl.BlockSpec((8, LANES), lambda i, h: (0, 0)),
            ),
        ),
        compiler_params=pltpu.CompilerParams(vmem_limit_bytes=VMEM),
        cost_estimate=cost(0, 8 * rows * 2 * features),
    )(half, near, far, gains, gains)


def pool_rows(pool_ref):
    block_rows = pool_ref.shape[1]
    pool = pool_ref[...].astype(jnp.float32)
    return jnp.concatenate([pool[:, i, :] for i in range(block_rows)], axis=0).astype(jnp.bfloat16)


def positions_in_slots(sent, source, cape):
    sources = sent.shape[0]
    slots = sources * cape
    column = iota((sources, slots), 1)
    rank = column - jnp.floor((column.astype(jnp.float32) + 0.5) * (1.0 / cape)).astype(jnp.int32) * cape
    at_source = (column >= source * cape) & (column < source * cape + cape)
    at_rank = (iota((LANES, slots), 0) == rank[:1]).astype(jnp.bfloat16)
    wide = jnp.dot(sent.astype(jnp.bfloat16), at_rank, preferred_element_type=jnp.float32)
    return jnp.sum(jnp.where(at_source, wide, 0.0), axis=0, keepdims=True).astype(jnp.int32)


def pool_kernel(cape, message_ref, pool_ref, owner_ref, fill_ref, out_ref, position_ref):
    sections, heads = out_ref.shape[0], out_ref.shape[1]
    held, block_rows, _ = pool_ref.shape
    request = iota((sections * GROUP, held), 0)
    owner = owner_ref[...]
    owned = (request >= owner * GROUP) & (request < owner * GROUP + GROUP)
    mask = jnp.concatenate(
        [(owned & (fill_ref[...] > i)).astype(jnp.float32) for i in range(block_rows)], axis=1
    )
    pool = pool_rows(pool_ref)
    for h in range(heads // GROUP):
        query = message_ref[:, h * GROUP : (h + 1) * GROUP, :].astype(jnp.float32)
        query = query.reshape(sections * GROUP, HD).astype(jnp.bfloat16)
        key = pool[:, 2 * h * HD : (2 * h + 1) * HD]
        value = pool[:, (2 * h + 1) * HD : (2 * h + 2) * HD]
        top, total, acc = attend(query, key, value, mask > 0.0)
        lane = iota((sections * GROUP, LANES), 1)
        state = jnp.where(lane == 0, top, jnp.where(lane == 1, total, 0.0))
        out_ref[:, h * GROUP : (h + 1) * GROUP, :HD] = acc.reshape(sections, GROUP, HD)
        out_ref[:, h * GROUP : (h + 1) * GROUP, HD:] = state.reshape(sections, GROUP, LANES)
    sent = message_ref[:, heads : heads + 1, :].astype(jnp.float32).reshape(sections, LANES)
    position_ref[...] = positions_in_slots(sent, iota((sections, 1), 0), cape)


def ring_pool_kernel(sections, cape, source_ref, *refs):
    told_refs = refs[:sections]
    pool_ref, owner_ref, fill_ref, out_ref, position_ref = refs[sections:]
    held, block_rows, _ = pool_ref.shape
    heads = out_ref.shape[1] // 2
    groups = heads // GROUP
    part = told_refs[0].shape[0] - GROUP - sections
    told = [ref[part:, :].astype(jnp.float32) for ref in told_refs]
    owner, fill = owner_ref[...], fill_ref[...]
    masks = []
    for j in range(sections):
        owned = owner == source_ref[j]
        mask = [(owned & (fill > i)).astype(jnp.float32) for i in range(block_rows)]
        masks.append(jnp.broadcast_to(jnp.concatenate(mask, axis=1), (GROUP, held * block_rows)))
    mask = jnp.concatenate(masks, axis=0) > 0.0
    pool = pool_rows(pool_ref)
    sums, states = [], []
    lane = iota((sections * GROUP, LANES), 1)
    for h in range(groups):
        query = jnp.concatenate([t[:GROUP, h * HD : (h + 1) * HD] for t in told], axis=0)
        key = pool[:, 2 * h * HD : (2 * h + 1) * HD]
        value = pool[:, (2 * h + 1) * HD : (2 * h + 2) * HD]
        top, total, acc = attend(query.astype(jnp.bfloat16), key, value, mask)
        terms = bf16_terms(top, 3) + bf16_terms(total, 2)
        state = jnp.zeros((sections * GROUP, LANES), jnp.float32)
        for k, term in enumerate(terms):
            state = jnp.where(lane == k, term, state)
        sums.append(acc)
        states.append(state)
    for j in range(sections):
        at = slice(j * GROUP, (j + 1) * GROUP)
        rows = jnp.concatenate([x[at] for x in sums] + [x[at] for x in states], axis=0)
        out_ref[source_ref[j]] = rows.astype(jnp.bfloat16)
    own = iota((sections, LANES), 0) == source_ref[0]
    sent = jnp.concatenate(
        [
            jnp.sum(jnp.where(own, t[GROUP:, :LANES], 0.0), axis=0, keepdims=True) for t in told
        ],
        axis=0,
    )
    source = jnp.zeros((sections, 1), jnp.int32)
    for j in range(sections):
        source = jnp.where(iota((sections, 1), 0) == j, source_ref[j], source)
    position_ref[...] = positions_in_slots(sent, source, cape)


def bf16_terms(value, count):
    terms = []
    for _ in range(count):
        term = value.astype(jnp.bfloat16).astype(jnp.float32)
        terms.append(term)
        value = value - term
    return terms


def attend(query, key, value, mask):
    scores = (
        lax.dot_general(query, key, (((1,), (1,)), ((), ())), preferred_element_type=jnp.float32)
        * SCALE
    )
    scores = jnp.where(mask, scores, NEG)
    top = jnp.max(scores, axis=1, keepdims=True)
    expo = jnp.where(mask, jnp.exp(scores - top), 0.0)
    total = jnp.sum(expo, axis=1, keepdims=True)
    acc = jnp.dot(expo.astype(jnp.bfloat16), value, preferred_element_type=jnp.float32)
    return top, total, acc


def product(rows_ref, block, quarter_ref, weights):
    near, middle, far = weights
    part = middle.shape[0] // 2
    turned = quarter_ref[0] * (2 * part + part)
    near_at = pl.multiple_of(turned, part)
    far_at = pl.multiple_of(3 * part - turned, part)

    def times(at, weight):
        return jnp.dot(rows_ref[block, :, at], weight, preferred_element_type=jnp.float32)

    return (
        times(pl.ds(part, 2 * part), middle)
        + times(pl.ds(near_at, part), near)
        + times(pl.ds(far_at, part), far)
    )


def step_kernel(
    step, index_ref, quarter_ref, text_ref, image_ref, near_up, middle_up, near_down, middle_down, far_ref,
    text_in, image_in, text_out, image_out
):
    part = middle_up.shape[0] // 2
    up = (near_up[:part], middle_up[...], far_ref[:part])
    down = (near_down[:part], middle_down[...], far_ref[part:])
    first, second = index_ref[2 * step - 1], index_ref[2 * step]
    for ref, given, out in ((text_ref, text_in, text_out), (image_ref, image_in, image_out)):
        out[...] = (
            given[...]
            + product(ref, first, quarter_ref, up)
            + product(ref, second, quarter_ref, down)
        )


def first_kernel(index_ref, text_ref, image_ref, weight_ref, text_out, image_out):
    weight = weight_ref[...]
    block = index_ref[0]
    text_out[...] = jnp.dot(text_ref[block], weight, preferred_element_type=jnp.float32)
    image_out[...] = jnp.dot(image_ref[block], weight, preferred_element_type=jnp.float32)


def last_kernel(
    step, index_ref, quarter_ref, text_ref, image_ref, near_ref, middle_ref, far_ref, text_in, image_in, bias_ref,
    slot_ref, partial_ref, text_out, send_out
):
    sections, cape, _ = send_out.shape
    width = image_in.shape[1]
    block = index_ref[step]
    weights = (near_ref[: middle_ref.shape[0] // 2], middle_ref[...], far_ref[...])
    image = image_in[...] + product(image_ref, block, quarter_ref, weights) + bias_ref[...]
    place = (iota((sections * cape, image.shape[0]), 0) == slot_ref[...]).astype(jnp.bfloat16)
    send = jnp.dot(place, image.astype(jnp.bfloat16), preferred_element_type=jnp.float32)
    send_out[:, :, :width] = send.astype(jnp.bfloat16).reshape(sections, cape, width)
    send_out[:, :, width:] = partial_ref[...]
    text = text_in[...] + product(text_ref, block, quarter_ref, weights) + bias_ref[...]
    text_out[...] = text.astype(jnp.bfloat16)


def finish_kernel(text_ref, image_ref, bias_ref, slot_ref, text_out, send_out):
    text_out[...] = (text_ref[...] + bias_ref[...]).astype(jnp.bfloat16)
    image = (image_ref[...] + bias_ref[...]).astype(jnp.bfloat16)
    place = (iota((send_out.shape[0], image.shape[0]), 0) == slot_ref[...]).astype(jnp.bfloat16)
    send_out[...] = jnp.dot(place, image, preferred_element_type=jnp.float32).astype(jnp.bfloat16)


def place_kernel(text_ref, arrived_ref, position_ref, slot_ref, count_ref, rows_ref, blocks_ref):
    rows = text_ref.shape[0]
    sections, cape, _ = arrived_ref.shape
    width = text_ref.shape[1]
    row = iota((rows, sections * cape), 0)
    match = (row == position_ref[...]) & (row < count_ref[0])
    filled = jnp.max(match.astype(jnp.float32), axis=1, keepdims=True) > 0.0
    arrived = arrived_ref[:, :, :width].astype(jnp.float32).reshape(sections * cape, width)
    placed = jnp.dot(
        match.astype(jnp.bfloat16), arrived.astype(jnp.bfloat16), preferred_element_type=jnp.float32
    )
    whole = jnp.where(filled, placed, text_ref[...].astype(jnp.float32)).astype(jnp.bfloat16)
    rows_ref[...] = whole
    slots = (iota((blocks_ref.shape[0], rows), 0) == slot_ref[...]).astype(jnp.bfloat16)
    blocks_ref[...] = jnp.dot(slots, whole, preferred_element_type=jnp.float32).astype(jnp.bfloat16)


def decode_kernel(packed, rows_ref, query_ref, partial_ref, length_ref, out_ref):
    rows = rows_ref.shape[0]
    heads = query_ref.shape[1] // HD
    mask = iota((GROUP, rows), 1) < length_ref[0]
    if packed:
        partial = partial_ref[:, : 2 * heads, rows_ref.shape[1] :].astype(jnp.float32)
    for h in range(heads // GROUP):
        at = slice(h * GROUP, (h + 1) * GROUP)
        key = rows_ref[:, 2 * h * HD : (2 * h + 1) * HD]
        value = rows_ref[:, (2 * h + 1) * HD : (2 * h + 2) * HD]
        query = query_group(query_ref, h).astype(jnp.bfloat16)
        top, total, acc = attend(query, key, value, mask)
        if packed:
            old_acc = partial[:, at, :]
            state = partial[:, heads + h * GROUP : heads + (h + 1) * GROUP, :]
            old_top = state[:, :, 0:1] + state[:, :, 1:2] + state[:, :, 2:3]
            old_total = state[:, :, 3:4] + state[:, :, 4:5]
        else:
            old_acc = partial_ref[:, at, :HD]
            old_top = partial_ref[:, at, HD : HD + 1]
            old_total = partial_ref[:, at, HD + 1 : HD + 2]
        best = jnp.maximum(top, jnp.max(old_top, axis=0))
        fresh_factor = jnp.exp(top - best)
        old_factor = jnp.exp(old_top - best[None])
        total = total * fresh_factor + jnp.sum(old_total * old_factor, axis=0)
        acc = acc * fresh_factor + jnp.sum(old_acc * old_factor, axis=0)
        result = (acc / total).astype(jnp.bfloat16)
        for j in range(GROUP):
            lane = (h * GROUP + j) * HD
            out_ref[:, lane : lane + HD] = result[j : j + 1]


def beside(x):
    return lax.ppermute(x, "tensor", [(0, 1), (1, 0)])


def exchange(x):
    return lax.all_to_all(x, "section", split_axis=0, concat_axis=0, tiled=True)


def ring_order(sections):
    return list(range(0, sections, 2)) + list(range(1, sections, 2))[::-1]


def ring_tables(sections, tensors):
    order = ring_order(sections)
    table = np.zeros((sections, tensors, 2 * sections), np.int32)
    distances = [0] + [s * d for d in range(1, sections // 2) for s in (1, -1)] + [sections // 2]
    for at, section in enumerate(order):
        for step, distance in enumerate(distances):
            source = order[(at - distance) % sections]
            for t in range(tensors):
                table[section, t, step] = (source - t * (sections // tensors)) % sections
            table[section, :, sections + step] = source
    return table


def after(values, *others):
    held = lax.optimization_barrier((tuple(values), others))
    return held[0]


def ring_path(
    text, image, target, weight, bias, gains, queries, pool, owner, fill, block_owner, half, cape, capr
):
    sections = lax.axis_size("section")
    order = ring_order(sections)
    ahead = [(order[i], order[(i + 1) % sections]) for i in range(sections)]
    back = [(b, a) for a, b in ahead]
    depth, width = weight.shape
    part = depth // 4
    rows = text.shape[0]
    heads = queries.shape[1] // HD
    group = lax.axis_index("groups").astype(jnp.int32)

    def up(x):
        return lax.ppermute(x, "section", ahead)

    def down(x):
        return lax.ppermute(x, "section", back)

    def across(x):
        return lax.ppermute(x, "groups", [(0, 1), (1, 0)])

    table = jnp.asarray(ring_tables(sections, lax.axis_size("tensor")))
    index = lax.dynamic_slice(
        table, (lax.axis_index("section"), lax.axis_index("tensor"), 0), (1, 1, 2 * sections)
    ).reshape(2 * sections)
    quarter = group.reshape(1)
    states = (jax.ShapeDtypeStruct((rows, width), jnp.float32),) * 2
    flops = 4 * rows * depth * width

    def step_product(step, state):
        return call(
            functools.partial(step_kernel, step), states, index, quarter, *normed,
            owns[step][0], middles[step][0], owns[step][1], middles[step][1], fars[step], *state,
            smem=(0, 1), aliases={9: 0, 10: 1}, cost=cost(2 * flops, 0),
        )

    own, middle, image_slot, block_slot = call(
        functools.partial(open_kernel, sections, cape, capr, pool.shape[1]),
        (
            jax.ShapeDtypeStruct((part + GROUP + sections, width), jnp.bfloat16),
            jax.ShapeDtypeStruct((2 * part, width), jnp.bfloat16),
            jax.ShapeDtypeStruct((1, rows), jnp.int32),
            jax.ShapeDtypeStruct((1, block_owner.shape[1] * pool.shape[1]), jnp.int32),
        ),
        quarter, weight, target, block_owner, queries,
        smem=(0,),
    )
    near_own = [up(own), down(own)]
    text_far = beside(text)
    near_middle = [up(middle), down(middle)]
    image_far = beside(image)
    last = sections // 2 - 1
    owns, middles, fars = {}, {}, {}
    told = [own]
    waiting, state = [], None
    for step in range(1, last + 1):
        *near_own, text_far = after((*near_own, text_far), *waiting)
        owns[step] = tuple(near_own)
        told += near_own
        fars[step] = across(jnp.concatenate([x[:part] for x in near_own], 0))
        near_own = [up(near_own[0])] + ([down(near_own[1])] if step < last else [])
        waiting = []
        if step == 1:
            normed_text, token = normalize(sections, half, text, text_far, gains)
            waiting = [token]
        elif step == 2:
            normed_image, token = normalize(sections, half, image, image_far, gains)
            normed = (normed_text, normed_image)
            state = call(
                first_kernel, states, index, *normed, weight, smem=(0,), cost=cost(flops, 0)
            )
            waiting = [token]
        else:
            state = step_product(step - 2, state)
            waiting = [*state]
        *near_middle, image_far = after((*near_middle, image_far), *waiting)
        middles[step] = tuple(near_middle)
        near_middle = ([up(near_middle[0])] if step < last else []) + [down(near_middle[1])]
        waiting = [fars[step]]
    state = step_product(last - 1, state)
    (last_own,) = after(near_own, *waiting, *state)
    last_far = across(last_own[:part])
    state = step_product(last, state)
    partial, position = call(
        functools.partial(ring_pool_kernel, sections, cape),
        (
            jax.ShapeDtypeStruct((sections, 2 * heads, HD), jnp.bfloat16),
            jax.ShapeDtypeStruct((1, sections * cape), jnp.int32),
        ),
        index[sections:], *told, last_own, pool, owner, fill,
        smem=(0,),
    )
    text_rows, send = call(
        functools.partial(last_kernel, sections - 1),
        (
            jax.ShapeDtypeStruct((rows, width), jnp.bfloat16),
            jax.ShapeDtypeStruct((sections, cape, width + HD), jnp.bfloat16),
        ),
        index, quarter, *normed, last_own, near_middle[0], last_far, *state, bias, image_slot, partial,
        smem=(0, 1), cost=cost(flops, 0),
    )
    arrived = exchange(send)
    return text_rows, arrived, position, block_slot, arrived


def gather_path(
    text, image, target, weight, bias, gains, queries, pool, owner, fill, block_owner, half, cape, capr
):
    sections = lax.axis_size("section")
    rows, near = text.shape
    width = weight.shape[1]
    heads = queries.shape[1] // HD
    image_slot, block_slot, message = call(
        functools.partial(prep_kernel, sections, cape, capr, pool.shape[1]),
        (
            jax.ShapeDtypeStruct((1, rows), jnp.int32),
            jax.ShapeDtypeStruct((1, block_owner.shape[1] * pool.shape[1]), jnp.int32),
            jax.ShapeDtypeStruct((sections, 2 * heads, LANES), jnp.bfloat16),
        ),
        target, block_owner, queries,
    )
    partial, position = call(
        functools.partial(pool_kernel, cape),
        (
            jax.ShapeDtypeStruct((sections, heads, 2 * HD), jnp.float32),
            jax.ShapeDtypeStruct((1, sections * cape), jnp.int32),
        ),
        exchange(message), pool, owner, fill,
    )
    normed = [normalize(2, half, x, beside(x), gains)[0] for x in (text, image)]
    whole = lax.all_gather(weight, "section", axis=0, tiled=True)
    first = lax.dynamic_slice_in_dim(whole, half[0] * near, near, 0)
    second = lax.dynamic_slice_in_dim(whole, (1 - half[0]) * near, near, 0)
    text_sum, image_sum = (
        jnp.dot(n[0], first, preferred_element_type=jnp.float32)
        + jnp.dot(n[1], second, preferred_element_type=jnp.float32)
        for n in normed
    )
    text_rows, send = call(
        finish_kernel,
        (
            jax.ShapeDtypeStruct((rows, width), jnp.bfloat16),
            jax.ShapeDtypeStruct((sections * cape, width), jnp.bfloat16),
        ),
        text_sum, image_sum, bias, image_slot,
    )
    arrived = exchange(send.reshape(sections, cape, width))
    return text_rows, arrived, position, block_slot, exchange(partial)


def shards(
    text_embed,
    image_embed,
    image_count,
    prompt_len,
    embed_target,
    kv_weight,
    kv_bias,
    norm_gain,
    queries,
    old_pool,
    pool_owner,
    pool_fill,
    block_owner,
):
    sections, tensors = lax.axis_size("section"), lax.axis_size("tensor")
    rows = text_embed.shape[0]
    width = kv_weight.shape[1]
    heads = queries.shape[1] // HD
    cape = rows // sections
    block_rows = old_pool.shape[1]
    capr = (block_owner.shape[0] + sections - 1) // sections * block_rows
    ring = (
        sections == 8
        and tensors == 2
        and lax.axis_size("groups") == 2
        and kv_weight.shape[0] % (8 * LANES) == 0
        and cape == 2 * heads
    )
    text_rows, arrived, position, block_slot, partial = (ring_path if ring else gather_path)(
        text_embed,
        image_embed,
        embed_target.reshape(1, -1),
        kv_weight,
        kv_bias.reshape(1, -1),
        norm_gain.reshape(1, -1),
        queries,
        old_pool,
        pool_owner.reshape(1, -1),
        pool_fill.reshape(1, -1),
        block_owner.reshape(1, -1),
        lax.axis_index("tensor").astype(jnp.int32).reshape(1),
        cape,
        capr,
    )
    whole_rows, block_data = call(
        place_kernel,
        (
            jax.ShapeDtypeStruct((rows, width), jnp.bfloat16),
            jax.ShapeDtypeStruct((sections * capr, width), jnp.bfloat16),
        ),
        text_rows,
        arrived,
        position,
        block_slot,
        image_count,
        smem=(4,),
    )
    fresh = exchange(block_data.reshape(sections, capr, width)).reshape(sections * capr, width)
    decoded = call(
        functools.partial(decode_kernel, ring),
        jax.ShapeDtypeStruct((1, heads * HD), jnp.bfloat16),
        whole_rows,
        queries,
        partial,
        prompt_len,
        smem=(3,),
    )
    return decoded, fresh


def solution(mesh):
    return jax.shard_map(
        shards,
        mesh=mesh,
        in_specs=(
            P(("groups", "section"), "tensor"),
            P(("groups", "section"), "tensor"),
            P(("groups", "section")),
            P(("groups", "section")),
            P(("groups", "section")),
            P("section", "tensor"),
            P("tensor"),
            P(),
            P(("groups", "section"), "tensor"),
            P(("groups", "section"), None, "tensor"),
            P(("groups", "section")),
            P(("groups", "section")),
            P(("groups", "section")),
        ),
        out_specs=(P(("groups", "section"), "tensor"), P(("groups", "section"), "tensor")),
        check_vma=False,
    )
```

time: 151 us -> 112 us (0.74)
  matrix products: 13 us -> 0 us
  starting transfers between devices: 43.1 us -> 33.1 us
  waiting for transfers between devices: 49.8 us -> 41.8 us
  local copies, waits for them, and re-layouts: 15.5 us -> 11.8 us
  other arithmetic: 3.97 us -> 0.95 us
    ppermute x7, waiting for transfers between devices: 27.1 us -> 11.1 us  [down(): return lax.ppermute(x, 'section', back)]
    dot_general x8 -> x0, matrix products: 13 us -> none  [product(): jnp.dot(normed[slot, :, first:last], block, preferred_element_type=jnp.fl...]
    unnamed x26 -> x47, local copies, waits for them, and re-layouts: 2.73 us -> 10.2 us
    all_to_all x4 -> x2, starting transfers between devices: 16.7 us -> 9.22 us  [exchange(): return lax.all_to_all(x, 'section', split_axis=0, concat_axis=0, tiled=True)]
    slice x4 -> x8, local copies, waits for them, and re-layouts: 6.25 us -> 0.2 us  [the longest x6 0.11 us: ring_path(): fars[step] = across(jnp.concatenate([x[:part] for x in near_own], 0))]
    ppermute x8 -> x7, waiting for transfers between devices: 10.7 us -> 16.3 us  [up(): return lax.ppermute(x, 'section', ahead)]
    ppermute x7, starting transfers between devices: 12.1 us -> 7.42 us  [down(): return lax.ppermute(x, 'section', back)]
    ppermute x8 -> x7, starting transfers between devices: 6.19 us -> 10.5 us  [up(): return lax.ppermute(x, 'section', ahead)]
  transfers between devices with their start and end apart: 28 -> 22, of which waited for: 9 -> 10; matrix products, arithmetic and copies ran while one was open for 20% -> 2% of each run, Pallas kernels for 15% -> 16%
where the time goes in v2:
time: 112 us; the launch traced here: 111 us
  waiting for transfers between devices  41.8 us (37%)
  starting transfers between devices  33.1 us (30%)
  Pallas kernels  21.6 us (19%)
  local copies, waits for them, and re-layouts  11.8 us (11%)
  between operations  2.15 us (2%)
    ppermute x7, waiting for transfers between devices, up(): return lax.ppermute(x, 'section', ahead)  16.3 us
    all_to_all x2, waiting for transfers between devices, exchange(): return lax.all_to_all(x, 'section', split_axis=0, concat_axis=0, tiled=True)  14.2 us
    pallas_call x9, Pallas kernels, call(): pl.pallas_call(kernel, out_shape=outs, in_specs=[pl.BlockSpec(memory_spac...  13.8 us
    ppermute x7, waiting for transfers between devices, down(): return lax.ppermute(x, 'section', back)  11.1 us
    ppermute x7, starting transfers between devices, up(): return lax.ppermute(x, 'section', ahead)  10.5 us
    unnamed x47, local copies, waits for them, and re-layouts  10.2 us
    all_to_all x2, starting transfers between devices, exchange(): return lax.all_to_all(x, 'section', split_axis=0, concat_axis=0, tiled=True)  9.22 us
    pallas_call x2, Pallas kernels, normalize(): pl.pallas_call(functools.partial(norm_kernel, blocks, 2 * features), out_...  7.8 us
  transfers between devices with their start and end apart: 22, of which 10 were waited for; matrix products, arithmetic and copies ran while one was open for 2% of the time, Pallas kernels for 16%

profile of v2, /device:TPU:0, one launch (start us, length us, event | category | flops | bytes accessed | tf_op | source)
XLA Modules:
  0.0 111.4 jit_solution(18030185243094024093)
XLA Ops:
  4.9 3.1 %collective-permute-start = (bf16[272,512]{1,0:T(8,128)(2,1)S(1)}, bf16[272,512]{1,0:T(8,128)(2,1)S(1)}, u32[]{:S(2)}, u32[]{:S(2)}) collective-permute-start(bf16[272,512]{1,0:T(8,128)(2,1)S(1)} %get-tuple-element.37.refs_0_), channel_id=1, source_target_pairs={{0,4},{4,8},{8,12},{12,14},{14,10},{10,6},{6,2},{2,0},{1,5},{5,9},... | collective-permute-start | bytes 835592 | tf_op jit(solution)/shard_map/ppermute | solution.py:434
  7.9 2.0 %collective-permute-start.3 = (bf16[512,512]{1,0:T(8,128)(2,1)S(1)}, bf16[512,512]{1,0:T(8,128)(2,1)S(1)}, u32[]{:S(2)}, u32[]{:S(2)}) collective-permute-start(bf16[512,512]{1,0:T(8,128)(2,1)S(1)} %get-tuple-element.40), channel_id=1, source_target_pairs={{0,4},{4,8},{8,12},{12,14},{14,10},{10,6},{6,2},{2,0},{1,5},{5,9},... | collective-permute-start | bytes 1572872 | tf_op jit(solution)/shard_map/ppermute | solution.py:434
  10.0 5.3 %collective-permute-done.near_up.refs_1_ = bf16[272,512]{1,0:T(8,128)(2,1)S(1)} collective-permute-done((bf16[272,512]{1,0:T(8,128)(2,1)S(1)}, bf16[272,512]{1,0:T(8,128)(2,1)S(1)}, u32[]{:S(2)}, u32[]{:S(2)}) %collective-permute-start) | collective-permute-done | bytes 278560 | tf_op jit(solution)/shard_map/ppermute | solution.py:434
  15.3 2.1 %collective-permute-start.4 = (bf16[512,512]{1,0:T(8,128)(2,1)S(1)}, bf16[512,512]{1,0:T(8,128)(2,1)S(1)}, u32[]{:S(2)}, u32[]{:S(2)}) collective-permute-start(bf16[512,512]{1,0:T(8,128)(2,1)S(1)} %get-tuple-element.40), channel_id=1, source_target_pairs={{4,0},{8,4},{12,8},{14,12},{10,14},{6,10},{2,6},{0,2},{5,1},{9,5},... | collective-permute-start | bytes 1572872 | tf_op jit(solution)/shard_map/ppermute | solution.py:437
  19.6 6.9 %collective-permute-done.3.middle_up = bf16[512,512]{1,0:T(8,128)(2,1)S(1)} collective-permute-done((bf16[512,512]{1,0:T(8,128)(2,1)S(1)}, bf16[512,512]{1,0:T(8,128)(2,1)S(1)}, u32[]{:S(2)}, u32[]{:S(2)}) %collective-permute-start.3) | collective-permute-done | bytes 524320 | tf_op jit(solution)/shard_map/ppermute | solution.py:434
  26.5 2.1 %collective-permute-start.7 = (bf16[272,512]{1,0:T(8,128)(2,1)S(1)}, bf16[272,512]{1,0:T(8,128)(2,1)S(1)}, u32[]{:S(2)}, u32[]{:S(2)}) collective-permute-start(bf16[272,512]{1,0:T(8,128)(2,1)S(1)} %collective-permute-done.1.near_down.refs_2_), channel_id=1, source_target_pairs={{4,0},{8,4},{12,8},{14,12},{10,14},{6,10},{2,6},{0,2},{5,1},{9,5},... | collective-permute-start | bytes 835592 | tf_op jit(solution)/shard_map/ppermute | solution.py:437
  33.6 2.6 %collective-permute-done.7.near_down.refs_4_ = bf16[272,512]{1,0:T(8,128)(2,1)S(1)} collective-permute-done((bf16[272,512]{1,0:T(8,128)(2,1)S(1)}, bf16[272,512]{1,0:T(8,128)(2,1)S(1)}, u32[]{:S(2)}, u32[]{:S(2)}) %collective-permute-start.7) | collective-permute-done | bytes 278560 | tf_op jit(solution)/shard_map/ppermute | solution.py:437
  37.1 1.7 %collective-permute-start.11 = (bf16[512,512]{1,0:T(8,128)(2,1)S(1)}, bf16[512,512]{1,0:T(8,128)(2,1)S(1)}, u32[]{:S(2)}, u32[]{:S(2)}) collective-permute-start(bf16[512,512]{1,0:T(8,128)(2,1)S(1)} %pad_maximum_fusion.1), channel_id=1, source_target_pairs={{0,16},{16,0},{1,17},{17,1},{2,18},{18,2},{3,19},{19,3},{4,20},{20... | collective-permute-start | bytes 1572872 | tf_op jit(solution)/shard_map/ppermute | solution.py:440
  40.9 4.0 %collective-permute-done.14.middle_up = bf16[512,512]{1,0:T(8,128)(2,1)S(1)} collective-permute-done((bf16[512,512]{1,0:T(8,128)(2,1)S(1)}, bf16[512,512]{1,0:T(8,128)(2,1)S(1)}, u32[]{:S(2)}, u32[]{:S(2)}) %collective-permute-start.14) | collective-permute-done | bytes 524320 | tf_op jit(solution)/shard_map/ppermute | solution.py:434
  44.8 2.7 %collective-permute-done.15.middle_down = bf16[512,512]{1,0:T(8,128)(2,1)S(1)} collective-permute-done((bf16[512,512]{1,0:T(8,128)(2,1)S(1)}, bf16[512,512]{1,0:T(8,128)(2,1)S(1)}, u32[]{:S(2)}, u32[]{:S(2)}) %collective-permute-start.15) | collective-permute-done | bytes 524320 | tf_op jit(solution)/shard_map/ppermute | solution.py:437
  47.5 1.7 %collective-permute-start.16 = (bf16[512,512]{1,0:T(8,128)(2,1)S(1)}, bf16[512,512]{1,0:T(8,128)(2,1)}, u32[]{:S(2)}, u32[]{:S(2)}) collective-permute-start(bf16[512,512]{1,0:T(8,128)(2,1)S(1)} %collective-permute-done.14.middle_up), channel_id=1, source_target_pairs={{0,4},{4,8},{8,12},{12,14},{14,10},{10,6},{6,2},{2,0},{1,5},{5,9},... | collective-permute-start | bytes 1572872 | tf_op jit(solution)/shard_map/ppermute | solution.py:434
  49.5 3.9 %collective-permute-done.10.near_down.refs_6_ = bf16[272,512]{1,0:T(8,128)(2,1)S(1)} collective-permute-done((bf16[272,512]{1,0:T(8,128)(2,1)S(1)}, bf16[272,512]{1,0:T(8,128)(2,1)S(1)}, u32[]{:S(2)}, u32[]{:S(2)}) %collective-permute-start.10) | collective-permute-done | bytes 278560 | tf_op jit(solution)/shard_map/ppermute | solution.py:437
  59.2 4.7 %shard_map.150 = (bf16[8,256,1024]{2,1,0:T(8,128)(2,1)S(1)}, f32[8,128]{1,0:T(8,128)}) custom-call(s32[1]{0:T(128)} %bitcast.2.half_ref, bf16[256,4096]{1,0:T(8,128)(2,1)S(1)} %copy-done.2, bf16[256,4096]{1,0:T(8,128)(2,1)} %collective-permute-done.2.far_ref, f32[1,8192]{1,0:T(1,128)S(1)} %bitcast.14, f32[1,8192]{1,0:T(1,128)S(1)} %bitcast.15), custom_call_target="tpu_custom_call" | custom-call | bytes 16777216 | tf_op jit(solution)/shard_map/pallas_call | solution.py:143
  63.9 3.1 %shard_map.151 = (bf16[8,256,1024]{2,1,0:T(8,128)(2,1)S(1)}, f32[8,128]{1,0:T(8,128)}) custom-call(s32[1]{0:T(128)} %bitcast.2.half_ref, bf16[256,4096]{1,0:T(8,128)(2,1)S(1)} %copy-done.3, bf16[256,4096]{1,0:T(8,128)(2,1)S(1)} %copy-done.5, f32[1,8192]{1,0:T(1,128)S(1)} %bitcast.16, f32[1,8192]{1,0:T(1,128)S(1)} %bitcast.17), custom_call_target="tpu_custom_call" | custom-call | bytes 16777216 | tf_op jit(solution)/shard_map/pallas_call | solution.py:143
  68.3 1.6 %collective-permute-start.12 = (bf16[272,512]{1,0:T(8,128)(2,1)S(1)}, bf16[272,512]{1,0:T(8,128)(2,1)S(1)}, u32[]{:S(2)}, u32[]{:S(2)}) collective-permute-start(bf16[272,512]{1,0:T(8,128)(2,1)S(1)} %collective-permute-done.9.near_up.refs_5_), channel_id=1, source_target_pairs={{0,4},{4,8},{8,12},{12,14},{14,10},{10,6},{6,2},{2,0},{1,5},{5,9},... | collective-permute-start | bytes 835592 | tf_op jit(solution)/shard_map/ppermute | solution.py:434
  69.9 1.9 %shard_map.153 = (f32[256,512]{1,0:T(8,128)S(1)}, f32[256,512]{1,0:T(8,128)S(1)}) custom-call(s32[16]{0:T(128)S(1)} %fusion.index_ref, s32[1]{0:T(128)} %bitcast.1.group_ref.quarter_ref, bf16[8,256,1024]{2,1,0:T(8,128)(2,1)S(1)} %get-tuple-element.39.text_ref, ...), custom_call_target="tpu_custom_call", output_to_operand_aliasing={{0}: (9, {}), {1}: (10, {})} | custom-call | flops 1073741824 | tf_op jit(solution)/shard_map/pallas_call | solution.py:26
  73.0 1.8 %shard_map.154 = (f32[256,512]{1,0:T(8,128)S(1)}, f32[256,512]{1,0:T(8,128)S(1)}) custom-call(s32[16]{0:T(128)S(1)} %fusion.index_ref, s32[1]{0:T(128)} %bitcast.1.group_ref.quarter_ref, bf16[8,256,1024]{2,1,0:T(8,128)(2,1)S(1)} %get-tuple-element.39.text_ref, ...), custom_call_target="tpu_custom_call", output_to_operand_aliasing={{0}: (9, {}), {1}: (10, {})} | custom-call | flops 1073741824 | tf_op jit(solution)/shard_map/pallas_call | solution.py:26
  76.7 2.6 %shard_map.155 = (f32[256,512]{1,0:T(8,128)S(1)}, f32[256,512]{1,0:T(8,128)S(1)}) custom-call(s32[16]{0:T(128)S(1)} %fusion.index_ref, s32[1]{0:T(128)} %bitcast.1.group_ref.quarter_ref, bf16[8,256,1024]{2,1,0:T(8,128)(2,1)S(1)} %get-tuple-element.39.text_ref, ...), custom_call_target="tpu_custom_call", output_to_operand_aliasing={{0}: (9, {}), {1}: (10, {})} | custom-call | flops 1073741824 | tf_op jit(solution)/shard_map/pallas_call | solution.py:26
  79.4 1.9 %collective-permute-done.18.middle_ref = bf16[512,512]{1,0:T(8,128)(2,1)S(1)} collective-permute-done((bf16[512,512]{1,0:T(8,128)(2,1)}, bf16[512,512]{1,0:T(8,128)(2,1)S(1)}, u32[]{:S(2)}, u32[]{:S(2)}) %collective-permute-start.18) | collective-permute-done | bytes 524320 | tf_op jit(solution)/shard_map/ppermute | solution.py:437
  81.3 2.1 %shard_map.157 = (bf16[256,512]{1,0:T(8,128)(2,1)S(1)}, bf16[8,32,640]{2,1,0:T(8,128)(2,1)}) custom-call(s32[16]{0:T(128)S(1)} %fusion.index_ref, s32[1]{0:T(128)} %bitcast.1.group_ref.quarter_ref, bf16[8,256,1024]{2,1,0:T(8,128)(2,1)S(1)} %get-tuple-element.39.text_ref, bf16[8,256,1024]{2,1,0:T(8,128)(2,1)S(1)} %get-tuple-element.42.image_ref, ...), custom_call_target="tpu_custom_call" | custom-call | flops 536870912 | tf_op jit(solution)/shard_map/pallas_call | solution.py:26
  83.5 5.8 %all-to-all-start = ((bf16[8,32,640]{2,1,0:T(8,128)(2,1)}), bf16[8,32,640]{2,1,0:T(8,128)(2,1)S(1)}, u32[]{:S(2)}, u32[]{:S(2)}) async-start(bf16[8,32,640]{2,1,0:T(8,128)(2,1)} %get-tuple-element.67), calls=%async_computation | async-start | bytes 655360 | tf_op jit(solution)/shard_map/all_to_all | solution.py:395
  89.9 8.0 %all-to-all-done.arrived_ref.partial_ref = bf16[8,32,640]{2,1,0:T(8,128)(2,1)S(1)} async-done(((bf16[8,32,640]{2,1,0:T(8,128)(2,1)}), bf16[8,32,640]{2,1,0:T(8,128)(2,1)S(1)}, u32[]{:S(2)}, u32[]{:S(2)}) %all-to-all-start) | async-done | bytes 327712 | tf_op jit(solution)/shard_map/all_to_all | solution.py:395
  99.1 3.4 %all-to-all-start.1 = ((bf16[8,32,512]{2,1,0:T(8,128)(2,1)}), bf16[8,32,512]{2,1,0:T(8,128)(2,1)S(1)}, u32[]{:S(2)}, u32[]{:S(2)}) async-start(bf16[8,32,512]{2,1,0:T(8,128)(2,1)} %bitcast.10), calls=%async_computation.1 | async-start | bytes 524288 | tf_op jit(solution)/shard_map/all_to_all | solution.py:395
  104.5 6.2 %all-to-all-done.1 = bf16[8,32,512]{2,1,0:T(8,128)(2,1)S(1)} async-done(((bf16[8,32,512]{2,1,0:T(8,128)(2,1)}), bf16[8,32,512]{2,1,0:T(8,128)(2,1)S(1)}, u32[]{:S(2)}, u32[]{:S(2)}) %all-to-all-start.1) | async-done | bytes 262176 | tf_op jit(solution)/shard_map/all_to_all | solution.py:395
  (91 shorter events, 28.0 us)
Async XLA Ops:
  0.6 16.7 %collective-permute-start.2 = (bf16[256,4096]{1,0:T(8,128)(2,1)}, bf16[256,4096]{1,0:T(8,128)(2,1)}, u32[]{:S(2)}, u32[]{:S(2)}) collective-permute-start(bf16[256,4096]{1,0:T(8,128)(2,1)} %near_ref.2), channel_id=1, source_target_pairs={{0,1},{1,0},{2,3},{3,2},{4,5},{5,4},{6,7},{7,6},{8,9},{9,8},{10,11... | collective-permute-start | bytes 6291464 | tf_op jit(solution)/shard_map/ppermute | solution.py:391
  1.1 27.5 %collective-permute-start.5 = (bf16[256,4096]{1,0:T(8,128)(2,1)}, bf16[256,4096]{1,0:T(8,128)(2,1)S(1)}, u32[]{:S(2)}, u32[]{:S(2)}) collective-permute-start(bf16[256,4096]{1,0:T(8,128)(2,1)} %near_ref.3), channel_id=1, source_target_pairs={{0,1},{1,0},{2,3},{3,2},{4,5},{5,4},{6,7},{7,6},{8,9},{9,8},{10,11... | collective-permute-start | bytes 6291464 | tf_op jit(solution)/shard_map/ppermute | solution.py:391
  4.9 10.4 %collective-permute-start = (bf16[272,512]{1,0:T(8,128)(2,1)S(1)}, bf16[272,512]{1,0:T(8,128)(2,1)S(1)}, u32[]{:S(2)}, u32[]{:S(2)}) collective-permute-start(bf16[272,512]{1,0:T(8,128)(2,1)S(1)} %get-tuple-element.37.refs_0_), channel_id=1, source_target_pairs={{0,4},{4,8},{8,12},{12,14},{14,10},{10,6},{6,2},{2,0},{1,5},{5,9},... | collective-permute-start | bytes 835592 | tf_op jit(solution)/shard_map/ppermute | solution.py:434
  7.9 9.4 %collective-permute-start.1 = (bf16[272,512]{1,0:T(8,128)(2,1)S(1)}, bf16[272,512]{1,0:T(8,128)(2,1)S(1)}, u32[]{:S(2)}, u32[]{:S(2)}) collective-permute-start(bf16[272,512]{1,0:T(8,128)(2,1)S(1)} %get-tuple-element.37.refs_0_), channel_id=1, source_target_pairs={{4,0},{8,4},{12,8},{14,12},{10,14},{6,10},{2,6},{0,2},{5,1},{9,5},... | collective-permute-start | bytes 835592 | tf_op jit(solution)/shard_map/ppermute | solution.py:437
  7.9 18.6 %collective-permute-start.3 = (bf16[512,512]{1,0:T(8,128)(2,1)S(1)}, bf16[512,512]{1,0:T(8,128)(2,1)S(1)}, u32[]{:S(2)}, u32[]{:S(2)}) collective-permute-start(bf16[512,512]{1,0:T(8,128)(2,1)S(1)} %get-tuple-element.40), channel_id=1, source_target_pairs={{0,4},{4,8},{8,12},{12,14},{14,10},{10,6},{6,2},{2,0},{1,5},{5,9},... | collective-permute-start | bytes 1572872 | tf_op jit(solution)/shard_map/ppermute | solution.py:434
  15.3 13.3 %collective-permute-start.4 = (bf16[512,512]{1,0:T(8,128)(2,1)S(1)}, bf16[512,512]{1,0:T(8,128)(2,1)S(1)}, u32[]{:S(2)}, u32[]{:S(2)}) collective-permute-start(bf16[512,512]{1,0:T(8,128)(2,1)S(1)} %get-tuple-element.40), channel_id=1, source_target_pairs={{4,0},{8,4},{12,8},{14,12},{10,14},{6,10},{2,6},{0,2},{5,1},{9,5},... | collective-permute-start | bytes 1572872 | tf_op jit(solution)/shard_map/ppermute | solution.py:437
  17.5 40.1 %copy-start.6 = (f32[8192]{0:T(1024)S(1)}, f32[8192]{0:T(1024)}, u32[]{:S(2)}) copy-start(f32[8192]{0:T(1024)} %param.21) | copy-start | bytes 98308
  17.5 18.8 %collective-permute-start.8 = (bf16[512,512]{1,0:T(8,128)(2,1)S(1)}, bf16[512,512]{1,0:T(8,128)(2,1)S(1)}, u32[]{:S(2)}, u32[]{:S(2)}) collective-permute-start(bf16[512,512]{1,0:T(8,128)(2,1)S(1)} %pad_maximum_fusion), channel_id=1, source_target_pairs={{0,16},{16,0},{1,17},{17,1},{2,18},{18,2},{3,19},{19,3},{4,20},{20... | collective-permute-start | bytes 1572872 | tf_op jit(solution)/shard_map/ppermute | solution.py:440
  19.1 14.6 %collective-permute-start.6 = (bf16[272,512]{1,0:T(8,128)(2,1)S(1)}, bf16[272,512]{1,0:T(8,128)(2,1)S(1)}, u32[]{:S(2)}, u32[]{:S(2)}) collective-permute-start(bf16[272,512]{1,0:T(8,128)(2,1)S(1)} %collective-permute-done.near_up.refs_1_), channel_id=1, source_target_pairs={{0,4},{4,8},{8,12},{12,14},{14,10},{10,6},{6,2},{2,0},{1,5},{5,9},... | collective-permute-start | bytes 835592 | tf_op jit(solution)/shard_map/ppermute | solution.py:434
  26.5 9.7 %collective-permute-start.7 = (bf16[272,512]{1,0:T(8,128)(2,1)S(1)}, bf16[272,512]{1,0:T(8,128)(2,1)S(1)}, u32[]{:S(2)}, u32[]{:S(2)}) collective-permute-start(bf16[272,512]{1,0:T(8,128)(2,1)S(1)} %collective-permute-done.1.near_down.refs_2_), channel_id=1, source_target_pairs={{4,0},{8,4},{12,8},{14,12},{10,14},{6,10},{2,6},{0,2},{5,1},{9,5},... | collective-permute-start | bytes 835592 | tf_op jit(solution)/shard_map/ppermute | solution.py:437
  30.0 14.9 %collective-permute-start.14 = (bf16[512,512]{1,0:T(8,128)(2,1)S(1)}, bf16[512,512]{1,0:T(8,128)(2,1)S(1)}, u32[]{:S(2)}, u32[]{:S(2)}) collective-permute-start(bf16[512,512]{1,0:T(8,128)(2,1)S(1)} %collective-permute-done.3.middle_up), channel_id=1, source_target_pairs={{0,4},{4,8},{8,12},{12,14},{14,10},{10,6},{6,2},{2,0},{1,5},{5,9},... | collective-permute-start | bytes 1572872 | tf_op jit(solution)/shard_map/ppermute | solution.py:434
  31.8 15.7 %collective-permute-start.15 = (bf16[512,512]{1,0:T(8,128)(2,1)S(1)}, bf16[512,512]{1,0:T(8,128)(2,1)S(1)}, u32[]{:S(2)}, u32[]{:S(2)}) collective-permute-start(bf16[512,512]{1,0:T(8,128)(2,1)S(1)} %collective-permute-done.4.middle_down), channel_id=1, source_target_pairs={{4,0},{8,4},{12,8},{14,12},{10,14},{6,10},{2,6},{0,2},{5,1},{9,5},... | collective-permute-start | bytes 1572872 | tf_op jit(solution)/shard_map/ppermute | solution.py:437
  37.1 16.3 %collective-permute-start.11 = (bf16[512,512]{1,0:T(8,128)(2,1)S(1)}, bf16[512,512]{1,0:T(8,128)(2,1)S(1)}, u32[]{:S(2)}, u32[]{:S(2)}) collective-permute-start(bf16[512,512]{1,0:T(8,128)(2,1)S(1)} %pad_maximum_fusion.1), channel_id=1, source_target_pairs={{0,16},{16,0},{1,17},{17,1},{2,18},{18,2},{3,19},{19,3},{4,20},{20... | collective-permute-start | bytes 1572872 | tf_op jit(solution)/shard_map/ppermute | solution.py:440
  38.8 14.6 %collective-permute-start.10 = (bf16[272,512]{1,0:T(8,128)(2,1)S(1)}, bf16[272,512]{1,0:T(8,128)(2,1)S(1)}, u32[]{:S(2)}, u32[]{:S(2)}) collective-permute-start(bf16[272,512]{1,0:T(8,128)(2,1)S(1)} %collective-permute-done.7.near_down.refs_4_), channel_id=1, source_target_pairs={{4,0},{8,4},{12,8},{14,12},{10,14},{6,10},{2,6},{0,2},{5,1},{9,5},... | collective-permute-start | bytes 835592 | tf_op jit(solution)/shard_map/ppermute | solution.py:437
  40.3 13.1 %collective-permute-start.9 = (bf16[272,512]{1,0:T(8,128)(2,1)S(1)}, bf16[272,512]{1,0:T(8,128)(2,1)S(1)}, u32[]{:S(2)}, u32[]{:S(2)}) collective-permute-start(bf16[272,512]{1,0:T(8,128)(2,1)S(1)} %collective-permute-done.6.near_up.refs_3_), channel_id=1, source_target_pairs={{0,4},{4,8},{8,12},{12,14},{14,10},{10,6},{6,2},{2,0},{1,5},{5,9},... | collective-permute-start | bytes 835592 | tf_op jit(solution)/shard_map/ppermute | solution.py:434
  47.5 24.3 %collective-permute-start.16 = (bf16[512,512]{1,0:T(8,128)(2,1)S(1)}, bf16[512,512]{1,0:T(8,128)(2,1)}, u32[]{:S(2)}, u32[]{:S(2)}) collective-permute-start(bf16[512,512]{1,0:T(8,128)(2,1)S(1)} %collective-permute-done.14.middle_up), channel_id=1, source_target_pairs={{0,4},{4,8},{8,12},{12,14},{14,10},{10,6},{6,2},{2,0},{1,5},{5,9},... | collective-permute-start | bytes 1572872 | tf_op jit(solution)/shard_map/ppermute | solution.py:434
  49.2 22.6 %collective-permute-start.17 = (bf16[512,512]{1,0:T(8,128)(2,1)S(1)}, bf16[512,512]{1,0:T(8,128)(2,1)}, u32[]{:S(2)}, u32[]{:S(2)}) collective-permute-start(bf16[512,512]{1,0:T(8,128)(2,1)S(1)} %collective-permute-done.15.middle_down), channel_id=1, source_target_pairs={{4,0},{8,4},{12,8},{14,12},{10,14},{6,10},{2,6},{0,2},{5,1},{9,5},... | collective-permute-start | bytes 1572872 | tf_op jit(solution)/shard_map/ppermute | solution.py:437
  55.3 19.6 %collective-permute-start.13 = (bf16[512,512]{1,0:T(8,128)(2,1)}, bf16[512,512]{1,0:T(8,128)(2,1)}, u32[]{:S(2)}, u32[]{:S(2)}) collective-permute-start(bf16[512,512]{1,0:T(8,128)(2,1)} %pad_maximum_fusion.2), channel_id=1, source_target_pairs={{0,16},{16,0},{1,17},{17,1},{2,18},{18,2},{3,19},{19,3},{4,20},{20... | collective-permute-start | bytes 1572872 | tf_op jit(solution)/shard_map/ppermute | solution.py:440
  68.3 6.6 %collective-permute-start.12 = (bf16[272,512]{1,0:T(8,128)(2,1)S(1)}, bf16[272,512]{1,0:T(8,128)(2,1)S(1)}, u32[]{:S(2)}, u32[]{:S(2)}) collective-permute-start(bf16[272,512]{1,0:T(8,128)(2,1)S(1)} %collective-permute-done.9.near_up.refs_5_), channel_id=1, source_target_pairs={{0,4},{4,8},{8,12},{12,14},{14,10},{10,6},{6,2},{2,0},{1,5},{5,9},... | collective-permute-start | bytes 835592 | tf_op jit(solution)/shard_map/ppermute | solution.py:434
  71.8 9.4 %collective-permute-start.18 = (bf16[512,512]{1,0:T(8,128)(2,1)}, bf16[512,512]{1,0:T(8,128)(2,1)S(1)}, u32[]{:S(2)}, u32[]{:S(2)}) collective-permute-start(bf16[512,512]{1,0:T(8,128)(2,1)} %collective-permute-done.17.middle_down), channel_id=1, source_target_pairs={{4,0},{8,4},{12,8},{14,12},{10,14},{6,10},{2,6},{0,2},{5,1},{9,5},... | collective-permute-start | bytes 1572872 | tf_op jit(solution)/shard_map/ppermute | solution.py:437
  74.9 6.4 %collective-permute-start.19 = (bf16[256,512]{1,0:T(8,128)(2,1)S(1)}, bf16[256,512]{1,0:T(8,128)(2,1)S(1)}, u32[]{:S(2)}, u32[]{:S(2)}) collective-permute-start(bf16[256,512]{1,0:T(8,128)(2,1)S(1)} %slice.33), channel_id=1, source_target_pairs={{0,16},{16,0},{1,17},{17,1},{2,18},{18,2},{3,19},{19,3},{4,20},{20... | collective-permute-start | bytes 786440 | tf_op jit(solution)/shard_map/ppermute | solution.py:440
  81.3 21.9 %copy-start.17 = (bf16[1,2048]{1,0:T(2,128)(2,1)S(1)}, bf16[1,2048]{1,0:T(2,128)(2,1)}, u32[]{:S(2)}) copy-start(bf16[1,2048]{1,0:T(2,128)(2,1)} %query_ref.3) | copy-start | bytes 12292
  83.5 14.5 %all-to-all-start = ((bf16[8,32,640]{2,1,0:T(8,128)(2,1)}), bf16[8,32,640]{2,1,0:T(8,128)(2,1)S(1)}, u32[]{:S(2)}, u32[]{:S(2)}) async-start(bf16[8,32,640]{2,1,0:T(8,128)(2,1)} %get-tuple-element.67), calls=%async_computation | async-start | bytes 655360 | tf_op jit(solution)/shard_map/all_to_all | solution.py:395
  99.1 11.6 %all-to-all-start.1 = ((bf16[8,32,512]{2,1,0:T(8,128)(2,1)}), bf16[8,32,512]{2,1,0:T(8,128)(2,1)S(1)}, u32[]{:S(2)}, u32[]{:S(2)}) async-start(bf16[8,32,512]{2,1,0:T(8,128)(2,1)} %bitcast.10), calls=%async_computation.1 | async-start | bytes 524288 | tf_op jit(solution)/shard_map/all_to_all | solution.py:395
  (21 other events, 45.8 us)

commit v3 on v2

--- a/solution.py
+++ b/solution.py
@@ -15,14 +15,15 @@
 SCALE = HD ** (-0.5)
 LANES = 128
 NEG = -1e30
-VMEM = 24 * 1024 * 1024
+VMEM = 14 * 1024 * 1024
+VMEM_ALL = 56 * 1024 * 1024
 
 
 def iota(shape, dim):
     return lax.broadcasted_iota(jnp.int32, shape, dim)
 
 
-def call(kernel, outs, *args, cost=None, smem=(), aliases=None):
+def call(kernel, outs, *args, cost=None, smem=(), aliases=None, scratch=()):
     return pl.pallas_call(
         kernel,
         out_shape=outs,
@@ -32,6 +33,7 @@
         ],
         out_specs=jax.tree.map(lambda _: pl.BlockSpec(memory_space=pltpu.VMEM), outs),
         input_output_aliases=aliases or {},
+        scratch_shapes=scratch,
         compiler_params=pltpu.CompilerParams(vmem_limit_bytes=VMEM),
         cost_estimate=cost,
     )(*args)
@@ -102,14 +104,29 @@
 
 
 def open_kernel(
-    sections, cape, capr, block_rows, group_ref, weight_ref, target_ref, owner_ref, query_ref,
-    out_own, out_middle, out_slot, out_block
+    sections, cape, capr, block_rows, group_ref, base_ref, half_ref, weight_hbm, target_hbm, owner_hbm, query_hbm,
+    out_own, out_middle, out_slot, out_block, target_ref, owner_ref, query_ref, sems
 ):
-    part = out_middle.shape[0] // 2
-    turned = pl.multiple_of(group_ref[0] * (weight_ref.shape[0] - part), part)
-    out_own[:part] = weight_ref[pl.ds(turned, part), :]
-    out_middle[...] = weight_ref[part : 3 * part, :]
+    depth, middle = weight_hbm.shape[0], out_middle.shape[0]
+    part = (depth - middle) // 2
+    turned = pl.multiple_of(group_ref[0] * (depth - part), 16)
+    copies = [
+        pltpu.make_async_copy(source, target, sems.at[k])
+        for k, (source, target) in enumerate(
+            (
+                (target_hbm, target_ref),
+                (query_hbm, query_ref),
+                (owner_hbm, owner_ref),
+                (weight_hbm.at[pl.ds(turned, part)], out_own.at[pl.ds(0, part)]),
+                (weight_hbm.at[pl.ds(part, middle)], out_middle),
+            )
+        )
+    ]
+    for copy in copies:
+        copy.start()
+    copies[0].wait()
     out_slot[...], positions = image_slots(target_ref[...], sections, cape)
+    copies[1].wait()
     groups = query_ref.shape[1] // (GROUP * HD)
     told = [query_group(query_ref, h) for h in range(groups)]
     told.append(jnp.zeros((GROUP, out_own.shape[1] - groups * HD), jnp.float32))
@@ -118,51 +135,73 @@
         [positions, jnp.zeros((sections, out_own.shape[1] - LANES), jnp.float32)], axis=1
     )
     out_own[part:] = jnp.concatenate([told, positions], axis=0).astype(jnp.bfloat16)
+    copies[2].wait()
     out_block[...] = block_slots(owner_ref[...], sections, capr, block_rows)
-
-
-def norm_kernel(blocks, features, half_ref, near_ref, far_ref, gain, gain_far, out_ref, done_ref):
-    half, width = blocks // 2, out_ref.shape[2]
-    near = near_ref[...].astype(jnp.float32)
-    far = far_ref[...].astype(jnp.float32)
-    total = jnp.sum(near * near, axis=1, keepdims=True) + jnp.sum(far * far, axis=1, keepdims=True)
-    factor = lax.rsqrt(total * (1.0 / features) + 1e-06)
-    for side, (ref, gains) in enumerate(((near_ref, gain), (far_ref, gain_far))):
-        for j in range(half):
-            at = pl.ds(j * width, width)
-            block = ref[:, at].astype(jnp.float32) * factor * gains[:, at]
-            out_ref[side * half + j] = block.astype(jnp.bfloat16)
+    copies[3].wait()
+    copies[4].wait()
+
+
+NORM_TILE = 64
+
+
+def norm_kernel(blocks, half_ref, near_hbm, far_hbm, gains_hbm, out_ref, done_ref, near, far, gain, sems):
+    tiles, tile, features = near.shape
+    width = out_ref.shape[2]
+    half = half_ref[0]
+    copies = []
+    for side in range(2):
+        at = pl.multiple_of((half if side == 0 else 1 - half) * features, features)
+        copies.append(
+            pltpu.make_async_copy(gains_hbm.at[:, pl.ds(at, features)], gain.at[side], sems.at[side])
+        )
+    for i in range(tiles):
+        at = pl.ds(i * tile, tile)
+        for side, (hbm, vmem) in enumerate(((near_hbm, near), (far_hbm, far))):
+            copies.append(
+                pltpu.make_async_copy(hbm.at[at], vmem.at[i], sems.at[2 + 2 * i + side])
+            )
+    for copy in copies:
+        copy.start()
     done_ref[...] = jnp.zeros_like(done_ref)
+    copies[0].wait()
+    copies[1].wait()
+    for i in range(tiles):
+        copies[2 + 2 * i].wait()
+        copies[3 + 2 * i].wait()
+        total = 0.0
+        for ref in (near, far):
+            value = ref[i].astype(jnp.float32)
+            total = total + jnp.sum(value * value, axis=1, keepdims=True)
+        factor = lax.rsqrt(total * (1.0 / (2 * features)) + 1e-06)
+        for side, ref in enumerate((near, far)):
+            for j in range(blocks // 2):
+                at = pl.ds(j * width, width)
+                block = ref[i, :, at].astype(jnp.float32) * factor * gain[side, :, at]
+                out_ref[side * (blocks // 2) + j, pl.ds(i * tile, tile)] = block.astype(jnp.bfloat16)
 
 
 def normalize(blocks, half, near, far, gains):
     rows, features = near.shape
-    width = 2 * features // blocks
-    tile = 64
-    rows_spec = pl.BlockSpec((tile, features), lambda i, h: (i, 0))
+    tile = min(NORM_TILE, rows)
+    held = pltpu.VMEM((rows // tile, tile, features), jnp.bfloat16)
     return pl.pallas_call(
-        functools.partial(norm_kernel, blocks, 2 * features),
+        functools.partial(norm_kernel, blocks),
         out_shape=(
-            jax.ShapeDtypeStruct((blocks, rows, width), jnp.bfloat16),
+            jax.ShapeDtypeStruct((blocks, rows, 2 * features // blocks), jnp.bfloat16),
             jax.ShapeDtypeStruct((8, LANES), jnp.float32),
         ),
-        grid_spec=pltpu.PrefetchScalarGridSpec(
-            num_scalar_prefetch=1,
-            grid=(rows // tile,),
-            in_specs=[
-                rows_spec,
-                rows_spec,
-                pl.BlockSpec((1, features), lambda i, h: (0, h[0])),
-                pl.BlockSpec((1, features), lambda i, h: (0, 1 - h[0])),
-            ],
-            out_specs=(
-                pl.BlockSpec((blocks, tile, width), lambda i, h: (0, i, 0)),
-                pl.BlockSpec((8, LANES), lambda i, h: (0, 0)),
-            ),
-        ),
+        in_specs=[pl.BlockSpec(memory_space=pltpu.SMEM)]
+        + [pl.BlockSpec(memory_space=pltpu.HBM)] * 3,
+        out_specs=[pl.BlockSpec(memory_space=pltpu.VMEM)] * 2,
+        scratch_shapes=[
+            held,
+            held,
+            pltpu.VMEM((2, 1, features), jnp.float32),
+            pltpu.SemaphoreType.DMA((2 + 2 * (rows // tile),)),
+        ],
         compiler_params=pltpu.CompilerParams(vmem_limit_bytes=VMEM),
-        cost_estimate=cost(0, 8 * rows * 2 * features),
-    )(half, near, far, gains, gains)
+        cost_estimate=cost(1, 1),
+    )(half, near, far, gains)
 
 
 def pool_rows(pool_ref):
@@ -206,9 +245,11 @@
     position_ref[...] = positions_in_slots(sent, iota((sections, 1), 0), cape)
 
 
-def ring_pool_kernel(sections, cape, source_ref, *refs):
+def ring_pool_kernel(sections, cape, index_ref, base_ref, *refs):
     told_refs = refs[:sections]
-    pool_ref, owner_ref, fill_ref, out_ref, position_ref = refs[sections:]
+    pool_ref, owner_ref, fill_ref = refs[sections : sections + 3]
+    out_ref, position_ref = refs[-2:]
+    sources = [index_ref[base_ref[0] + sections + j] for j in range(sections)]
     held, block_rows, _ = pool_ref.shape
     heads = out_ref.shape[1] // 2
     groups = heads // GROUP
@@ -217,7 +258,7 @@
     owner, fill = owner_ref[...], fill_ref[...]
     masks = []
     for j in range(sections):
-        owned = owner == source_ref[j]
+        owned = owner == sources[j]
         mask = [(owned & (fill > i)).astype(jnp.float32) for i in range(block_rows)]
         masks.append(jnp.broadcast_to(jnp.concatenate(mask, axis=1), (GROUP, held * block_rows)))
     mask = jnp.concatenate(masks, axis=0) > 0.0
@@ -238,8 +279,8 @@
     for j in range(sections):
         at = slice(j * GROUP, (j + 1) * GROUP)
         rows = jnp.concatenate([x[at] for x in sums] + [x[at] for x in states], axis=0)
-        out_ref[source_ref[j]] = rows.astype(jnp.bfloat16)
-    own = iota((sections, LANES), 0) == source_ref[0]
+        out_ref[sources[j]] = rows.astype(jnp.bfloat16)
+    own = iota((sections, LANES), 0) == sources[0]
     sent = jnp.concatenate(
         [
             jnp.sum(jnp.where(own, t[GROUP:, :LANES], 0.0), axis=0, keepdims=True) for t in told
@@ -248,7 +289,7 @@
     )
     source = jnp.zeros((sections, 1), jnp.int32)
     for j in range(sections):
-        source = jnp.where(iota((sections, 1), 0) == j, source_ref[j], source)
+        source = jnp.where(iota((sections, 1), 0) == j, sources[j], source)
     position_ref[...] = positions_in_slots(sent, source, cape)
 
 
@@ -274,61 +315,60 @@
     return top, total, acc
 
 
-def product(rows_ref, block, quarter_ref, weights):
-    near, middle, far = weights
-    part = middle.shape[0] // 2
-    turned = quarter_ref[0] * (2 * part + part)
-    near_at = pl.multiple_of(turned, part)
-    far_at = pl.multiple_of(3 * part - turned, part)
-
-    def times(at, weight):
-        return jnp.dot(rows_ref[block, :, at], weight, preferred_element_type=jnp.float32)
-
-    return (
-        times(pl.ds(part, 2 * part), middle)
-        + times(pl.ds(near_at, part), near)
-        + times(pl.ds(far_at, part), far)
-    )
+def fill_slice(whole_ref, group, near, middles, far):
+    part, depth = far.shape[0], whole_ref.shape[0]
+    own_at = pl.multiple_of(group * (depth - part), 16)
+    far_at = pl.multiple_of((1 - group) * (depth - part), 16)
+    whole_ref[pl.ds(own_at, part)] = near[:part]
+    whole_ref[pl.ds(far_at, part)] = far
+    at = part
+    for middle in middles:
+        whole_ref[at : at + middle.shape[0]] = middle
+        at += middle.shape[0]
+
+
+def times(rows_ref, block, weight_ref):
+    return jnp.dot(rows_ref[block], weight_ref[...], preferred_element_type=jnp.float32)
 
 
 def step_kernel(
-    step, index_ref, quarter_ref, text_ref, image_ref, near_up, middle_up, near_down, middle_down, far_ref,
-    text_in, image_in, text_out, image_out
+    step, index_ref, base_ref, group_ref, text_ref, image_ref, near_up, middle_up, near_down, middle_down, far_ref,
+    text_in, image_in, text_out, image_out, first_ref, second_ref
 ):
-    part = middle_up.shape[0] // 2
-    up = (near_up[:part], middle_up[...], far_ref[:part])
-    down = (near_down[:part], middle_down[...], far_ref[part:])
-    first, second = index_ref[2 * step - 1], index_ref[2 * step]
+    part = far_ref.shape[0] // 2
+    fill_slice(first_ref, group_ref[0], near_up[...], [middle_up[...]], far_ref[:part])
+    fill_slice(second_ref, group_ref[0], near_down[...], [middle_down[...]], far_ref[part:])
+    first, second = (index_ref[base_ref[0] + k] for k in (2 * step - 1, 2 * step))
     for ref, given, out in ((text_ref, text_in, text_out), (image_ref, image_in, image_out)):
-        out[...] = (
-            given[...]
-            + product(ref, first, quarter_ref, up)
-            + product(ref, second, quarter_ref, down)
-        )
-
-
-def first_kernel(index_ref, text_ref, image_ref, weight_ref, text_out, image_out):
-    weight = weight_ref[...]
-    block = index_ref[0]
-    text_out[...] = jnp.dot(text_ref[block], weight, preferred_element_type=jnp.float32)
-    image_out[...] = jnp.dot(image_ref[block], weight, preferred_element_type=jnp.float32)
-
-
-def last_kernel(
-    step, index_ref, quarter_ref, text_ref, image_ref, near_ref, middle_ref, far_ref, text_in, image_in, bias_ref,
-    slot_ref, partial_ref, text_out, send_out
+        out[...] = given[...] + times(ref, first, first_ref) + times(ref, second, second_ref)
+
+
+def first_kernel(index_ref, base_ref, text_ref, image_ref, weight_ref, text_out, image_out):
+    block = index_ref[base_ref[0]]
+    text_out[...] = times(text_ref, block, weight_ref)
+    image_out[...] = times(image_ref, block, weight_ref)
+
+
+def last_image_kernel(
+    step, index_ref, base_ref, group_ref, image_ref, near_ref, middle_ref, far_ref, image_in, bias_ref,
+    slot_ref, partial_ref, send_out, whole_ref
 ):
     sections, cape, _ = send_out.shape
     width = image_in.shape[1]
-    block = index_ref[step]
-    weights = (near_ref[: middle_ref.shape[0] // 2], middle_ref[...], far_ref[...])
-    image = image_in[...] + product(image_ref, block, quarter_ref, weights) + bias_ref[...]
+    fill_slice(whole_ref, group_ref[0], near_ref[...], [middle_ref[...]], far_ref[...])
+    image = times(image_ref, index_ref[base_ref[0] + step], whole_ref)
+    image = image_in[...] + image + bias_ref[...]
     place = (iota((sections * cape, image.shape[0]), 0) == slot_ref[...]).astype(jnp.bfloat16)
     send = jnp.dot(place, image.astype(jnp.bfloat16), preferred_element_type=jnp.float32)
     send_out[:, :, :width] = send.astype(jnp.bfloat16).reshape(sections, cape, width)
     send_out[:, :, width:] = partial_ref[...]
-    text = text_in[...] + product(text_ref, block, quarter_ref, weights) + bias_ref[...]
-    text_out[...] = text.astype(jnp.bfloat16)
+
+
+def last_text_kernel(
+    step, index_ref, base_ref, text_ref, whole_ref, text_in, bias_ref, text_out
+):
+    text = times(text_ref, index_ref[base_ref[0] + step], whole_ref)
+    text_out[...] = (text_in[...] + text + bias_ref[...]).astype(jnp.bfloat16)
 
 
 def finish_kernel(text_ref, image_ref, bias_ref, slot_ref, text_out, send_out):
@@ -339,20 +379,17 @@
 
 
 def place_kernel(text_ref, arrived_ref, position_ref, slot_ref, count_ref, rows_ref, blocks_ref):
-    rows = text_ref.shape[0]
+    rows, width = text_ref.shape
     sections, cape, _ = arrived_ref.shape
-    width = text_ref.shape[1]
     row = iota((rows, sections * cape), 0)
     match = (row == position_ref[...]) & (row < count_ref[0])
     filled = jnp.max(match.astype(jnp.float32), axis=1, keepdims=True) > 0.0
-    arrived = arrived_ref[:, :, :width].astype(jnp.float32).reshape(sections * cape, width)
-    placed = jnp.dot(
-        match.astype(jnp.bfloat16), arrived.astype(jnp.bfloat16), preferred_element_type=jnp.float32
-    )
+    arrived = arrived_ref[:, :, :width].reshape(sections * cape, width)
+    placed = jnp.dot(match.astype(jnp.bfloat16), arrived, preferred_element_type=jnp.float32)
     whole = jnp.where(filled, placed, text_ref[...].astype(jnp.float32)).astype(jnp.bfloat16)
-    rows_ref[...] = whole
     slots = (iota((blocks_ref.shape[0], rows), 0) == slot_ref[...]).astype(jnp.bfloat16)
     blocks_ref[...] = jnp.dot(slots, whole, preferred_element_type=jnp.float32).astype(jnp.bfloat16)
+    rows_ref[...] = whole
 
 
 def decode_kernel(packed, rows_ref, query_ref, partial_ref, length_ref, out_ref):
@@ -412,9 +449,8 @@
     return table
 
 
-def after(values, *others):
-    held = lax.optimization_barrier((tuple(values), others))
-    return held[0]
+def after(values, others):
+    return lax.optimization_barrier((tuple(values), tuple(others)))
 
 
 def ring_path(
@@ -429,6 +465,7 @@
     rows = text.shape[0]
     heads = queries.shape[1] // HD
     group = lax.axis_index("groups").astype(jnp.int32)
+    whole_slice = pltpu.VMEM((depth, width), jnp.bfloat16)
 
     def up(x):
         return lax.ppermute(x, "section", ahead)
@@ -439,87 +476,101 @@
     def across(x):
         return lax.ppermute(x, "groups", [(0, 1), (1, 0)])
 
-    table = jnp.asarray(ring_tables(sections, lax.axis_size("tensor")))
-    index = lax.dynamic_slice(
-        table, (lax.axis_index("section"), lax.axis_index("tensor"), 0), (1, 1, 2 * sections)
-    ).reshape(2 * sections)
-    quarter = group.reshape(1)
+    tensors = lax.axis_size("tensor")
+    index = jnp.asarray(ring_tables(sections, tensors).reshape(-1))
+    base = (lax.axis_index("section") * tensors + lax.axis_index("tensor")) * (2 * sections)
+    group, base = group.reshape(1), base.astype(jnp.int32).reshape(1)
     states = (jax.ShapeDtypeStruct((rows, width), jnp.float32),) * 2
     flops = 4 * rows * depth * width
 
     def step_product(step, state):
         return call(
-            functools.partial(step_kernel, step), states, index, quarter, *normed,
+            functools.partial(step_kernel, step), states, index, base, group, *normed,
             owns[step][0], middles[step][0], owns[step][1], middles[step][1], fars[step], *state,
-            smem=(0, 1), aliases={9: 0, 10: 1}, cost=cost(2 * flops, 0),
+            smem=(0, 1, 2), aliases={10: 0, 11: 1}, cost=cost(1, 1),
+            scratch=[whole_slice] * 2,
         )
 
-    own, middle, image_slot, block_slot = call(
+    spaces = [pltpu.SMEM] * 3 + [pltpu.HBM] * 4
+    own, middle, image_slot, block_slot = pl.pallas_call(
         functools.partial(open_kernel, sections, cape, capr, pool.shape[1]),
-        (
+        out_shape=(
             jax.ShapeDtypeStruct((part + GROUP + sections, width), jnp.bfloat16),
-            jax.ShapeDtypeStruct((2 * part, width), jnp.bfloat16),
+            jax.ShapeDtypeStruct((depth - 2 * part, width), jnp.bfloat16),
             jax.ShapeDtypeStruct((1, rows), jnp.int32),
             jax.ShapeDtypeStruct((1, block_owner.shape[1] * pool.shape[1]), jnp.int32),
         ),
-        quarter, weight, target, block_owner, queries,
-        smem=(0,),
-    )
+        in_specs=[pl.BlockSpec(memory_space=space) for space in spaces],
+        out_specs=[pl.BlockSpec(memory_space=pltpu.VMEM)] * 4,
+        scratch_shapes=[
+            pltpu.VMEM(target.shape, jnp.int32),
+            pltpu.VMEM(block_owner.shape, jnp.int32),
+            pltpu.VMEM(queries.shape, jnp.bfloat16),
+            pltpu.SemaphoreType.DMA((5,)),
+        ],
+        compiler_params=pltpu.CompilerParams(vmem_limit_bytes=VMEM_ALL),
+    )(group, base, half, weight, target, block_owner, queries)
     near_own = [up(own), down(own)]
-    text_far = beside(text)
+    text_far, image_far = beside(text), beside(image)
+    (middle,), (text_far, image_far) = after((middle,), (text_far, image_far))
     near_middle = [up(middle), down(middle)]
-    image_far = beside(image)
     last = sections // 2 - 1
     owns, middles, fars = {}, {}, {}
     told = [own]
-    waiting, state = [], None
+    normed_text, token = normalize(sections, half, text, text_far, gains)
+    waiting = [token]
     for step in range(1, last + 1):
-        *near_own, text_far = after((*near_own, text_far), *waiting)
-        owns[step] = tuple(near_own)
+        near_own, waiting = after(near_own, waiting)
+        owns[step] = near_own
         told += near_own
+        if step > 1:
+            fars[step - 1] = waiting[0]
+            waiting = waiting[1:]
         fars[step] = across(jnp.concatenate([x[:part] for x in near_own], 0))
         near_own = [up(near_own[0])] + ([down(near_own[1])] if step < last else [])
-        waiting = []
+        near_middle, waiting = after(near_middle, [*waiting, image_far])
+        *waiting, image_far = waiting
+        middles[step] = near_middle
+        near_middle = ([up(near_middle[0])] if step < last else []) + [down(near_middle[1])]
         if step == 1:
-            normed_text, token = normalize(sections, half, text, text_far, gains)
-            waiting = [token]
-        elif step == 2:
             normed_image, token = normalize(sections, half, image, image_far, gains)
             normed = (normed_text, normed_image)
             state = call(
-                first_kernel, states, index, *normed, weight, smem=(0,), cost=cost(flops, 0)
+                first_kernel, states, index, base, *normed, weight, smem=(0, 1), cost=cost(1, 1)
             )
-            waiting = [token]
+            waiting = [*waiting, token, *state]
         else:
-            state = step_product(step - 2, state)
-            waiting = [*state]
-        *near_middle, image_far = after((*near_middle, image_far), *waiting)
-        middles[step] = tuple(near_middle)
-        near_middle = ([up(near_middle[0])] if step < last else []) + [down(near_middle[1])]
-        waiting = [fars[step]]
-    state = step_product(last - 1, state)
-    (last_own,) = after(near_own, *waiting, *state)
+            waiting = [*waiting[:-2], *step_product(step - 1, waiting[-2:])]
+        waiting = [fars[step], *waiting]
+    (last_own,), waiting = after(near_own, waiting)
+    fars[last] = waiting[0]
     last_far = across(last_own[:part])
-    state = step_product(last, state)
+    state = step_product(last, waiting[-2:])
     partial, position = call(
         functools.partial(ring_pool_kernel, sections, cape),
         (
             jax.ShapeDtypeStruct((sections, 2 * heads, HD), jnp.bfloat16),
             jax.ShapeDtypeStruct((1, sections * cape), jnp.int32),
         ),
-        index[sections:], *told, last_own, pool, owner, fill,
-        smem=(0,),
-    )
-    text_rows, send = call(
-        functools.partial(last_kernel, sections - 1),
+        index, base, *told, last_own, pool, owner, fill, *waiting[1:-2],
+        smem=(0, 1),
+    )
+    send, whole = call(
+        functools.partial(last_image_kernel, sections - 1),
         (
-            jax.ShapeDtypeStruct((rows, width), jnp.bfloat16),
             jax.ShapeDtypeStruct((sections, cape, width + HD), jnp.bfloat16),
-        ),
-        index, quarter, *normed, last_own, near_middle[0], last_far, *state, bias, image_slot, partial,
-        smem=(0, 1), cost=cost(flops, 0),
+            jax.ShapeDtypeStruct((depth, width), jnp.bfloat16),
+        ),
+        index, base, group, normed[1], last_own, *near_middle, last_far, state[1], bias, image_slot, partial,
+        smem=(0, 1, 2), cost=cost(1, 1),
     )
     arrived = exchange(send)
+    text_rows = call(
+        functools.partial(last_text_kernel, sections - 1),
+        jax.ShapeDtypeStruct((rows, width), jnp.bfloat16),
+        index, base, normed[0], whole, state[0], bias,
+        smem=(0, 1), cost=cost(1, 1),
+    )
     return text_rows, arrived, position, block_slot, arrived
 
 
@@ -594,7 +645,7 @@
         sections == 8
         and tensors == 2
         and lax.axis_size("groups") == 2
-        and kv_weight.shape[0] % (8 * LANES) == 0
+        and kv_weight.shape[0] % 1024 == 0
         and cape == 2 * heads
     )
     text_rows, arrived, position, block_slot, partial = (ring_path if ring else gather_path)(

time: 112 us -> 104 us (0.929)
  local copies, waits for them, and re-layouts: 11.8 us -> 5.43 us
  waiting for transfers between devices: 41.8 us -> 40.3 us
    unnamed x47 -> x33, local copies, waits for them, and re-layouts: 10.2 us -> 5.3 us
    ppermute x7, starting transfers between devices: 7.42 us -> 2.87 us  [down(): return lax.ppermute(x, 'section', back)]
    ppermute x7, starting transfers between devices: 10.5 us -> 13.9 us  [up(): return lax.ppermute(x, 'section', ahead)]
    ppermute x7, waiting for transfers between devices: 11.1 us -> 7.86 us  [down(): return lax.ppermute(x, 'section', back)]
    all_to_all x2, waiting for transfers between devices: 14.2 us -> 11.2 us  [exchange(): return lax.all_to_all(x, 'section', split_axis=0, concat_axis=0, tiled=True)]
    ppermute x4, waiting for transfers between devices: 0.1 us -> 2.69 us  [across(): return lax.ppermute(x, 'groups', [(0, 1), (1, 0)])]
    ppermute x4, starting transfers between devices: 5.37 us -> 7.03 us  [across(): return lax.ppermute(x, 'groups', [(0, 1), (1, 0)])]
    ppermute x2, waiting for transfers between devices: 0.01 us -> 1.61 us  [beside(): return lax.ppermute(x, 'tensor', [(0, 1), (1, 0)])]
  transfers between devices with their start and end apart: 22 -> 22, of which waited for: 10 -> 15; matrix products, arithmetic and copies ran while one was open for 2% -> 0% of each run, Pallas kernels for 16% -> 18%
where the time goes in v3:
time: 104 us; the launch traced here: 103 us
  waiting for transfers between devices  40.3 us (39%)
  starting transfers between devices  33.3 us (32%)
  Pallas kernels  21.9 us (21%)
  local copies, waits for them, and re-layouts  5.43 us (5%)
  between operations  2.27 us (2%)
    ppermute x7, waiting for transfers between devices, up(): return lax.ppermute(x, 'section', ahead)  16.9 us
    ppermute x7, starting transfers between devices, up(): return lax.ppermute(x, 'section', ahead)  13.9 us
    pallas_call x9, Pallas kernels, call(): pl.pallas_call(kernel, out_shape=outs, in_specs=[pl.BlockSpec(memory_spac...  13.8 us
    all_to_all x2, waiting for transfers between devices, exchange(): return lax.all_to_all(x, 'section', split_axis=0, concat_axis=0, tiled=True)  11.2 us
    all_to_all x2, starting transfers between devices, exchange(): return lax.all_to_all(x, 'section', split_axis=0, concat_axis=0, tiled=True)  8.94 us
    ppermute x7, waiting for transfers between devices, down(): return lax.ppermute(x, 'section', back)  7.86 us
    ppermute x4, starting transfers between devices, across(): return lax.ppermute(x, 'groups', [(0, 1), (1, 0)])  7.03 us
    pallas_call x2, Pallas kernels, normalize(): pl.pallas_call(functools.partial(norm_kernel, blocks), out_shape=(jax.Sha...  5.81 us
  transfers between devices with their start and end apart: 22, of which 15 were waited for; matrix products, arithmetic and copies ran while one was open for 0% of the time, Pallas kernels for 18%

profile of v3, /device:TPU:0, one launch (start us, length us, event | category | flops | bytes accessed | tf_op | source)
XLA Modules:
  0.0 103.3 jit_solution(3385836767181938451)
XLA Ops:
  1.2 2.2 %shard_map.149 = (bf16[272,512]{1,0:T(8,128)(2,1)}, bf16[512,512]{1,0:T(8,128)(2,1)}, s32[1,256]{1,0:T(1,128)}, s32[1,256]{1,0:T(1,128)}) custom-call(s32[1]{0:T(128)} %bitcast.2.group_ref, s32[1]{0:T(128)} %bitcast.base_ref, s32[1]{0:T(128)} %bitcast.1.half_ref, bf16[1024,512]{1,0:T(8,128)(2,1)} %weight_ref.1, s32[1,256]{1,0:T(1,128)} %bitcast.18, ...), custom_call_target="tpu_custom_call" | custom-call | tf_op jit(solution)/shard_map/pallas_call | solution.py:495
  3.5 3.1 %collective-permute-start.4 = (bf16[272,512]{1,0:T(8,128)(2,1)}, bf16[272,512]{1,0:T(8,128)(2,1)S(1)}, u32[]{:S(2)}, u32[]{:S(2)}) collective-permute-start(bf16[272,512]{1,0:T(8,128)(2,1)} %get-tuple-element.70.refs_0_), channel_id=1, source_target_pairs={{0,4},{4,8},{8,12},{12,14},{14,10},{10,6},{6,2},{2,0},{1,5},{5,9},... | collective-permute-start | bytes 835592 | tf_op jit(solution)/shard_map/ppermute | solution.py:471
  8.1 2.9 %collective-permute-start.2 = (bf16[512,512]{1,0:T(8,128)(2,1)}, bf16[512,512]{1,0:T(8,128)(2,1)S(1)}, u32[]{:S(2)}, u32[]{:S(2)}) collective-permute-start(bf16[512,512]{1,0:T(8,128)(2,1)} %get-tuple-element.69), channel_id=1, source_target_pairs={{0,4},{4,8},{8,12},{12,14},{14,10},{10,6},{6,2},{2,0},{1,5},{5,9},... | collective-permute-start | bytes 1572872 | tf_op jit(solution)/shard_map/ppermute | solution.py:471
  11.1 1.6 %copy-done.3 = bf16[256,4096]{1,0:T(8,128)(2,1)S(1)} copy-done((bf16[256,4096]{1,0:T(8,128)(2,1)S(1)}, bf16[256,4096]{1,0:T(8,128)(2,1)}, u32[]{:S(2)}) %copy-start.3) | copy-done | bytes 2097176
  13.4 3.3 %shard_map.150 = (bf16[8,256,1024]{2,1,0:T(8,128)(2,1)S(1)}, f32[8,128]{1,0:T(8,128)S(1)}) custom-call(s32[1]{0:T(128)} %bitcast.1.half_ref, bf16[256,4096]{1,0:T(8,128)(2,1)S(1)} %copy-done.3, bf16[256,4096]{1,0:T(8,128)(2,1)} %collective-permute-done.far_hbm, f32[1,8192]{1,0:T(1,128)S(1)} %bitcast.11), custom_call_target="tpu_custom_call" | custom-call | flops 1 | bytes 1 | tf_op jit(solution)/shard_map/pallas_call | solution.py:187
  16.9 2.0 %collective-permute-start.8 = (bf16[512,512]{1,0:T(8,128)(2,1)S(1)}, bf16[512,512]{1,0:T(8,128)(2,1)S(1)}, u32[]{:S(2)}, u32[]{:S(2)}) collective-permute-start(bf16[512,512]{1,0:T(8,128)(2,1)S(1)} %pad_maximum_fusion), channel_id=1, source_target_pairs={{0,16},{16,0},{1,17},{17,1},{2,18},{18,2},{3,19},{19,3},{4,20},{20... | collective-permute-start | bytes 1572872 | tf_op jit(solution)/shard_map/ppermute | solution.py:477
  21.0 4.4 %collective-permute-done.2.middle_up = bf16[512,512]{1,0:T(8,128)(2,1)S(1)} collective-permute-done((bf16[512,512]{1,0:T(8,128)(2,1)}, bf16[512,512]{1,0:T(8,128)(2,1)S(1)}, u32[]{:S(2)}, u32[]{:S(2)}) %collective-permute-start.2) | collective-permute-done | bytes 524320 | tf_op jit(solution)/shard_map/ppermute | solution.py:471
  25.3 2.2 %collective-permute-done.3.middle_down = bf16[512,512]{1,0:T(8,128)(2,1)S(1)} collective-permute-done((bf16[512,512]{1,0:T(8,128)(2,1)}, bf16[512,512]{1,0:T(8,128)(2,1)S(1)}, u32[]{:S(2)}, u32[]{:S(2)}) %collective-permute-start.3) | collective-permute-done | bytes 524320 | tf_op jit(solution)/shard_map/ppermute | solution.py:474
  29.6 2.5 %shard_map.151 = (bf16[8,256,1024]{2,1,0:T(8,128)(2,1)S(1)}, f32[8,128]{1,0:T(8,128)S(1)}) custom-call(s32[1]{0:T(128)} %bitcast.1.half_ref, bf16[256,4096]{1,0:T(8,128)(2,1)S(1)} %copy-done.4, bf16[256,4096]{1,0:T(8,128)(2,1)S(1)} %collective-permute-done.1.far_hbm, f32[1,8192]{1,0:T(1,128)S(1)} %bitcast.12), custom_call_target="tpu_custom_call" | custom-call | flops 1 | bytes 1 | tf_op jit(solution)/shard_map/pallas_call | solution.py:187
  37.2 5.3 %collective-permute-done.12.middle_up = bf16[512,512]{1,0:T(8,128)(2,1)S(1)} collective-permute-done((bf16[512,512]{1,0:T(8,128)(2,1)S(1)}, bf16[512,512]{1,0:T(8,128)(2,1)S(1)}, u32[]{:S(2)}, u32[]{:S(2)}) %collective-permute-start.12) | collective-permute-done | bytes 524320 | tf_op jit(solution)/shard_map/ppermute | solution.py:471
  42.5 2.2 %collective-permute-done.13.middle_down = bf16[512,512]{1,0:T(8,128)(2,1)S(1)} collective-permute-done((bf16[512,512]{1,0:T(8,128)(2,1)S(1)}, bf16[512,512]{1,0:T(8,128)(2,1)S(1)}, u32[]{:S(2)}, u32[]{:S(2)}) %collective-permute-start.13) | collective-permute-done | bytes 524320 | tf_op jit(solution)/shard_map/ppermute | solution.py:474
  46.8 2.0 %shard_map.153 = (f32[256,512]{1,0:T(8,128)S(1)}, f32[256,512]{1,0:T(8,128)S(1)}) custom-call(s32[256]{0:T(256)S(1)} %copy-done.9, s32[1]{0:T(128)} %bitcast.base_ref, s32[1]{0:T(128)} %bitcast.2.group_ref, bf16[8,256,1024]{2,1,0:T(8,128)(2,1)S(1)} %get-tuple-element.68.text_ref, ...), custom_call_target="tpu_custom_call", output_to_operand_aliasing={{0}: (10, {}), {1}: (11, {})} | custom-call | flops 1 | bytes 1 | tf_op jit(solution)/shard_map/pallas_call | solution.py:27
  48.7 2.0 %collective-permute-done.10.near_down.refs_6_ = bf16[272,512]{1,0:T(8,128)(2,1)S(1)} collective-permute-done((bf16[272,512]{1,0:T(8,128)(2,1)S(1)}, bf16[272,512]{1,0:T(8,128)(2,1)S(1)}, u32[]{:S(2)}, u32[]{:S(2)}) %collective-permute-start.10) | collective-permute-done | bytes 278560 | tf_op jit(solution)/shard_map/ppermute | solution.py:474
  54.0 5.8 %collective-permute-done.16.middle_up = bf16[512,512]{1,0:T(8,128)(2,1)S(1)} collective-permute-done((bf16[512,512]{1,0:T(8,128)(2,1)S(1)}, bf16[512,512]{1,0:T(8,128)(2,1)S(1)}, u32[]{:S(2)}, u32[]{:S(2)}) %collective-permute-start.16) | collective-permute-done | bytes 524320 | tf_op jit(solution)/shard_map/ppermute | solution.py:471
  61.8 2.0 %shard_map.154 = (f32[256,512]{1,0:T(8,128)S(1)}, f32[256,512]{1,0:T(8,128)S(1)}) custom-call(s32[256]{0:T(256)S(1)} %copy-done.9, s32[1]{0:T(128)} %bitcast.base_ref, s32[1]{0:T(128)} %bitcast.2.group_ref, bf16[8,256,1024]{2,1,0:T(8,128)(2,1)S(1)} %get-tuple-element.68.text_ref, ...), custom_call_target="tpu_custom_call", output_to_operand_aliasing={{0}: (10, {}), {1}: (11, {})} | custom-call | flops 1 | bytes 1 | tf_op jit(solution)/shard_map/pallas_call | solution.py:27
  65.2 1.8 %collective-permute-start.19 = (bf16[256,512]{1,0:T(8,128)(2,1)S(1)}, bf16[256,512]{1,0:T(8,128)(2,1)S(1)}, u32[]{:S(2)}, u32[]{:S(2)}) collective-permute-start(bf16[256,512]{1,0:T(8,128)(2,1)S(1)} %slice.27), channel_id=1, source_target_pairs={{0,16},{16,0},{1,17},{17,1},{2,18},{18,2},{3,19},{19,3},{4,20},{20... | collective-permute-start | bytes 786440 | tf_op jit(solution)/shard_map/ppermute | solution.py:477
  67.1 2.0 %shard_map.155 = (f32[256,512]{1,0:T(8,128)S(1)}, f32[256,512]{1,0:T(8,128)S(1)}) custom-call(s32[256]{0:T(256)S(1)} %copy-done.9, s32[1]{0:T(128)} %bitcast.base_ref, s32[1]{0:T(128)} %bitcast.2.group_ref, bf16[8,256,1024]{2,1,0:T(8,128)(2,1)S(1)} %get-tuple-element.68.text_ref, ...), custom_call_target="tpu_custom_call", output_to_operand_aliasing={{0}: (10, {}), {1}: (11, {})} | custom-call | flops 1 | bytes 1 | tf_op jit(solution)/shard_map/pallas_call | solution.py:27
  70.4 2.7 %collective-permute-done.19.far_ref = bf16[256,512]{1,0:T(8,128)(2,1)S(1)} collective-permute-done((bf16[256,512]{1,0:T(8,128)(2,1)S(1)}, bf16[256,512]{1,0:T(8,128)(2,1)S(1)}, u32[]{:S(2)}, u32[]{:S(2)}) %collective-permute-start.19) | collective-permute-done | bytes 262176 | tf_op jit(solution)/shard_map/ppermute | solution.py:477
  73.5 2.0 %shard_map.157 = (bf16[8,32,640]{2,1,0:T(8,128)(2,1)}, bf16[1024,512]{1,0:T(8,128)(2,1)S(1)}) custom-call(s32[256]{0:T(256)S(1)} %copy-done.9, s32[1]{0:T(128)} %bitcast.base_ref, s32[1]{0:T(128)} %bitcast.2.group_ref, bf16[8,256,1024]{2,1,0:T(8,128)(2,1)S(1)} %get-tuple-element.75.image_ref, bf16[272,512]{1,0:T(8,128)(2,1)S(1)} %collective-permute-done.14.refs_7_.near_ref, ...), custom_call_target="tpu_custom_call" | custom-call | flops 1 | bytes 1 | tf_op jit(solution)/shard_map/pallas_call | solution.py:27
  75.5 5.3 %all-to-all-start = ((bf16[8,32,640]{2,1,0:T(8,128)(2,1)}), bf16[8,32,640]{2,1,0:T(8,128)(2,1)S(1)}, u32[]{:S(2)}, u32[]{:S(2)}) async-start(bf16[8,32,640]{2,1,0:T(8,128)(2,1)} %get-tuple-element.125), calls=%async_computation | async-start | bytes 655360 | tf_op jit(solution)/shard_map/all_to_all | solution.py:432
  81.5 2.2 %copy-done.1 = bf16[8,256,1024]{2,1,0:T(8,128)(2,1)S(1)} copy-done((bf16[8,256,1024]{2,1,0:T(8,128)(2,1)S(1)}, bf16[8,256,1024]{2,1,0:T(8,128)(2,1)}, u32[]{:S(2)}) %copy-start.1) | copy-done | bytes 4194328
  84.6 4.9 %all-to-all-done.arrived_ref.partial_ref = bf16[8,32,640]{2,1,0:T(8,128)(2,1)S(1)} async-done(((bf16[8,32,640]{2,1,0:T(8,128)(2,1)}), bf16[8,32,640]{2,1,0:T(8,128)(2,1)S(1)}, u32[]{:S(2)}, u32[]{:S(2)}) %all-to-all-start) | async-done | bytes 327712 | tf_op jit(solution)/shard_map/all_to_all | solution.py:432
  90.7 3.6 %all-to-all-start.1 = ((bf16[8,32,512]{2,1,0:T(8,128)(2,1)}), bf16[8,32,512]{2,1,0:T(8,128)(2,1)S(1)}, u32[]{:S(2)}, u32[]{:S(2)}) async-start(bf16[8,32,512]{2,1,0:T(8,128)(2,1)} %bitcast.9), calls=%async_computation.1 | async-start | bytes 524288 | tf_op jit(solution)/shard_map/all_to_all | solution.py:432
  96.3 6.3 %all-to-all-done.1 = bf16[8,32,512]{2,1,0:T(8,128)(2,1)S(1)} async-done(((bf16[8,32,512]{2,1,0:T(8,128)(2,1)}), bf16[8,32,512]{2,1,0:T(8,128)(2,1)S(1)}, u32[]{:S(2)}, u32[]{:S(2)}) %all-to-all-start.1) | async-done | bytes 262176 | tf_op jit(solution)/shard_map/all_to_all | solution.py:432
  (75 shorter events, 26.8 us)
Async XLA Ops:
  0.6 6.8 %collective-permute-start = (bf16[256,4096]{1,0:T(8,128)(2,1)}, bf16[256,4096]{1,0:T(8,128)(2,1)}, u32[]{:S(2)}, u32[]{:S(2)}) collective-permute-start(bf16[256,4096]{1,0:T(8,128)(2,1)} %near_hbm.2), channel_id=1, source_target_pairs={{0,1},{1,0},{2,3},{3,2},{4,5},{5,4},{6,7},{7,6},{8,9},{9,8},{10,11... | collective-permute-start | bytes 6291464 | tf_op jit(solution)/shard_map/ppermute | solution.py:428
  1.1 7.0 %collective-permute-start.1 = (bf16[256,4096]{1,0:T(8,128)(2,1)}, bf16[256,4096]{1,0:T(8,128)(2,1)S(1)}, u32[]{:S(2)}, u32[]{:S(2)}) collective-permute-start(bf16[256,4096]{1,0:T(8,128)(2,1)} %near_hbm.3), channel_id=1, source_target_pairs={{0,1},{1,0},{2,3},{3,2},{4,5},{5,4},{6,7},{7,6},{8,9},{9,8},{10,11... | collective-permute-start | bytes 6291464 | tf_op jit(solution)/shard_map/ppermute | solution.py:428
  3.5 13.3 %collective-permute-start.4 = (bf16[272,512]{1,0:T(8,128)(2,1)}, bf16[272,512]{1,0:T(8,128)(2,1)S(1)}, u32[]{:S(2)}, u32[]{:S(2)}) collective-permute-start(bf16[272,512]{1,0:T(8,128)(2,1)} %get-tuple-element.70.refs_0_), channel_id=1, source_target_pairs={{0,4},{4,8},{8,12},{12,14},{14,10},{10,6},{6,2},{2,0},{1,5},{5,9},... | collective-permute-start | bytes 835592 | tf_op jit(solution)/shard_map/ppermute | solution.py:471
  6.5 10.2 %collective-permute-start.5 = (bf16[272,512]{1,0:T(8,128)(2,1)}, bf16[272,512]{1,0:T(8,128)(2,1)S(1)}, u32[]{:S(2)}, u32[]{:S(2)}) collective-permute-start(bf16[272,512]{1,0:T(8,128)(2,1)} %get-tuple-element.70.refs_0_), channel_id=1, source_target_pairs={{4,0},{8,4},{12,8},{14,12},{10,14},{6,10},{2,6},{0,2},{5,1},{9,5},... | collective-permute-start | bytes 835592 | tf_op jit(solution)/shard_map/ppermute | solution.py:474
  8.1 17.2 %collective-permute-start.2 = (bf16[512,512]{1,0:T(8,128)(2,1)}, bf16[512,512]{1,0:T(8,128)(2,1)S(1)}, u32[]{:S(2)}, u32[]{:S(2)}) collective-permute-start(bf16[512,512]{1,0:T(8,128)(2,1)} %get-tuple-element.69), channel_id=1, source_target_pairs={{0,4},{4,8},{8,12},{12,14},{14,10},{10,6},{6,2},{2,0},{1,5},{5,9},... | collective-permute-start | bytes 1572872 | tf_op jit(solution)/shard_map/ppermute | solution.py:471
  11.1 16.4 %collective-permute-start.3 = (bf16[512,512]{1,0:T(8,128)(2,1)}, bf16[512,512]{1,0:T(8,128)(2,1)S(1)}, u32[]{:S(2)}, u32[]{:S(2)}) collective-permute-start(bf16[512,512]{1,0:T(8,128)(2,1)} %get-tuple-element.69), channel_id=1, source_target_pairs={{4,0},{8,4},{12,8},{14,12},{10,14},{6,10},{2,6},{0,2},{5,1},{9,5},... | collective-permute-start | bytes 1572872 | tf_op jit(solution)/shard_map/ppermute | solution.py:474
  13.4 16.1 %copy-start.8 = (f32[8192]{0:T(1024)S(1)}, f32[8192]{0:T(1024)}, u32[]{:S(2)}) copy-start(f32[8192]{0:T(1024)} %param.21) | copy-start | bytes 98308
  16.7 50.3 %copy-start = (bf16[8,256,1024]{2,1,0:T(8,128)(2,1)}, bf16[8,256,1024]{2,1,0:T(8,128)(2,1)S(1)}, u32[]{:S(2)}) copy-start(bf16[8,256,1024]{2,1,0:T(8,128)(2,1)S(1)} %get-tuple-element.68.text_ref) | copy-start | bytes 12582916
  16.9 16.6 %collective-permute-start.8 = (bf16[512,512]{1,0:T(8,128)(2,1)S(1)}, bf16[512,512]{1,0:T(8,128)(2,1)S(1)}, u32[]{:S(2)}, u32[]{:S(2)}) collective-permute-start(bf16[512,512]{1,0:T(8,128)(2,1)S(1)} %pad_maximum_fusion), channel_id=1, source_target_pairs={{0,16},{16,0},{1,17},{17,1},{2,18},{18,2},{3,19},{19,3},{4,20},{20... | collective-permute-start | bytes 1572872 | tf_op jit(solution)/shard_map/ppermute | solution.py:477
  18.9 14.4 %collective-permute-start.6 = (bf16[272,512]{1,0:T(8,128)(2,1)S(1)}, bf16[272,512]{1,0:T(8,128)(2,1)S(1)}, u32[]{:S(2)}, u32[]{:S(2)}) collective-permute-start(bf16[272,512]{1,0:T(8,128)(2,1)S(1)} %collective-permute-done.4.near_up.refs_1_), channel_id=1, source_target_pairs={{0,4},{4,8},{8,12},{12,14},{14,10},{10,6},{6,2},{2,0},{1,5},{5,9},... | collective-permute-start | bytes 835592 | tf_op jit(solution)/shard_map/ppermute | solution.py:471
  20.5 13.0 %collective-permute-start.7 = (bf16[272,512]{1,0:T(8,128)(2,1)S(1)}, bf16[272,512]{1,0:T(8,128)(2,1)S(1)}, u32[]{:S(2)}, u32[]{:S(2)}) collective-permute-start(bf16[272,512]{1,0:T(8,128)(2,1)S(1)} %collective-permute-done.5.near_down.refs_2_), channel_id=1, source_target_pairs={{4,0},{8,4},{12,8},{14,12},{10,14},{6,10},{2,6},{0,2},{5,1},{9,5},... | collective-permute-start | bytes 835592 | tf_op jit(solution)/shard_map/ppermute | solution.py:474
  27.5 15.0 %collective-permute-start.12 = (bf16[512,512]{1,0:T(8,128)(2,1)S(1)}, bf16[512,512]{1,0:T(8,128)(2,1)S(1)}, u32[]{:S(2)}, u32[]{:S(2)}) collective-permute-start(bf16[512,512]{1,0:T(8,128)(2,1)S(1)} %collective-permute-done.2.middle_up), channel_id=1, source_target_pairs={{0,4},{4,8},{8,12},{12,14},{14,10},{10,6},{6,2},{2,0},{1,5},{5,9},... | collective-permute-start | bytes 1572872 | tf_op jit(solution)/shard_map/ppermute | solution.py:471
  29.1 15.6 %collective-permute-start.13 = (bf16[512,512]{1,0:T(8,128)(2,1)S(1)}, bf16[512,512]{1,0:T(8,128)(2,1)S(1)}, u32[]{:S(2)}, u32[]{:S(2)}) collective-permute-start(bf16[512,512]{1,0:T(8,128)(2,1)S(1)} %collective-permute-done.3.middle_down), channel_id=1, source_target_pairs={{4,0},{8,4},{12,8},{14,12},{10,14},{6,10},{2,6},{0,2},{5,1},{9,5},... | collective-permute-start | bytes 1572872 | tf_op jit(solution)/shard_map/ppermute | solution.py:474
  33.6 17.1 %collective-permute-start.11 = (bf16[512,512]{1,0:T(8,128)(2,1)S(1)}, bf16[512,512]{1,0:T(8,128)(2,1)S(1)}, u32[]{:S(2)}, u32[]{:S(2)}) collective-permute-start(bf16[512,512]{1,0:T(8,128)(2,1)S(1)} %pad_maximum_fusion.1), channel_id=1, source_target_pairs={{0,16},{16,0},{1,17},{17,1},{2,18},{18,2},{3,19},{19,3},{4,20},{20... | collective-permute-start | bytes 1572872 | tf_op jit(solution)/shard_map/ppermute | solution.py:477
  35.2 15.5 %collective-permute-start.10 = (bf16[272,512]{1,0:T(8,128)(2,1)S(1)}, bf16[272,512]{1,0:T(8,128)(2,1)S(1)}, u32[]{:S(2)}, u32[]{:S(2)}) collective-permute-start(bf16[272,512]{1,0:T(8,128)(2,1)S(1)} %collective-permute-done.7.near_down.refs_4_), channel_id=1, source_target_pairs={{4,0},{8,4},{12,8},{14,12},{10,14},{6,10},{2,6},{0,2},{5,1},{9,5},... | collective-permute-start | bytes 835592 | tf_op jit(solution)/shard_map/ppermute | solution.py:474
  35.6 15.1 %collective-permute-start.9 = (bf16[272,512]{1,0:T(8,128)(2,1)S(1)}, bf16[272,512]{1,0:T(8,128)(2,1)S(1)}, u32[]{:S(2)}, u32[]{:S(2)}) collective-permute-start(bf16[272,512]{1,0:T(8,128)(2,1)S(1)} %collective-permute-done.6.near_up.refs_3_), channel_id=1, source_target_pairs={{0,4},{4,8},{8,12},{12,14},{14,10},{10,6},{6,2},{2,0},{1,5},{5,9},... | collective-permute-start | bytes 835592 | tf_op jit(solution)/shard_map/ppermute | solution.py:471
  44.7 15.0 %collective-permute-start.16 = (bf16[512,512]{1,0:T(8,128)(2,1)S(1)}, bf16[512,512]{1,0:T(8,128)(2,1)S(1)}, u32[]{:S(2)}, u32[]{:S(2)}) collective-permute-start(bf16[512,512]{1,0:T(8,128)(2,1)S(1)} %collective-permute-done.12.middle_up), channel_id=1, source_target_pairs={{0,4},{4,8},{8,12},{12,14},{14,10},{10,6},{6,2},{2,0},{1,5},{5,9},... | collective-permute-start | bytes 1572872 | tf_op jit(solution)/shard_map/ppermute | solution.py:471
  46.3 14.4 %collective-permute-start.17 = (bf16[512,512]{1,0:T(8,128)(2,1)S(1)}, bf16[512,512]{1,0:T(8,128)(2,1)S(1)}, u32[]{:S(2)}, u32[]{:S(2)}) collective-permute-start(bf16[512,512]{1,0:T(8,128)(2,1)S(1)} %collective-permute-done.13.middle_down), channel_id=1, source_target_pairs={{4,0},{8,4},{12,8},{14,12},{10,14},{6,10},{2,6},{0,2},{5,1},{9,5},... | collective-permute-start | bytes 1572872 | tf_op jit(solution)/shard_map/ppermute | solution.py:474
  50.8 14.4 %collective-permute-start.15 = (bf16[512,512]{1,0:T(8,128)(2,1)S(1)}, bf16[512,512]{1,0:T(8,128)(2,1)S(1)}, u32[]{:S(2)}, u32[]{:S(2)}) collective-permute-start(bf16[512,512]{1,0:T(8,128)(2,1)S(1)} %pad_maximum_fusion.2), channel_id=1, source_target_pairs={{0,16},{16,0},{1,17},{17,1},{2,18},{18,2},{3,19},{19,3},{4,20},{20... | collective-permute-start | bytes 1572872 | tf_op jit(solution)/shard_map/ppermute | solution.py:477
  52.4 12.8 %collective-permute-start.14 = (bf16[272,512]{1,0:T(8,128)(2,1)S(1)}, bf16[272,512]{1,0:T(8,128)(2,1)S(1)}, u32[]{:S(2)}, u32[]{:S(2)}) collective-permute-start(bf16[272,512]{1,0:T(8,128)(2,1)S(1)} %collective-permute-done.9.near_up.refs_5_), channel_id=1, source_target_pairs={{0,4},{4,8},{8,12},{12,14},{14,10},{10,6},{6,2},{2,0},{1,5},{5,9},... | collective-permute-start | bytes 835592 | tf_op jit(solution)/shard_map/ppermute | solution.py:471
  60.8 12.8 %collective-permute-start.18 = (bf16[512,512]{1,0:T(8,128)(2,1)S(1)}, bf16[512,512]{1,0:T(8,128)(2,1)S(1)}, u32[]{:S(2)}, u32[]{:S(2)}) collective-permute-start(bf16[512,512]{1,0:T(8,128)(2,1)S(1)} %collective-permute-done.17.middle_down), channel_id=1, source_target_pairs={{4,0},{8,4},{12,8},{14,12},{10,14},{6,10},{2,6},{0,2},{5,1},{9,5},... | collective-permute-start | bytes 1572872 | tf_op jit(solution)/shard_map/ppermute | solution.py:474
  65.2 7.8 %collective-permute-start.19 = (bf16[256,512]{1,0:T(8,128)(2,1)S(1)}, bf16[256,512]{1,0:T(8,128)(2,1)S(1)}, u32[]{:S(2)}, u32[]{:S(2)}) collective-permute-start(bf16[256,512]{1,0:T(8,128)(2,1)S(1)} %slice.27), channel_id=1, source_target_pairs={{0,16},{16,0},{1,17},{17,1},{2,18},{18,2},{3,19},{19,3},{4,20},{20... | collective-permute-start | bytes 786440 | tf_op jit(solution)/shard_map/ppermute | solution.py:477
  75.5 14.1 %all-to-all-start = ((bf16[8,32,640]{2,1,0:T(8,128)(2,1)}), bf16[8,32,640]{2,1,0:T(8,128)(2,1)S(1)}, u32[]{:S(2)}, u32[]{:S(2)}) async-start(bf16[8,32,640]{2,1,0:T(8,128)(2,1)} %get-tuple-element.125), calls=%async_computation | async-start | bytes 655360 | tf_op jit(solution)/shard_map/all_to_all | solution.py:432
  90.7 11.8 %all-to-all-start.1 = ((bf16[8,32,512]{2,1,0:T(8,128)(2,1)}), bf16[8,32,512]{2,1,0:T(8,128)(2,1)S(1)}, u32[]{:S(2)}, u32[]{:S(2)}) async-start(bf16[8,32,512]{2,1,0:T(8,128)(2,1)} %bitcast.9), calls=%async_computation.1 | async-start | bytes 524288 | tf_op jit(solution)/shard_map/all_to_all | solution.py:432
  (14 other events, 89.5 us)

commit v4 on v3

--- a/solution.py
+++ b/solution.py
@@ -15,6 +15,7 @@
 SCALE = HD ** (-0.5)
 LANES = 128
 NEG = -1e30
+LEAST_IMAGE = 4
 VMEM = 14 * 1024 * 1024
 VMEM_ALL = 56 * 1024 * 1024
 
@@ -105,22 +106,35 @@
 
 def open_kernel(
     sections, cape, capr, block_rows, group_ref, base_ref, half_ref, weight_hbm, target_hbm, owner_hbm, query_hbm,
-    out_own, out_middle, out_slot, out_block, target_ref, owner_ref, query_ref, sems
+    image_hbm, text_hbm, out_a, out_b, out_slot, out_block, out_pick, target_ref, owner_ref, query_ref, sems
 ):
-    depth, middle = weight_hbm.shape[0], out_middle.shape[0]
-    part = (depth - middle) // 2
-    turned = pl.multiple_of(group_ref[0] * (depth - part), 16)
+    piece_b = out_b.shape[0]
+    piece = out_a.shape[0] - GROUP - sections
+    at = pl.multiple_of(group_ref[0] * (piece + piece_b), LANES)
+    moves = [
+        (target_hbm, target_ref),
+        (query_hbm, query_ref),
+        (owner_hbm, owner_ref),
+        (weight_hbm.at[pl.ds(at, piece)], out_a.at[pl.ds(0, piece)]),
+        (weight_hbm.at[pl.ds(at + piece, piece_b)], out_b),
+    ]
+    width = piece + piece_b
+    row = 0
+    for kind, source in enumerate((image_hbm, text_hbm)):
+        rows = source.shape[0] if kind == 0 else out_pick.shape[0] - row
+        first = source.shape[0] - rows
+        for j in range(out_pick.shape[1] // width):
+            lane = pl.multiple_of((2 * j + 1 - group_ref[0]) * width, LANES)
+            moves.append(
+                (
+                    source.at[pl.ds(first, rows), pl.ds(lane, width)],
+                    out_pick.at[pl.ds(row, rows), pl.ds(j * width, width)],
+                )
+            )
+        row += rows
     copies = [
         pltpu.make_async_copy(source, target, sems.at[k])
-        for k, (source, target) in enumerate(
-            (
-                (target_hbm, target_ref),
-                (query_hbm, query_ref),
-                (owner_hbm, owner_ref),
-                (weight_hbm.at[pl.ds(turned, part)], out_own.at[pl.ds(0, part)]),
-                (weight_hbm.at[pl.ds(part, middle)], out_middle),
-            )
-        )
+        for k, (source, target) in enumerate(moves)
     ]
     for copy in copies:
         copy.start()
@@ -129,16 +143,140 @@
     copies[1].wait()
     groups = query_ref.shape[1] // (GROUP * HD)
     told = [query_group(query_ref, h) for h in range(groups)]
-    told.append(jnp.zeros((GROUP, out_own.shape[1] - groups * HD), jnp.float32))
+    told.append(jnp.zeros((GROUP, out_a.shape[1] - groups * HD), jnp.float32))
     told = jnp.concatenate(told, axis=1)
     positions = jnp.concatenate(
-        [positions, jnp.zeros((sections, out_own.shape[1] - LANES), jnp.float32)], axis=1
-    )
-    out_own[part:] = jnp.concatenate([told, positions], axis=0).astype(jnp.bfloat16)
+        [positions, jnp.zeros((sections, out_a.shape[1] - LANES), jnp.float32)], axis=1
+    )
+    out_a[piece:] = jnp.concatenate([told, positions], axis=0).astype(jnp.bfloat16)
     copies[2].wait()
     out_block[...] = block_slots(owner_ref[...], sections, capr, block_rows)
-    copies[3].wait()
-    copies[4].wait()
+    for copy in copies[3:]:
+        copy.wait()
+
+
+FACTOR_ROWS = 16
+
+
+def factor_kernel(image_ref, text_ref, out_ref):
+    terms = [term for ref in (image_ref, text_ref) for term in bf16_terms(ref[...], 3)]
+    terms.append(jnp.zeros((out_ref.shape[0] - len(terms), out_ref.shape[1]), jnp.float32))
+    out_ref[...] = jnp.concatenate(terms, axis=0).astype(jnp.bfloat16)
+
+
+def diagonal(size):
+    return iota((size, size), 0) == iota((size, size), 1)
+
+
+def own_norm_kernel(
+    slices, group_ref, half_ref, near_hbm, far_hbm, gains_hbm, out_ref, factor_ref, near, far, gain, sems
+):
+    tiles, tile, features = near.shape
+    width = out_ref.shape[2]
+    first = near_hbm.shape[0] - tiles * tile
+    half, group = half_ref[0], group_ref[0]
+    copies = []
+    for side in range(2):
+        at = pl.multiple_of((half if side == 0 else 1 - half) * features, features)
+        copies.append(
+            pltpu.make_async_copy(gains_hbm.at[:, pl.ds(at, features)], gain.at[side], sems.at[side])
+        )
+    for i in range(tiles):
+        at = pl.ds(first + i * tile, tile)
+        for side, (hbm, vmem) in enumerate(((near_hbm, near), (far_hbm, far))):
+            copies.append(
+                pltpu.make_async_copy(hbm.at[at], vmem.at[i], sems.at[2 + 2 * i + side])
+            )
+    for copy in copies:
+        copy.start()
+    copies[0].wait()
+    copies[1].wait()
+    factors = []
+    for i in range(tiles):
+        copies[2 + 2 * i].wait()
+        copies[3 + 2 * i].wait()
+        total = 0.0
+        for ref in (near, far):
+            value = ref[i].astype(jnp.float32)
+            total = total + jnp.sum(value * value, axis=1, keepdims=True)
+        factor = lax.rsqrt(total * (1.0 / (2 * features)) + 1e-06)
+        factors.append(jnp.sum(jnp.where(diagonal(tile), factor, 0.0), axis=0, keepdims=True))
+        for side, ref in enumerate((near, far)):
+            for j in range(slices // 2):
+                at = pl.ds(pl.multiple_of((2 * j + group) * width, LANES), width)
+                block = ref[i, :, at].astype(jnp.float32) * factor * gain[side, :, at]
+                out_ref[side * (slices // 2) + j, pl.ds(i * tile, tile)] = block.astype(jnp.bfloat16)
+    missing = factor_ref.shape[1] - tiles * tile
+    if missing:
+        factors.append(jnp.zeros((1, missing), jnp.float32))
+    factor_ref[...] = jnp.concatenate(factors, axis=1)
+
+
+def own_norm(slices, group, half, near, far, gains, rows):
+    features = near.shape[1]
+    tile = NORM_TILE
+    held = pltpu.VMEM((rows // tile, tile, features), jnp.bfloat16)
+    return pl.pallas_call(
+        functools.partial(own_norm_kernel, slices),
+        out_shape=(
+            jax.ShapeDtypeStruct((slices, rows, features // slices), jnp.bfloat16),
+            jax.ShapeDtypeStruct((1, near.shape[0]), jnp.float32),
+        ),
+        in_specs=[pl.BlockSpec(memory_space=pltpu.SMEM)] * 2
+        + [pl.BlockSpec(memory_space=pltpu.HBM)] * 3,
+        out_specs=[pl.BlockSpec(memory_space=pltpu.VMEM)] * 2,
+        scratch_shapes=[
+            held,
+            held,
+            pltpu.VMEM((2, 1, features), jnp.float32),
+            pltpu.SemaphoreType.DMA((2 + 2 * (rows // tile),)),
+        ],
+        compiler_params=pltpu.CompilerParams(vmem_limit_bytes=VMEM),
+        cost_estimate=cost(1, 1),
+    )(group, half, near, far, gains)
+
+
+def other_kernel(
+    first_term, first, group_ref, half_ref, index_ref, base_ref, near_hbm, far_hbm, factor_ref, gains_ref, *refs
+):
+    *weights, out_ref, held, sems = refs
+    slices, rows, width = held.shape
+    half = slices // 2
+    copies = [
+        pltpu.make_async_copy(
+            hbm.at[pl.ds(first, rows), pl.ds(j * width, width)],
+            held.at[side * half + j],
+            sems.at[side * half + j],
+        )
+        for side, hbm in enumerate((near_hbm, far_hbm))
+        for j in range(half)
+    ]
+    for copy in copies:
+        copy.start()
+    terms = factor_ref[...].astype(jnp.float32)
+    factor = terms[first_term : first_term + 1]
+    for k in range(1, 3):
+        factor = factor + terms[first_term + k : first_term + k + 1]
+    factor = jnp.sum(jnp.where(diagonal(rows), factor[:, :rows], 0.0), axis=1, keepdims=True)
+    for copy in copies:
+        copy.wait()
+    total = 0.0
+    for k in range(slices):
+        block = index_ref[base_ref[0] + k]
+        far = (block >= half).astype(jnp.int32)
+        side = half_ref[0] + far - 2 * far * half_ref[0]
+        lane = (2 * (side * half + block - far * half) + group_ref[0]) * width
+        value = held[block].astype(jnp.float32) * factor
+        value = value * gains_ref[:, pl.ds(pl.multiple_of(lane, LANES), width)]
+        value = value.astype(jnp.bfloat16)
+        at = 0
+        for weight in weights[2 * k : 2 * k + 2]:
+            depth = weight.shape[0] // LANES * LANES
+            total = total + jnp.dot(
+                value[:, at : at + depth], weight[:depth], preferred_element_type=jnp.float32
+            )
+            at += depth
+    out_ref[...] = total.astype(jnp.bfloat16)
 
 
 NORM_TILE = 64
@@ -247,8 +385,8 @@
 
 def ring_pool_kernel(sections, cape, index_ref, base_ref, *refs):
     told_refs = refs[:sections]
-    pool_ref, owner_ref, fill_ref = refs[sections : sections + 3]
-    out_ref, position_ref = refs[-2:]
+    pool_ref, owner_ref, fill_ref, slot_ref, out_ref, position_ref, place_ref = refs[sections:]
+    place_ref[...] = (iota(place_ref.shape, 0) == slot_ref[...]).astype(jnp.bfloat16)
     sources = [index_ref[base_ref[0] + sections + j] for j in range(sections)]
     held, block_rows, _ = pool_ref.shape
     heads = out_ref.shape[1] // 2
@@ -315,60 +453,34 @@
     return top, total, acc
 
 
-def fill_slice(whole_ref, group, near, middles, far):
-    part, depth = far.shape[0], whole_ref.shape[0]
-    own_at = pl.multiple_of(group * (depth - part), 16)
-    far_at = pl.multiple_of((1 - group) * (depth - part), 16)
-    whole_ref[pl.ds(own_at, part)] = near[:part]
-    whole_ref[pl.ds(far_at, part)] = far
-    at = part
-    for middle in middles:
-        whole_ref[at : at + middle.shape[0]] = middle
-        at += middle.shape[0]
-
-
-def times(rows_ref, block, weight_ref):
-    return jnp.dot(rows_ref[block], weight_ref[...], preferred_element_type=jnp.float32)
-
-
-def step_kernel(
-    step, index_ref, base_ref, group_ref, text_ref, image_ref, near_up, middle_up, near_down, middle_down, far_ref,
-    text_in, image_in, text_out, image_out, first_ref, second_ref
-):
-    part = far_ref.shape[0] // 2
-    fill_slice(first_ref, group_ref[0], near_up[...], [middle_up[...]], far_ref[:part])
-    fill_slice(second_ref, group_ref[0], near_down[...], [middle_down[...]], far_ref[part:])
-    first, second = (index_ref[base_ref[0] + k] for k in (2 * step - 1, 2 * step))
-    for ref, given, out in ((text_ref, text_in, text_out), (image_ref, image_in, image_out)):
-        out[...] = given[...] + times(ref, first, first_ref) + times(ref, second, second_ref)
-
-
-def first_kernel(index_ref, base_ref, text_ref, image_ref, weight_ref, text_out, image_out):
-    block = index_ref[base_ref[0]]
-    text_out[...] = times(text_ref, block, weight_ref)
-    image_out[...] = times(image_ref, block, weight_ref)
-
-
-def last_image_kernel(
-    step, index_ref, base_ref, group_ref, image_ref, near_ref, middle_ref, far_ref, image_in, bias_ref,
-    slot_ref, partial_ref, send_out, whole_ref
-):
+def dots_kernel(first, count, biased, index_ref, base_ref, *refs):
+    bias = 0.0
+    if biased:
+        bias, refs = refs[0][...], refs[1:]
+    weights, refs = refs[: 2 * count], refs[2 * count :]
+    kinds = len(refs) // 3 if len(refs) % 3 == 0 else len(refs) // 2
+    rows_refs, given, outs = refs[:kinds], refs[kinds:-kinds], refs[-kinds:]
+    pieces = (rows_refs[0].shape[2] - weights[1].shape[0], weights[1].shape[0])
+    for kind, (rows_ref, out) in enumerate(zip(rows_refs, outs)):
+        total = given[kind][...] + bias if given else 0.0
+        for k in range(count):
+            block = index_ref[base_ref[0] + first + k]
+            for p, at in enumerate((slice(0, pieces[0]), slice(pieces[0], sum(pieces)))):
+                total = total + jnp.dot(
+                    rows_ref[block, :, at],
+                    weights[2 * k + p][: pieces[p]],
+                    preferred_element_type=jnp.float32,
+                )
+        out[...] = total.astype(out.dtype)
+
+
+def last_image_kernel(image_ref, other_ref, place_ref, partial_ref, send_out):
     sections, cape, _ = send_out.shape
-    width = image_in.shape[1]
-    fill_slice(whole_ref, group_ref[0], near_ref[...], [middle_ref[...]], far_ref[...])
-    image = times(image_ref, index_ref[base_ref[0] + step], whole_ref)
-    image = image_in[...] + image + bias_ref[...]
-    place = (iota((sections * cape, image.shape[0]), 0) == slot_ref[...]).astype(jnp.bfloat16)
-    send = jnp.dot(place, image.astype(jnp.bfloat16), preferred_element_type=jnp.float32)
+    width = image_ref.shape[1]
+    image = image_ref[...] + other_ref[...].astype(jnp.float32)
+    send = jnp.dot(place_ref[...], image.astype(jnp.bfloat16), preferred_element_type=jnp.float32)
     send_out[:, :, :width] = send.astype(jnp.bfloat16).reshape(sections, cape, width)
     send_out[:, :, width:] = partial_ref[...]
-
-
-def last_text_kernel(
-    step, index_ref, base_ref, text_ref, whole_ref, text_in, bias_ref, text_out
-):
-    text = times(text_ref, index_ref[base_ref[0] + step], whole_ref)
-    text_out[...] = (text_in[...] + text + bias_ref[...]).astype(jnp.bfloat16)
 
 
 def finish_kernel(text_ref, image_ref, bias_ref, slot_ref, text_out, send_out):
@@ -378,15 +490,23 @@
     send_out[...] = jnp.dot(place, image, preferred_element_type=jnp.float32).astype(jnp.bfloat16)
 
 
-def place_kernel(text_ref, arrived_ref, position_ref, slot_ref, count_ref, rows_ref, blocks_ref):
-    rows, width = text_ref.shape
+def place_kernel(
+    split, text_ref, *refs
+):
+    arrived_ref, position_ref, slot_ref, count_ref, rows_ref, blocks_ref = refs[-6:]
+    rows, width = rows_ref.shape
+    text = text_ref[...].astype(jnp.float32)
+    if split:
+        text = (text + refs[0][...].astype(jnp.float32)).astype(jnp.bfloat16)
+        lead = jnp.zeros((rows - text.shape[0], width), jnp.float32)
+        text = jnp.concatenate([lead, text.astype(jnp.float32)], axis=0)
     sections, cape, _ = arrived_ref.shape
     row = iota((rows, sections * cape), 0)
     match = (row == position_ref[...]) & (row < count_ref[0])
     filled = jnp.max(match.astype(jnp.float32), axis=1, keepdims=True) > 0.0
     arrived = arrived_ref[:, :, :width].reshape(sections * cape, width)
     placed = jnp.dot(match.astype(jnp.bfloat16), arrived, preferred_element_type=jnp.float32)
-    whole = jnp.where(filled, placed, text_ref[...].astype(jnp.float32)).astype(jnp.bfloat16)
+    whole = jnp.where(filled, placed, text).astype(jnp.bfloat16)
     slots = (iota((blocks_ref.shape[0], rows), 0) == slot_ref[...]).astype(jnp.bfloat16)
     blocks_ref[...] = jnp.dot(slots, whole, preferred_element_type=jnp.float32).astype(jnp.bfloat16)
     rows_ref[...] = whole
@@ -457,15 +577,16 @@
     text, image, target, weight, bias, gains, queries, pool, owner, fill, block_owner, half, cape, capr
 ):
     sections = lax.axis_size("section")
+    tensors = lax.axis_size("tensor")
     order = ring_order(sections)
     ahead = [(order[i], order[(i + 1) % sections]) for i in range(sections)]
     back = [(b, a) for a, b in ahead]
     depth, width = weight.shape
-    part = depth // 4
+    piece = depth // 4
     rows = text.shape[0]
+    text_rows = rows - rows // LEAST_IMAGE
     heads = queries.shape[1] // HD
-    group = lax.axis_index("groups").astype(jnp.int32)
-    whole_slice = pltpu.VMEM((depth, width), jnp.bfloat16)
+    group = lax.axis_index("groups").astype(jnp.int32).reshape(1)
 
     def up(x):
         return lax.ppermute(x, "section", ahead)
@@ -476,102 +597,119 @@
     def across(x):
         return lax.ppermute(x, "groups", [(0, 1), (1, 0)])
 
-    tensors = lax.axis_size("tensor")
     index = jnp.asarray(ring_tables(sections, tensors).reshape(-1))
     base = (lax.axis_index("section") * tensors + lax.axis_index("tensor")) * (2 * sections)
-    group, base = group.reshape(1), base.astype(jnp.int32).reshape(1)
-    states = (jax.ShapeDtypeStruct((rows, width), jnp.float32),) * 2
-    flops = 4 * rows * depth * width
-
-    def step_product(step, state):
+    base = base.astype(jnp.int32).reshape(1)
+
+    def dots(first, count, inputs, states, dtype, *added):
+        parts = [*added, *(p for pair in slices[first : first + count] for p in pair)]
+        shapes = tuple(jax.ShapeDtypeStruct((x.shape[1], width), dtype) for x in inputs)
         return call(
-            functools.partial(step_kernel, step), states, index, base, group, *normed,
-            owns[step][0], middles[step][0], owns[step][1], middles[step][1], fars[step], *state,
-            smem=(0, 1, 2), aliases={10: 0, 11: 1}, cost=cost(1, 1),
-            scratch=[whole_slice] * 2,
+            functools.partial(dots_kernel, first, count, len(added)),
+            shapes, index, base, *parts, *inputs, *states,
+            smem=(0, 1), cost=cost(1, 1),
+            aliases={2 + len(parts) + len(inputs) + k: k for k in range(len(states))},
         )
 
-    spaces = [pltpu.SMEM] * 3 + [pltpu.HBM] * 4
-    own, middle, image_slot, block_slot = pl.pallas_call(
+    def other_rows(first_term, first, rows):
+        parts = [p for pair in slices for p in pair]
+        return pl.pallas_call(
+            functools.partial(other_kernel, first_term, first),
+            out_shape=jax.ShapeDtypeStruct((rows, width), jnp.bfloat16),
+            in_specs=[pl.BlockSpec(memory_space=pltpu.SMEM)] * 4
+            + [pl.BlockSpec(memory_space=pltpu.HBM)] * 2
+            + [pl.BlockSpec(memory_space=pltpu.VMEM)] * (2 + len(parts)),
+            out_specs=pl.BlockSpec(memory_space=pltpu.VMEM),
+            scratch_shapes=[
+                pltpu.VMEM((sections, rows, depth // 2), jnp.bfloat16),
+                pltpu.SemaphoreType.DMA((sections,)),
+            ],
+            compiler_params=pltpu.CompilerParams(vmem_limit_bytes=VMEM),
+            cost_estimate=cost(1, 1),
+        )(group, half, index, base, others, others_far, factors, gains, *parts)
+
+    spaces = [pltpu.SMEM] * 3 + [pltpu.HBM] * 6
+    own_a, own_b, image_slot, block_slot, picked = pl.pallas_call(
         functools.partial(open_kernel, sections, cape, capr, pool.shape[1]),
         out_shape=(
-            jax.ShapeDtypeStruct((part + GROUP + sections, width), jnp.bfloat16),
-            jax.ShapeDtypeStruct((depth - 2 * part, width), jnp.bfloat16),
+            jax.ShapeDtypeStruct((piece + GROUP + sections, width), jnp.bfloat16),
+            jax.ShapeDtypeStruct((depth // 2 - piece, width), jnp.bfloat16),
             jax.ShapeDtypeStruct((1, rows), jnp.int32),
             jax.ShapeDtypeStruct((1, block_owner.shape[1] * pool.shape[1]), jnp.int32),
+            jax.ShapeDtypeStruct((rows + text_rows, text.shape[1] // 2), jnp.bfloat16),
         ),
         in_specs=[pl.BlockSpec(memory_space=space) for space in spaces],
-        out_specs=[pl.BlockSpec(memory_space=pltpu.VMEM)] * 4,
+        out_specs=[pl.BlockSpec(memory_space=pltpu.VMEM)] * 5,
         scratch_shapes=[
             pltpu.VMEM(target.shape, jnp.int32),
             pltpu.VMEM(block_owner.shape, jnp.int32),
             pltpu.VMEM(queries.shape, jnp.bfloat16),
-            pltpu.SemaphoreType.DMA((5,)),
+            pltpu.SemaphoreType.DMA((5 + sections,)),
         ],
         compiler_params=pltpu.CompilerParams(vmem_limit_bytes=VMEM_ALL),
-    )(group, base, half, weight, target, block_owner, queries)
-    near_own = [up(own), down(own)]
+    )(group, base, half, weight, target, block_owner, queries, image, text)
+    near_a = [up(own_a), down(own_a)]
+    others = across(picked)
     text_far, image_far = beside(text), beside(image)
-    (middle,), (text_far, image_far) = after((middle,), (text_far, image_far))
-    near_middle = [up(middle), down(middle)]
+    (own_b,), (text_far, image_far) = after((own_b,), (text_far, image_far))
+    near_b = [up(own_b), down(own_b)]
     last = sections // 2 - 1
-    owns, middles, fars = {}, {}, {}
-    told = [own]
-    normed_text, token = normalize(sections, half, text, text_far, gains)
-    waiting = [token]
+    slices = [(own_a, own_b)]
+    normed_image, image_factor = own_norm(sections, group, half, image, image_far, gains, rows)
+    waiting, late = [image_factor], text_far
     for step in range(1, last + 1):
-        near_own, waiting = after(near_own, waiting)
-        owns[step] = near_own
-        told += near_own
-        if step > 1:
-            fars[step - 1] = waiting[0]
-            waiting = waiting[1:]
-        fars[step] = across(jnp.concatenate([x[:part] for x in near_own], 0))
-        near_own = [up(near_own[0])] + ([down(near_own[1])] if step < last else [])
-        near_middle, waiting = after(near_middle, [*waiting, image_far])
-        *waiting, image_far = waiting
-        middles[step] = near_middle
-        near_middle = ([up(near_middle[0])] if step < last else []) + [down(near_middle[1])]
+        near_a, waiting = after(near_a, waiting)
+        held_a = near_a
+        near_a = [up(near_a[0])] + ([down(near_a[1])] if step < last else [])
+        near_b, waiting = after(near_b, [*waiting, late])
+        *waiting, late = waiting
+        slices += list(zip(held_a, near_b))
+        near_b = ([up(near_b[0])] if step < last else []) + [down(near_b[1])]
         if step == 1:
-            normed_image, token = normalize(sections, half, image, image_far, gains)
-            normed = (normed_text, normed_image)
-            state = call(
-                first_kernel, states, index, base, *normed, weight, smem=(0, 1), cost=cost(1, 1)
+            image_factor = waiting[0]
+            normed_text, text_factor = own_norm(
+                sections, group, half, text, late, gains, text_rows
             )
-            waiting = [*waiting, token, *state]
-        else:
-            waiting = [*waiting[:-2], *step_product(step - 1, waiting[-2:])]
-        waiting = [fars[step], *waiting]
-    (last_own,), waiting = after(near_own, waiting)
-    fars[last] = waiting[0]
-    last_far = across(last_own[:part])
-    state = step_product(last, waiting[-2:])
-    partial, position = call(
+            waiting, late = [image_factor, text_factor], image_factor
+        elif step == 2:
+            factors = call(
+                factor_kernel,
+                jax.ShapeDtypeStruct((FACTOR_ROWS, rows), jnp.bfloat16),
+                *waiting,
+            )
+            state = dots(0, 2 * step + 1, (normed_text, normed_image), (), jnp.float32)
+            waiting, late = [*state], factors
+    state = waiting
+    (others, factors), last_slice = after((others, late), (*near_a, *near_b))
+    slices.append(last_slice)
+    others_far, factors = beside(others), across(factors)
+    told = [a for a, _ in slices]
+    partial, position, place = call(
         functools.partial(ring_pool_kernel, sections, cape),
         (
             jax.ShapeDtypeStruct((sections, 2 * heads, HD), jnp.bfloat16),
             jax.ShapeDtypeStruct((1, sections * cape), jnp.int32),
+            jax.ShapeDtypeStruct((sections * cape, rows), jnp.bfloat16),
         ),
-        index, base, *told, last_own, pool, owner, fill, *waiting[1:-2],
+        index, base, *told, pool, owner, fill, image_slot,
         smem=(0, 1),
     )
-    send, whole = call(
-        functools.partial(last_image_kernel, sections - 1),
-        (
-            jax.ShapeDtypeStruct((sections, cape, width + HD), jnp.bfloat16),
-            jax.ShapeDtypeStruct((depth, width), jnp.bfloat16),
-        ),
-        index, base, group, normed[1], last_own, *near_middle, last_far, state[1], bias, image_slot, partial,
-        smem=(0, 1, 2), cost=cost(1, 1),
+    done = 2 * last - 1
+    sums = dots(done, sections - done, (normed_text, normed_image), state, jnp.float32, bias)
+    (others_far, factors), (*sums, partial, place) = after(
+        (others_far, factors), (*sums, partial, place)
+    )
+    image_back = across(other_rows(0, 0, rows))
+    text_back = other_rows(3, rows, text_rows)
+    (image_back,), (text_back,) = after((image_back,), (text_back,))
+    text_back = across(text_back)
+    send = call(
+        last_image_kernel,
+        jax.ShapeDtypeStruct((sections, cape, width + HD), jnp.bfloat16),
+        sums[1], image_back, place, partial,
     )
     arrived = exchange(send)
-    text_rows = call(
-        functools.partial(last_text_kernel, sections - 1),
-        jax.ShapeDtypeStruct((rows, width), jnp.bfloat16),
-        index, base, normed[0], whole, state[0], bias,
-        smem=(0, 1), cost=cost(1, 1),
-    )
-    return text_rows, arrived, position, block_slot, arrived
+    return (sums[0], text_back), arrived, position, block_slot, arrived
 
 
 def gather_path(
@@ -616,7 +754,7 @@
         text_sum, image_sum, bias, image_slot,
     )
     arrived = exchange(send.reshape(sections, cape, width))
-    return text_rows, arrived, position, block_slot, exchange(partial)
+    return (text_rows,), arrived, position, block_slot, exchange(partial)
 
 
 def shards(
@@ -645,7 +783,8 @@
         sections == 8
         and tensors == 2
         and lax.axis_size("groups") == 2
-        and kv_weight.shape[0] % 1024 == 0
+        and kv_weight.shape[0] == 1024
+        and rows == 2 * LANES
         and cape == 2 * heads
     )
     text_rows, arrived, position, block_slot, partial = (ring_path if ring else gather_path)(
@@ -665,17 +804,17 @@
         capr,
     )
     whole_rows, block_data = call(
-        place_kernel,
+        functools.partial(place_kernel, ring),
         (
             jax.ShapeDtypeStruct((rows, width), jnp.bfloat16),
             jax.ShapeDtypeStruct((sections * capr, width), jnp.bfloat16),
         ),
-        text_rows,
+        *text_rows,
         arrived,
         position,
         block_slot,
         image_count,
-        smem=(4,),
+        smem=(len(text_rows) + 3,),
     )
     fresh = exchange(block_data.reshape(sections, capr, width)).reshape(sections * capr, width)
     decoded = call(

time: 104 us -> 97.9 us (0.941)
  local copies, waits for them, and re-layouts: 5.43 us -> 0.76 us
  waiting for transfers between devices: 40.3 us -> 44 us
  starting transfers between devices: 33.3 us -> 30.9 us
  Pallas kernels: 21.9 us -> 19.8 us
    ppermute x4, waiting for transfers between devices: 2.69 us -> 9.58 us  [across(): return lax.ppermute(x, 'groups', [(0, 1), (1, 0)])]
    pallas_call x9 -> x7, Pallas kernels: 13.8 us -> 8.2 us  [call(): pl.pallas_call(kernel, out_shape=outs, in_specs=[pl.BlockSpec(memory_spac...]
    unnamed x33 -> x27, local copies, waits for them, and re-layouts: 5.3 us -> 0.76 us
    ppermute x7, waiting for transfers between devices: 16.9 us -> 12.8 us  [up(): return lax.ppermute(x, 'section', ahead)]
    ppermute x7, waiting for transfers between devices: 7.86 us -> 11 us  [down(): return lax.ppermute(x, 'section', back)]
    ppermute x7, starting transfers between devices: 13.9 us -> 11.1 us  [up(): return lax.ppermute(x, 'section', ahead)]
    pallas_call x2 -> x4, Pallas kernels: 5.81 us -> 8.27 us  [the longest x2 4.14 us: other_rows(): pl.pallas_call(functools.partial(other_kernel, first_term, first), out_sh...]
    ppermute x2 -> x3, waiting for transfers between devices: 1.61 us -> 0.14 us  [beside(): return lax.ppermute(x, 'tensor', [(0, 1), (1, 0)])]
  transfers between devices with their start and end apart: 22 -> 23, of which waited for: 15 -> 19; matrix products, arithmetic and copies ran while one was open for 0% -> 0% of each run, Pallas kernels for 18% -> 16%
where the time goes in v4:
time: 97.9 us; the launch traced here: 97.5 us
  waiting for transfers between devices  44 us (45%)
  starting transfers between devices  30.9 us (32%)
  Pallas kernels  19.8 us (20%)
  between operations  2.1 us (2%)
    ppermute x7, waiting for transfers between devices, up(): return lax.ppermute(x, 'section', ahead)  12.8 us
    ppermute x7, starting transfers between devices, up(): return lax.ppermute(x, 'section', ahead)  11.1 us
    ppermute x7, waiting for transfers between devices, down(): return lax.ppermute(x, 'section', back)  11 us
    all_to_all x2, waiting for transfers between devices, exchange(): return lax.all_to_all(x, 'section', split_axis=0, concat_axis=0, tiled=True)  10.5 us
    ppermute x4, waiting for transfers between devices, across(): return lax.ppermute(x, 'groups', [(0, 1), (1, 0)])  9.58 us
    all_to_all x2, starting transfers between devices, exchange(): return lax.all_to_all(x, 'section', split_axis=0, concat_axis=0, tiled=True)  9 us
    pallas_call x7, Pallas kernels, call(): pl.pallas_call(kernel, out_shape=outs, in_specs=[pl.BlockSpec(memory_spac...  8.2 us
    ppermute x4, starting transfers between devices, across(): return lax.ppermute(x, 'groups', [(0, 1), (1, 0)])  6.1 us
  transfers between devices with their start and end apart: 23, of which 19 were waited for; matrix products, arithmetic and copies ran while one was open for 0% of the time, Pallas kernels for 16%

profile of v4, /device:TPU:0, one launch (start us, length us, event | category | flops | bytes accessed | tf_op | source)
XLA Modules:
  0.0 97.5 jit_solution(13518730379284811025)
XLA Ops:
  1.2 3.3 %shard_map.149 = (bf16[272,512]{1,0:T(8,128)(2,1)}, bf16[256,512]{1,0:T(8,128)(2,1)}, s32[1,256]{1,0:T(1,128)}, s32[1,256]{1,0:T(1,128)}, bf16[448,2048]{1,0:T(8,128)(2,1)}) custom-call(s32[1]{0:T(128)} %bitcast.group_ref, s32[1]{0:T(128)} %bitcast.1.base_ref, s32[1]{0:T(128)} %bitcast.2.half_ref, bf16[1024,512]{1,0:T(8,128)(2,1)} %weight_hbm.1, ...), custom_call_target="tpu_custom_call" | custom-call | tf_op jit(solution)/shard_map/pallas_call | solution.py:632
  4.6 3.0 %collective-permute-start = (bf16[448,2048]{1,0:T(8,128)(2,1)}, bf16[448,2048]{1,0:T(8,128)(2,1)S(1)}, u32[]{:S(2)}, u32[]{:S(2)}) collective-permute-start(bf16[448,2048]{1,0:T(8,128)(2,1)} %get-tuple-element.59), channel_id=1, source_target_pairs={{0,16},{16,0},{1,17},{17,1},{2,18},{18,2},{3,19},{19,3},{4,20},{20... | collective-permute-start | bytes 5505032 | tf_op jit(solution)/shard_map/ppermute | solution.py:598
  7.6 1.6 %collective-permute-start.5 = (bf16[272,512]{1,0:T(8,128)(2,1)}, bf16[272,512]{1,0:T(8,128)(2,1)S(1)}, u32[]{:S(2)}, u32[]{:S(2)}) collective-permute-start(bf16[272,512]{1,0:T(8,128)(2,1)} %get-tuple-element.62.refs_0_), channel_id=1, source_target_pairs={{0,4},{4,8},{8,12},{12,14},{14,10},{10,6},{6,2},{2,0},{1,5},{5,9},... | collective-permute-start | bytes 835592 | tf_op jit(solution)/shard_map/ppermute | solution.py:592
  9.6 1.6 %collective-permute-start.3 = (bf16[256,512]{1,0:T(8,128)(2,1)}, bf16[256,512]{1,0:T(8,128)(2,1)S(1)}, u32[]{:S(2)}, u32[]{:S(2)}) collective-permute-start(bf16[256,512]{1,0:T(8,128)(2,1)} %get-tuple-element.61.refs_1_), channel_id=1, source_target_pairs={{0,4},{4,8},{8,12},{12,14},{14,10},{10,6},{6,2},{2,0},{1,5},{5,9},... | collective-permute-start | bytes 786440 | tf_op jit(solution)/shard_map/ppermute | solution.py:592
  11.6 2.8 %shard_map.150 = (bf16[8,256,512]{2,1,0:T(8,128)(2,1)S(1)}, f32[1,256]{1,0:T(1,128)S(1)}) custom-call(s32[1]{0:T(128)} %bitcast.group_ref, s32[1]{0:T(128)} %bitcast.2.half_ref, bf16[256,4096]{1,0:T(8,128)(2,1)S(1)} %copy-done, bf16[256,4096]{1,0:T(8,128)(2,1)} %collective-permute-done.2.far_hbm, f32[1,8192]{1,0:T(1,128)S(1)} %bitcast.11), custom_call_target="tpu_custom_call" | custom-call | flops 1 | bytes 1 | tf_op jit(solution)/shard_map/pallas_call | solution.py:219
  14.4 2.9 %collective-permute-done.5.refs_2_.refs_1_ = bf16[272,512]{1,0:T(8,128)(2,1)S(1)} collective-permute-done((bf16[272,512]{1,0:T(8,128)(2,1)}, bf16[272,512]{1,0:T(8,128)(2,1)S(1)}, u32[]{:S(2)}, u32[]{:S(2)}) %collective-permute-start.5) | collective-permute-done | bytes 278560 | tf_op jit(solution)/shard_map/ppermute | solution.py:592
  17.3 1.6 %collective-permute-done.6.refs_4_.refs_2_ = bf16[272,512]{1,0:T(8,128)(2,1)S(1)} collective-permute-done((bf16[272,512]{1,0:T(8,128)(2,1)}, bf16[272,512]{1,0:T(8,128)(2,1)S(1)}, u32[]{:S(2)}, u32[]{:S(2)}) %collective-permute-start.6) | collective-permute-done | bytes 278560 | tf_op jit(solution)/shard_map/ppermute | solution.py:595
  21.0 2.0 %collective-permute-done.3.refs_3_ = bf16[256,512]{1,0:T(8,128)(2,1)S(1)} collective-permute-done((bf16[256,512]{1,0:T(8,128)(2,1)}, bf16[256,512]{1,0:T(8,128)(2,1)S(1)}, u32[]{:S(2)}, u32[]{:S(2)}) %collective-permute-start.3) | collective-permute-done | bytes 262176 | tf_op jit(solution)/shard_map/ppermute | solution.py:592
  22.9 1.6 %collective-permute-done.4.refs_5_ = bf16[256,512]{1,0:T(8,128)(2,1)S(1)} collective-permute-done((bf16[256,512]{1,0:T(8,128)(2,1)}, bf16[256,512]{1,0:T(8,128)(2,1)S(1)}, u32[]{:S(2)}, u32[]{:S(2)}) %collective-permute-start.4) | collective-permute-done | bytes 262176 | tf_op jit(solution)/shard_map/ppermute | solution.py:595
  28.0 2.6 %collective-permute-done.10.refs_8_.refs_4_ = bf16[272,512]{1,0:T(8,128)(2,1)S(1)} collective-permute-done((bf16[272,512]{1,0:T(8,128)(2,1)S(1)}, bf16[272,512]{1,0:T(8,128)(2,1)S(1)}, u32[]{:S(2)}, u32[]{:S(2)}) %collective-permute-start.10) | collective-permute-done | bytes 278560 | tf_op jit(solution)/shard_map/ppermute | solution.py:595
  30.5 1.6 %collective-permute-start.13 = (bf16[272,512]{1,0:T(8,128)(2,1)S(1)}, bf16[272,512]{1,0:T(8,128)(2,1)S(1)}, u32[]{:S(2)}, u32[]{:S(2)}) collective-permute-start(bf16[272,512]{1,0:T(8,128)(2,1)S(1)} %collective-permute-done.9.refs_6_.refs_3_), channel_id=1, source_target_pairs={{0,4},{4,8},{8,12},{12,14},{14,10},{10,6},{6,2},{2,0},{1,5},{5,9},... | collective-permute-start | bytes 835592 | tf_op jit(solution)/shard_map/ppermute | solution.py:592
  32.6 2.1 %collective-permute-done.7.refs_7_ = bf16[256,512]{1,0:T(8,128)(2,1)S(1)} collective-permute-done((bf16[256,512]{1,0:T(8,128)(2,1)S(1)}, bf16[256,512]{1,0:T(8,128)(2,1)S(1)}, u32[]{:S(2)}, u32[]{:S(2)}) %collective-permute-start.7) | collective-permute-done | bytes 262176 | tf_op jit(solution)/shard_map/ppermute | solution.py:592
  38.2 1.9 %shard_map.152 = (f32[192,512]{1,0:T(8,128)S(1)}, f32[256,512]{1,0:T(8,128)S(1)}) custom-call(s32[256]{0:T(256)S(1)} %copy-done.7, s32[1]{0:T(128)} %bitcast.1.base_ref, bf16[272,512]{1,0:T(8,128)(2,1)S(1)} %copy-done.2, bf16[256,512]{1,0:T(8,128)(2,1)S(1)} %copy-done.3, bf16[272,512]{1,0:T(8,128)(2,1)S(1)} %collective-permute-done.5.refs_2_.refs_1_, ...), custom_call_target="tpu_custom_call" | custom-call | flops 1 | bytes 1 | tf_op jit(solution)/shard_map/pallas_call | solution.py:28
  43.7 2.5 %collective-permute-done.11.refs_2_.refs_11_ = bf16[256,512]{1,0:T(8,128)(2,1)S(1)} collective-permute-done((bf16[256,512]{1,0:T(8,128)(2,1)S(1)}, bf16[256,512]{1,0:T(8,128)(2,1)S(1)}, u32[]{:S(2)}, u32[]{:S(2)}) %collective-permute-start.11) | collective-permute-done | bytes 262176 | tf_op jit(solution)/shard_map/ppermute | solution.py:592
  48.0 2.9 %collective-permute-done.15.refs_5_.refs_7_.refs_14_ = bf16[272,512]{1,0:T(8,128)(2,1)S(1)} collective-permute-done((bf16[272,512]{1,0:T(8,128)(2,1)S(1)}, bf16[272,512]{1,0:T(8,128)(2,1)S(1)}, u32[]{:S(2)}, u32[]{:S(2)}) %collective-permute-start.15) | collective-permute-done | bytes 278560 | tf_op jit(solution)/shard_map/ppermute | solution.py:592
  50.9 2.1 %collective-permute-done.16.refs_6_.refs_15_ = bf16[256,512]{1,0:T(8,128)(2,1)S(1)} collective-permute-done((bf16[256,512]{1,0:T(8,128)(2,1)S(1)}, bf16[256,512]{1,0:T(8,128)(2,1)S(1)}, u32[]{:S(2)}, u32[]{:S(2)}) %collective-permute-start.16) | collective-permute-done | bytes 262176 | tf_op jit(solution)/shard_map/ppermute | solution.py:595
  56.8 2.2 %shard_map.156 = bf16[256,512]{1,0:T(8,128)(2,1)S(1)} custom-call(s32[1]{0:T(128)} %bitcast.group_ref, s32[1]{0:T(128)} %bitcast.2.half_ref, s32[256]{0:T(256)S(1)} %copy-done.7, s32[1]{0:T(128)} %bitcast.1.base_ref, bf16[448,2048]{1,0:T(8,128)(2,1)S(1)} %collective-permute-done.near_hbm, bf16[448,2048]{1,0:T(8,128)(2,1)S(1)} %collective-permute-done.17.far_hbm, ...), custom_call_target="tpu_custom_call" | custom-call | flops 1 | bytes 1 | tf_op jit(solution)/shard_map/pallas_call | solution.py:616
  60.3 2.0 %shard_map.157 = bf16[192,512]{1,0:T(8,128)(2,1)S(1)} custom-call(s32[1]{0:T(128)} %bitcast.group_ref, s32[1]{0:T(128)} %bitcast.2.half_ref, s32[256]{0:T(256)S(1)} %copy-done.7, s32[1]{0:T(128)} %bitcast.1.base_ref, bf16[448,2048]{1,0:T(8,128)(2,1)S(1)} %collective-permute-done.near_hbm, bf16[448,2048]{1,0:T(8,128)(2,1)S(1)} %collective-permute-done.17.far_hbm, ...), custom_call_target="tpu_custom_call" | custom-call | flops 1 | bytes 1 | tf_op jit(solution)/shard_map/pallas_call | solution.py:616
  62.3 5.1 %collective-permute-done.19.other_ref = bf16[256,512]{1,0:T(8,128)(2,1)S(1)} collective-permute-done((bf16[256,512]{1,0:T(8,128)(2,1)S(1)}, bf16[256,512]{1,0:T(8,128)(2,1)S(1)}, u32[]{:S(2)}, u32[]{:S(2)}) %collective-permute-start.19) | collective-permute-done | bytes 262176 | tf_op jit(solution)/shard_map/ppermute | solution.py:598
  68.4 5.4 %all-to-all-start = ((bf16[8,32,640]{2,1,0:T(8,128)(2,1)}), bf16[8,32,640]{2,1,0:T(8,128)(2,1)S(1)}, u32[]{:S(2)}, u32[]{:S(2)}) async-start(bf16[8,32,640]{2,1,0:T(8,128)(2,1)} %shard_map.158), calls=%async_computation | async-start | bytes 655360 | tf_op jit(solution)/shard_map/all_to_all | solution.py:552
  75.7 3.9 %collective-permute-done.20.refs_0_ = bf16[192,512]{1,0:T(8,128)(2,1)S(1)} collective-permute-done((bf16[192,512]{1,0:T(8,128)(2,1)S(1)}, bf16[192,512]{1,0:T(8,128)(2,1)S(1)}, u32[]{:S(2)}, u32[]{:S(2)}) %collective-permute-start.20) | collective-permute-done | bytes 196640 | tf_op jit(solution)/shard_map/ppermute | solution.py:598
  79.6 3.9 %all-to-all-done.refs_1_.partial_ref = bf16[8,32,640]{2,1,0:T(8,128)(2,1)S(1)} async-done(((bf16[8,32,640]{2,1,0:T(8,128)(2,1)}), bf16[8,32,640]{2,1,0:T(8,128)(2,1)S(1)}, u32[]{:S(2)}, u32[]{:S(2)}) %all-to-all-start) | async-done | bytes 327712 | tf_op jit(solution)/shard_map/all_to_all | solution.py:552
  84.7 3.6 %all-to-all-start.1 = ((bf16[8,32,512]{2,1,0:T(8,128)(2,1)}), bf16[8,32,512]{2,1,0:T(8,128)(2,1)S(1)}, u32[]{:S(2)}, u32[]{:S(2)}) async-start(bf16[8,32,512]{2,1,0:T(8,128)(2,1)} %bitcast.9), calls=%async_computation.1 | async-start | bytes 524288 | tf_op jit(solution)/shard_map/all_to_all | solution.py:552
  90.3 6.6 %all-to-all-done.1 = bf16[8,32,512]{2,1,0:T(8,128)(2,1)S(1)} async-done(((bf16[8,32,512]{2,1,0:T(8,128)(2,1)}), bf16[8,32,512]{2,1,0:T(8,128)(2,1)S(1)}, u32[]{:S(2)}, u32[]{:S(2)}) %all-to-all-start.1) | async-done | bytes 262176 | tf_op jit(solution)/shard_map/all_to_all | solution.py:552
  (61 shorter events, 26.8 us)
Async XLA Ops:
  0.6 9.0 %collective-permute-start.1 = (bf16[256,4096]{1,0:T(8,128)(2,1)}, bf16[256,4096]{1,0:T(8,128)(2,1)S(1)}, u32[]{:S(2)}, u32[]{:S(2)}) collective-permute-start(bf16[256,4096]{1,0:T(8,128)(2,1)} %near_hbm.3), channel_id=1, source_target_pairs={{0,1},{1,0},{2,3},{3,2},{4,5},{5,4},{6,7},{7,6},{8,9},{9,8},{10,11... | collective-permute-start | bytes 6291464 | tf_op jit(solution)/shard_map/ppermute | solution.py:548
  1.1 8.4 %collective-permute-start.2 = (bf16[256,4096]{1,0:T(8,128)(2,1)}, bf16[256,4096]{1,0:T(8,128)(2,1)}, u32[]{:S(2)}, u32[]{:S(2)}) collective-permute-start(bf16[256,4096]{1,0:T(8,128)(2,1)} %near_hbm.2), channel_id=1, source_target_pairs={{0,1},{1,0},{2,3},{3,2},{4,5},{5,4},{6,7},{7,6},{8,9},{9,8},{10,11... | collective-permute-start | bytes 6291464 | tf_op jit(solution)/shard_map/ppermute | solution.py:548
  4.6 43.5 %collective-permute-start = (bf16[448,2048]{1,0:T(8,128)(2,1)}, bf16[448,2048]{1,0:T(8,128)(2,1)S(1)}, u32[]{:S(2)}, u32[]{:S(2)}) collective-permute-start(bf16[448,2048]{1,0:T(8,128)(2,1)} %get-tuple-element.59), channel_id=1, source_target_pairs={{0,16},{16,0},{1,17},{17,1},{2,18},{18,2},{3,19},{19,3},{4,20},{20... | collective-permute-start | bytes 5505032 | tf_op jit(solution)/shard_map/ppermute | solution.py:598
  7.6 9.8 %collective-permute-start.5 = (bf16[272,512]{1,0:T(8,128)(2,1)}, bf16[272,512]{1,0:T(8,128)(2,1)S(1)}, u32[]{:S(2)}, u32[]{:S(2)}) collective-permute-start(bf16[272,512]{1,0:T(8,128)(2,1)} %get-tuple-element.62.refs_0_), channel_id=1, source_target_pairs={{0,4},{4,8},{8,12},{12,14},{14,10},{10,6},{6,2},{2,0},{1,5},{5,9},... | collective-permute-start | bytes 835592 | tf_op jit(solution)/shard_map/ppermute | solution.py:592
  9.1 9.8 %collective-permute-start.6 = (bf16[272,512]{1,0:T(8,128)(2,1)}, bf16[272,512]{1,0:T(8,128)(2,1)S(1)}, u32[]{:S(2)}, u32[]{:S(2)}) collective-permute-start(bf16[272,512]{1,0:T(8,128)(2,1)} %get-tuple-element.62.refs_0_), channel_id=1, source_target_pairs={{4,0},{8,4},{12,8},{14,12},{10,14},{6,10},{2,6},{0,2},{5,1},{9,5},... | collective-permute-start | bytes 835592 | tf_op jit(solution)/shard_map/ppermute | solution.py:595
  9.6 13.3 %collective-permute-start.3 = (bf16[256,512]{1,0:T(8,128)(2,1)}, bf16[256,512]{1,0:T(8,128)(2,1)S(1)}, u32[]{:S(2)}, u32[]{:S(2)}) collective-permute-start(bf16[256,512]{1,0:T(8,128)(2,1)} %get-tuple-element.61.refs_1_), channel_id=1, source_target_pairs={{0,4},{4,8},{8,12},{12,14},{14,10},{10,6},{6,2},{2,0},{1,5},{5,9},... | collective-permute-start | bytes 786440 | tf_op jit(solution)/shard_map/ppermute | solution.py:592
  11.2 13.3 %collective-permute-start.4 = (bf16[256,512]{1,0:T(8,128)(2,1)}, bf16[256,512]{1,0:T(8,128)(2,1)S(1)}, u32[]{:S(2)}, u32[]{:S(2)}) collective-permute-start(bf16[256,512]{1,0:T(8,128)(2,1)} %get-tuple-element.61.refs_1_), channel_id=1, source_target_pairs={{4,0},{8,4},{12,8},{14,12},{10,14},{6,10},{2,6},{0,2},{5,1},{9,5},... | collective-permute-start | bytes 786440 | tf_op jit(solution)/shard_map/ppermute | solution.py:595
  19.0 11.6 %collective-permute-start.10 = (bf16[272,512]{1,0:T(8,128)(2,1)S(1)}, bf16[272,512]{1,0:T(8,128)(2,1)S(1)}, u32[]{:S(2)}, u32[]{:S(2)}) collective-permute-start(bf16[272,512]{1,0:T(8,128)(2,1)S(1)} %collective-permute-done.6.refs_4_.refs_2_), channel_id=1, source_target_pairs={{4,0},{8,4},{12,8},{14,12},{10,14},{6,10},{2,6},{0,2},{5,1},{9,5},... | collective-permute-start | bytes 835592 | tf_op jit(solution)/shard_map/ppermute | solution.py:595
  19.4 11.1 %collective-permute-start.9 = (bf16[272,512]{1,0:T(8,128)(2,1)S(1)}, bf16[272,512]{1,0:T(8,128)(2,1)S(1)}, u32[]{:S(2)}, u32[]{:S(2)}) collective-permute-start(bf16[272,512]{1,0:T(8,128)(2,1)S(1)} %collective-permute-done.5.refs_2_.refs_1_), channel_id=1, source_target_pairs={{0,4},{4,8},{8,12},{12,14},{14,10},{10,6},{6,2},{2,0},{1,5},{5,9},... | collective-permute-start | bytes 835592 | tf_op jit(solution)/shard_map/ppermute | solution.py:592
  24.6 10.1 %collective-permute-start.7 = (bf16[256,512]{1,0:T(8,128)(2,1)S(1)}, bf16[256,512]{1,0:T(8,128)(2,1)S(1)}, u32[]{:S(2)}, u32[]{:S(2)}) collective-permute-start(bf16[256,512]{1,0:T(8,128)(2,1)S(1)} %collective-permute-done.3.refs_3_), channel_id=1, source_target_pairs={{0,4},{4,8},{8,12},{12,14},{14,10},{10,6},{6,2},{2,0},{1,5},{5,9},... | collective-permute-start | bytes 786440 | tf_op jit(solution)/shard_map/ppermute | solution.py:592
  26.1 10.0 %collective-permute-start.8 = (bf16[256,512]{1,0:T(8,128)(2,1)S(1)}, bf16[256,512]{1,0:T(8,128)(2,1)S(1)}, u32[]{:S(2)}, u32[]{:S(2)}) collective-permute-start(bf16[256,512]{1,0:T(8,128)(2,1)S(1)} %collective-permute-done.4.refs_5_), channel_id=1, source_target_pairs={{4,0},{8,4},{12,8},{14,12},{10,14},{6,10},{2,6},{0,2},{5,1},{9,5},... | collective-permute-start | bytes 786440 | tf_op jit(solution)/shard_map/ppermute | solution.py:595
  30.5 10.1 %collective-permute-start.13 = (bf16[272,512]{1,0:T(8,128)(2,1)S(1)}, bf16[272,512]{1,0:T(8,128)(2,1)S(1)}, u32[]{:S(2)}, u32[]{:S(2)}) collective-permute-start(bf16[272,512]{1,0:T(8,128)(2,1)S(1)} %collective-permute-done.9.refs_6_.refs_3_), channel_id=1, source_target_pairs={{0,4},{4,8},{8,12},{12,14},{14,10},{10,6},{6,2},{2,0},{1,5},{5,9},... | collective-permute-start | bytes 835592 | tf_op jit(solution)/shard_map/ppermute | solution.py:592
  32.1 10.0 %collective-permute-start.14 = (bf16[272,512]{1,0:T(8,128)(2,1)S(1)}, bf16[272,512]{1,0:T(8,128)(2,1)S(1)}, u32[]{:S(2)}, u32[]{:S(2)}) collective-permute-start(bf16[272,512]{1,0:T(8,128)(2,1)S(1)} %collective-permute-done.10.refs_8_.refs_4_), channel_id=1, source_target_pairs={{4,0},{8,4},{12,8},{14,12},{10,14},{6,10},{2,6},{0,2},{5,1},{9,5},... | collective-permute-start | bytes 835592 | tf_op jit(solution)/shard_map/ppermute | solution.py:595
  36.1 10.1 %collective-permute-start.11 = (bf16[256,512]{1,0:T(8,128)(2,1)S(1)}, bf16[256,512]{1,0:T(8,128)(2,1)S(1)}, u32[]{:S(2)}, u32[]{:S(2)}) collective-permute-start(bf16[256,512]{1,0:T(8,128)(2,1)S(1)} %collective-permute-done.7.refs_7_), channel_id=1, source_target_pairs={{0,4},{4,8},{8,12},{12,14},{14,10},{10,6},{6,2},{2,0},{1,5},{5,9},... | collective-permute-start | bytes 786440 | tf_op jit(solution)/shard_map/ppermute | solution.py:592
  37.7 8.5 %collective-permute-start.12 = (bf16[256,512]{1,0:T(8,128)(2,1)S(1)}, bf16[256,512]{1,0:T(8,128)(2,1)S(1)}, u32[]{:S(2)}, u32[]{:S(2)}) collective-permute-start(bf16[256,512]{1,0:T(8,128)(2,1)S(1)} %collective-permute-done.8.refs_9_), channel_id=1, source_target_pairs={{4,0},{8,4},{12,8},{14,12},{10,14},{6,10},{2,6},{0,2},{5,1},{9,5},... | collective-permute-start | bytes 786440 | tf_op jit(solution)/shard_map/ppermute | solution.py:595
  42.1 8.8 %collective-permute-start.15 = (bf16[272,512]{1,0:T(8,128)(2,1)S(1)}, bf16[272,512]{1,0:T(8,128)(2,1)S(1)}, u32[]{:S(2)}, u32[]{:S(2)}) collective-permute-start(bf16[272,512]{1,0:T(8,128)(2,1)S(1)} %collective-permute-done.13.refs_1_.refs_5_.refs_10_), channel_id=1, source_target_pairs={{0,4},{4,8},{8,12},{12,14},{14,10},{10,6},{6,2},{2,0},{1,5},{5,9},... | collective-permute-start | bytes 835592 | tf_op jit(solution)/shard_map/ppermute | solution.py:592
  46.2 6.8 %collective-permute-start.16 = (bf16[256,512]{1,0:T(8,128)(2,1)S(1)}, bf16[256,512]{1,0:T(8,128)(2,1)S(1)}, u32[]{:S(2)}, u32[]{:S(2)}) collective-permute-start(bf16[256,512]{1,0:T(8,128)(2,1)S(1)} %collective-permute-done.12.refs_4_.refs_13_), channel_id=1, source_target_pairs={{4,0},{8,4},{12,8},{14,12},{10,14},{6,10},{2,6},{0,2},{5,1},{9,5},... | collective-permute-start | bytes 786440 | tf_op jit(solution)/shard_map/ppermute | solution.py:595
  53.0 3.8 %collective-permute-start.17 = (bf16[448,2048]{1,0:T(8,128)(2,1)S(1)}, bf16[448,2048]{1,0:T(8,128)(2,1)S(1)}, u32[]{:S(2)}, u32[]{:S(2)}) collective-permute-start(bf16[448,2048]{1,0:T(8,128)(2,1)S(1)} %collective-permute-done.near_hbm), channel_id=1, source_target_pairs={{0,1},{1,0},{2,3},{3,2},{4,5},{5,4},{6,7},{7,6},{8,9},{9,8},{10,11... | collective-permute-start | bytes 5505032 | tf_op jit(solution)/shard_map/ppermute | solution.py:548
  53.0 3.7 %collective-permute-start.18 = (bf16[16,256]{1,0:T(8,128)(2,1)S(1)}, bf16[16,256]{1,0:T(8,128)(2,1)S(1)}, u32[]{:S(2)}, u32[]{:S(2)}) collective-permute-start(bf16[16,256]{1,0:T(8,128)(2,1)S(1)} %shard_map.153), channel_id=1, source_target_pairs={{0,16},{16,0},{1,17},{17,1},{2,18},{18,2},{3,19},{19,3},{4,20},{20... | collective-permute-start | bytes 24584 | tf_op jit(solution)/shard_map/ppermute | solution.py:598
  59.0 8.4 %collective-permute-start.19 = (bf16[256,512]{1,0:T(8,128)(2,1)S(1)}, bf16[256,512]{1,0:T(8,128)(2,1)S(1)}, u32[]{:S(2)}, u32[]{:S(2)}) collective-permute-start(bf16[256,512]{1,0:T(8,128)(2,1)S(1)} %shard_map.156), channel_id=1, source_target_pairs={{0,16},{16,0},{1,17},{17,1},{2,18},{18,2},{3,19},{19,3},{4,20},{20... | collective-permute-start | bytes 786440 | tf_op jit(solution)/shard_map/ppermute | solution.py:598
  62.3 26.7 %copy-start.6 = (bf16[1,2048]{1,0:T(2,128)(2,1)S(1)}, bf16[1,2048]{1,0:T(2,128)(2,1)}, u32[]{:S(2)}) copy-start(bf16[1,2048]{1,0:T(2,128)(2,1)} %query_ref.1) | copy-start | bytes 12292
  68.4 15.1 %all-to-all-start = ((bf16[8,32,640]{2,1,0:T(8,128)(2,1)}), bf16[8,32,640]{2,1,0:T(8,128)(2,1)S(1)}, u32[]{:S(2)}, u32[]{:S(2)}) async-start(bf16[8,32,640]{2,1,0:T(8,128)(2,1)} %shard_map.158), calls=%async_computation | async-start | bytes 655360 | tf_op jit(solution)/shard_map/all_to_all | solution.py:552
  73.8 5.8 %collective-permute-start.20 = (bf16[192,512]{1,0:T(8,128)(2,1)S(1)}, bf16[192,512]{1,0:T(8,128)(2,1)S(1)}, u32[]{:S(2)}, u32[]{:S(2)}) collective-permute-start(bf16[192,512]{1,0:T(8,128)(2,1)S(1)} %shard_map.157), channel_id=1, source_target_pairs={{0,16},{16,0},{1,17},{17,1},{2,18},{18,2},{3,19},{19,3},{4,20},{20... | collective-permute-start | bytes 589832 | tf_op jit(solution)/shard_map/ppermute | solution.py:598
  84.7 12.2 %all-to-all-start.1 = ((bf16[8,32,512]{2,1,0:T(8,128)(2,1)}), bf16[8,32,512]{2,1,0:T(8,128)(2,1)S(1)}, u32[]{:S(2)}, u32[]{:S(2)}) async-start(bf16[8,32,512]{2,1,0:T(8,128)(2,1)} %bitcast.9), calls=%async_computation.1 | async-start | bytes 524288 | tf_op jit(solution)/shard_map/all_to_all | solution.py:552
  (12 other events, 139.8 us)

commit v5 on v4

--- a/solution.py
+++ b/solution.py
@@ -237,36 +237,24 @@
 
 
 def other_kernel(
-    first_term, first, group_ref, half_ref, index_ref, base_ref, near_hbm, far_hbm, factor_ref, gains_ref, *refs
+    first_term, group_ref, half_ref, index_ref, base_ref, near_ref, far_ref, factor_ref, gains_ref, *refs
 ):
-    *weights, out_ref, held, sems = refs
-    slices, rows, width = held.shape
-    half = slices // 2
-    copies = [
-        pltpu.make_async_copy(
-            hbm.at[pl.ds(first, rows), pl.ds(j * width, width)],
-            held.at[side * half + j],
-            sems.at[side * half + j],
-        )
-        for side, hbm in enumerate((near_hbm, far_hbm))
-        for j in range(half)
-    ]
-    for copy in copies:
-        copy.start()
+    *weights, out_ref = refs
+    slices, rows = len(weights) // 2, out_ref.shape[0]
+    half, width = slices // 2, near_ref.shape[1] // (slices // 2)
     terms = factor_ref[...].astype(jnp.float32)
     factor = terms[first_term : first_term + 1]
     for k in range(1, 3):
         factor = factor + terms[first_term + k : first_term + k + 1]
     factor = jnp.sum(jnp.where(diagonal(rows), factor[:, :rows], 0.0), axis=1, keepdims=True)
-    for copy in copies:
-        copy.wait()
     total = 0.0
     for k in range(slices):
         block = index_ref[base_ref[0] + k]
         far = (block >= half).astype(jnp.int32)
         side = half_ref[0] + far - 2 * far * half_ref[0]
         lane = (2 * (side * half + block - far * half) + group_ref[0]) * width
-        value = held[block].astype(jnp.float32) * factor
+        at = pl.ds(pl.multiple_of((block - far * half) * width, LANES), width)
+        value = jnp.where(far > 0, far_ref[:, at], near_ref[:, at]).astype(jnp.float32) * factor
         value = value * gains_ref[:, pl.ds(pl.multiple_of(lane, LANES), width)]
         value = value.astype(jnp.bfloat16)
         at = 0
@@ -611,22 +599,18 @@
             aliases={2 + len(parts) + len(inputs) + k: k for k in range(len(states))},
         )
 
-    def other_rows(first_term, first, rows):
+    def other_rows(first_term, near, far):
+        rows = near.shape[0]
         parts = [p for pair in slices for p in pair]
         return pl.pallas_call(
-            functools.partial(other_kernel, first_term, first),
+            functools.partial(other_kernel, first_term),
             out_shape=jax.ShapeDtypeStruct((rows, width), jnp.bfloat16),
             in_specs=[pl.BlockSpec(memory_space=pltpu.SMEM)] * 4
-            + [pl.BlockSpec(memory_space=pltpu.HBM)] * 2
-            + [pl.BlockSpec(memory_space=pltpu.VMEM)] * (2 + len(parts)),
+            + [pl.BlockSpec(memory_space=pltpu.VMEM)] * (4 + len(parts)),
             out_specs=pl.BlockSpec(memory_space=pltpu.VMEM),
-            scratch_shapes=[
-                pltpu.VMEM((sections, rows, depth // 2), jnp.bfloat16),
-                pltpu.SemaphoreType.DMA((sections,)),
-            ],
             compiler_params=pltpu.CompilerParams(vmem_limit_bytes=VMEM),
             cost_estimate=cost(1, 1),
-        )(group, half, index, base, others, others_far, factors, gains, *parts)
+        )(group, half, index, base, near, far, factors, gains, *parts)
 
     spaces = [pltpu.SMEM] * 3 + [pltpu.HBM] * 6
     own_a, own_b, image_slot, block_slot, picked = pl.pallas_call(
@@ -680,9 +664,11 @@
             state = dots(0, 2 * step + 1, (normed_text, normed_image), (), jnp.float32)
             waiting, late = [*state], factors
     state = waiting
-    (others, factors), last_slice = after((others, late), (*near_a, *near_b))
+    (other_image, other_text, factors), last_slice = after(
+        (others[:rows], others[rows:], late), (*near_a, *near_b)
+    )
     slices.append(last_slice)
-    others_far, factors = beside(others), across(factors)
+    image_far, factors = beside(other_image), across(factors)
     told = [a for a, _ in slices]
     partial, position, place = call(
         functools.partial(ring_pool_kernel, sections, cape),
@@ -696,12 +682,12 @@
     )
     done = 2 * last - 1
     sums = dots(done, sections - done, (normed_text, normed_image), state, jnp.float32, bias)
-    (others_far, factors), (*sums, partial, place) = after(
-        (others_far, factors), (*sums, partial, place)
-    )
-    image_back = across(other_rows(0, 0, rows))
-    text_back = other_rows(3, rows, text_rows)
-    (image_back,), (text_back,) = after((image_back,), (text_back,))
+    (image_far, factors), sums = after((image_far, factors), sums)
+    image_back = across(other_rows(0, other_image, image_far))
+    text_back = other_rows(3, other_text, beside(other_text))
+    (image_back,), (text_back, partial, place) = after(
+        (image_back,), (text_back, partial, place)
+    )
     text_back = across(text_back)
     send = call(
         last_image_kernel,

time: 97.9 us -> 95 us (0.970)
  waiting for transfers between devices: 44 us -> 42.5 us
    all_to_all x2, waiting for transfers between devices: 10.5 us -> 9.19 us  [exchange(): return lax.all_to_all(x, 'section', split_axis=0, concat_axis=0, tiled=True)]
    ppermute x4, starting transfers between devices: 6.1 us -> 4.95 us  [across(): return lax.ppermute(x, 'groups', [(0, 1), (1, 0)])]
  transfers between devices with their start and end apart: 23 -> 24, of which waited for: 19 -> 18; matrix products, arithmetic and copies ran while one was open for 0% -> 0% of each run, Pallas kernels for 16% -> 18%
where the time goes in v5:
time: 95 us; the launch traced here: 94.7 us
  waiting for transfers between devices  42.5 us (45%)
  starting transfers between devices  30 us (32%)
  Pallas kernels  19.1 us (20%)
  between operations  2.11 us (2%)
    ppermute x7, waiting for transfers between devices, up(): return lax.ppermute(x, 'section', ahead)  12.6 us
    ppermute x7, starting transfers between devices, up(): return lax.ppermute(x, 'section', ahead)  11.1 us
    ppermute x7, waiting for transfers between devices, down(): return lax.ppermute(x, 'section', back)  11 us
    ppermute x4, waiting for transfers between devices, across(): return lax.ppermute(x, 'groups', [(0, 1), (1, 0)])  9.66 us
    all_to_all x2, waiting for transfers between devices, exchange(): return lax.all_to_all(x, 'section', split_axis=0, concat_axis=0, tiled=True)  9.19 us
    all_to_all x2, starting transfers between devices, exchange(): return lax.all_to_all(x, 'section', split_axis=0, concat_axis=0, tiled=True)  8.76 us
    pallas_call x7, Pallas kernels, call(): pl.pallas_call(kernel, out_shape=outs, in_specs=[pl.BlockSpec(memory_spac...  8.19 us
    ppermute x4, starting transfers between devices, across(): return lax.ppermute(x, 'groups', [(0, 1), (1, 0)])  4.95 us
  transfers between devices with their start and end apart: 24, of which 18 were waited for; matrix products, arithmetic and copies ran while one was open for 0% of the time, Pallas kernels for 18%

profile of v5, /device:TPU:0, one launch (start us, length us, event | category | flops | bytes accessed | tf_op | source)
XLA Modules:
  0.0 94.7 jit_solution(2110576518058419338)
XLA Ops:
  1.2 3.3 %shard_map.149 = (bf16[272,512]{1,0:T(8,128)(2,1)}, bf16[256,512]{1,0:T(8,128)(2,1)}, s32[1,256]{1,0:T(1,128)}, s32[1,256]{1,0:T(1,128)}, bf16[448,2048]{1,0:T(8,128)(2,1)}) custom-call(s32[1]{0:T(128)} %bitcast.group_ref, s32[1]{0:T(128)} %bitcast.1.base_ref, s32[1]{0:T(128)} %bitcast.2.half_ref, bf16[1024,512]{1,0:T(8,128)(2,1)} %weight_hbm.1, ...), custom_call_target="tpu_custom_call" | custom-call | tf_op jit(solution)/shard_map/pallas_call | solution.py:616
  4.6 3.0 %collective-permute-start = (bf16[448,2048]{1,0:T(8,128)(2,1)}, bf16[448,2048]{1,0:T(8,128)(2,1)S(1)}, u32[]{:S(2)}, u32[]{:S(2)}) collective-permute-start(bf16[448,2048]{1,0:T(8,128)(2,1)} %get-tuple-element.60), channel_id=1, source_target_pairs={{0,16},{16,0},{1,17},{17,1},{2,18},{18,2},{3,19},{19,3},{4,20},{20... | collective-permute-start | bytes 5505032 | tf_op jit(solution)/shard_map/ppermute | solution.py:586
  7.6 1.6 %collective-permute-start.5 = (bf16[272,512]{1,0:T(8,128)(2,1)}, bf16[272,512]{1,0:T(8,128)(2,1)S(1)}, u32[]{:S(2)}, u32[]{:S(2)}) collective-permute-start(bf16[272,512]{1,0:T(8,128)(2,1)} %get-tuple-element.63.refs_0_), channel_id=1, source_target_pairs={{0,4},{4,8},{8,12},{12,14},{14,10},{10,6},{6,2},{2,0},{1,5},{5,9},... | collective-permute-start | bytes 835592 | tf_op jit(solution)/shard_map/ppermute | solution.py:580
  9.6 1.6 %collective-permute-start.3 = (bf16[256,512]{1,0:T(8,128)(2,1)}, bf16[256,512]{1,0:T(8,128)(2,1)S(1)}, u32[]{:S(2)}, u32[]{:S(2)}) collective-permute-start(bf16[256,512]{1,0:T(8,128)(2,1)} %get-tuple-element.62.refs_1_), channel_id=1, source_target_pairs={{0,4},{4,8},{8,12},{12,14},{14,10},{10,6},{6,2},{2,0},{1,5},{5,9},... | collective-permute-start | bytes 786440 | tf_op jit(solution)/shard_map/ppermute | solution.py:580
  11.6 2.8 %shard_map.150 = (bf16[8,256,512]{2,1,0:T(8,128)(2,1)S(1)}, f32[1,256]{1,0:T(1,128)S(1)}) custom-call(s32[1]{0:T(128)} %bitcast.group_ref, s32[1]{0:T(128)} %bitcast.2.half_ref, bf16[256,4096]{1,0:T(8,128)(2,1)S(1)} %copy-done, bf16[256,4096]{1,0:T(8,128)(2,1)} %collective-permute-done.2.far_hbm, f32[1,8192]{1,0:T(1,128)S(1)} %bitcast.11), custom_call_target="tpu_custom_call" | custom-call | flops 1 | bytes 1 | tf_op jit(solution)/shard_map/pallas_call | solution.py:219
  14.4 2.9 %collective-permute-done.5.refs_2_.refs_1_ = bf16[272,512]{1,0:T(8,128)(2,1)S(1)} collective-permute-done((bf16[272,512]{1,0:T(8,128)(2,1)}, bf16[272,512]{1,0:T(8,128)(2,1)S(1)}, u32[]{:S(2)}, u32[]{:S(2)}) %collective-permute-start.5) | collective-permute-done | bytes 278560 | tf_op jit(solution)/shard_map/ppermute | solution.py:580
  17.3 1.6 %collective-permute-done.6.refs_4_.refs_2_ = bf16[272,512]{1,0:T(8,128)(2,1)S(1)} collective-permute-done((bf16[272,512]{1,0:T(8,128)(2,1)}, bf16[272,512]{1,0:T(8,128)(2,1)S(1)}, u32[]{:S(2)}, u32[]{:S(2)}) %collective-permute-start.6) | collective-permute-done | bytes 278560 | tf_op jit(solution)/shard_map/ppermute | solution.py:583
  21.0 2.0 %collective-permute-done.3.refs_3_ = bf16[256,512]{1,0:T(8,128)(2,1)S(1)} collective-permute-done((bf16[256,512]{1,0:T(8,128)(2,1)}, bf16[256,512]{1,0:T(8,128)(2,1)S(1)}, u32[]{:S(2)}, u32[]{:S(2)}) %collective-permute-start.3) | collective-permute-done | bytes 262176 | tf_op jit(solution)/shard_map/ppermute | solution.py:580
  22.9 1.6 %collective-permute-done.4.refs_5_ = bf16[256,512]{1,0:T(8,128)(2,1)S(1)} collective-permute-done((bf16[256,512]{1,0:T(8,128)(2,1)}, bf16[256,512]{1,0:T(8,128)(2,1)S(1)}, u32[]{:S(2)}, u32[]{:S(2)}) %collective-permute-start.4) | collective-permute-done | bytes 262176 | tf_op jit(solution)/shard_map/ppermute | solution.py:583
  28.0 2.6 %collective-permute-done.10.refs_8_.refs_4_ = bf16[272,512]{1,0:T(8,128)(2,1)S(1)} collective-permute-done((bf16[272,512]{1,0:T(8,128)(2,1)S(1)}, bf16[272,512]{1,0:T(8,128)(2,1)S(1)}, u32[]{:S(2)}, u32[]{:S(2)}) %collective-permute-start.10) | collective-permute-done | bytes 278560 | tf_op jit(solution)/shard_map/ppermute | solution.py:583
  30.5 1.6 %collective-permute-start.13 = (bf16[272,512]{1,0:T(8,128)(2,1)S(1)}, bf16[272,512]{1,0:T(8,128)(2,1)S(1)}, u32[]{:S(2)}, u32[]{:S(2)}) collective-permute-start(bf16[272,512]{1,0:T(8,128)(2,1)S(1)} %collective-permute-done.9.refs_6_.refs_3_), channel_id=1, source_target_pairs={{0,4},{4,8},{8,12},{12,14},{14,10},{10,6},{6,2},{2,0},{1,5},{5,9},... | collective-permute-start | bytes 835592 | tf_op jit(solution)/shard_map/ppermute | solution.py:580
  32.6 2.1 %collective-permute-done.7.refs_7_ = bf16[256,512]{1,0:T(8,128)(2,1)S(1)} collective-permute-done((bf16[256,512]{1,0:T(8,128)(2,1)S(1)}, bf16[256,512]{1,0:T(8,128)(2,1)S(1)}, u32[]{:S(2)}, u32[]{:S(2)}) %collective-permute-start.7) | collective-permute-done | bytes 262176 | tf_op jit(solution)/shard_map/ppermute | solution.py:580
  38.2 1.9 %shard_map.152 = (f32[192,512]{1,0:T(8,128)S(1)}, f32[256,512]{1,0:T(8,128)S(1)}) custom-call(s32[256]{0:T(256)S(1)} %copy-done.7, s32[1]{0:T(128)} %bitcast.1.base_ref, bf16[272,512]{1,0:T(8,128)(2,1)S(1)} %copy-done.2, bf16[256,512]{1,0:T(8,128)(2,1)S(1)} %copy-done.3, bf16[272,512]{1,0:T(8,128)(2,1)S(1)} %collective-permute-done.5.refs_2_.refs_1_, ...), custom_call_target="tpu_custom_call" | custom-call | flops 1 | bytes 1 | tf_op jit(solution)/shard_map/pallas_call | solution.py:28
  43.7 2.5 %collective-permute-done.11.refs_2_.refs_11_ = bf16[256,512]{1,0:T(8,128)(2,1)S(1)} collective-permute-done((bf16[256,512]{1,0:T(8,128)(2,1)S(1)}, bf16[256,512]{1,0:T(8,128)(2,1)S(1)}, u32[]{:S(2)}, u32[]{:S(2)}) %collective-permute-start.11) | collective-permute-done | bytes 262176 | tf_op jit(solution)/shard_map/ppermute | solution.py:580
  48.2 2.7 %collective-permute-done.15.refs_5_.refs_14_.refs_7_ = bf16[272,512]{1,0:T(8,128)(2,1)S(1)} collective-permute-done((bf16[272,512]{1,0:T(8,128)(2,1)S(1)}, bf16[272,512]{1,0:T(8,128)(2,1)S(1)}, u32[]{:S(2)}, u32[]{:S(2)}) %collective-permute-start.15) | collective-permute-done | bytes 278560 | tf_op jit(solution)/shard_map/ppermute | solution.py:580
  50.9 2.1 %collective-permute-done.16.refs_6_.refs_15_ = bf16[256,512]{1,0:T(8,128)(2,1)S(1)} collective-permute-done((bf16[256,512]{1,0:T(8,128)(2,1)S(1)}, bf16[256,512]{1,0:T(8,128)(2,1)S(1)}, u32[]{:S(2)}, u32[]{:S(2)}) %collective-permute-start.16) | collective-permute-done | bytes 262176 | tf_op jit(solution)/shard_map/ppermute | solution.py:583
  57.2 1.9 %shard_map.155 = bf16[256,512]{1,0:T(8,128)(2,1)S(1)} custom-call(s32[1]{0:T(128)} %bitcast.group_ref, s32[1]{0:T(128)} %bitcast.2.half_ref, s32[256]{0:T(256)S(1)} %copy-done.7, s32[1]{0:T(128)} %bitcast.1.base_ref, bf16[256,2048]{1,0:T(8,128)(2,1)S(1)} %slice.8.near_ref, bf16[256,2048]{1,0:T(8,128)(2,1)S(1)} %collective-permute-done.17.far_ref, ...), custom_call_target="tpu_custom_call" | custom-call | flops 1 | bytes 1 | tf_op jit(solution)/shard_map/pallas_call | solution.py:605
  61.0 1.6 %shard_map.156 = bf16[192,512]{1,0:T(8,128)(2,1)S(1)} custom-call(s32[1]{0:T(128)} %bitcast.group_ref, s32[1]{0:T(128)} %bitcast.2.half_ref, s32[256]{0:T(256)S(1)} %copy-done.7, s32[1]{0:T(128)} %bitcast.1.base_ref, bf16[192,2048]{1,0:T(8,128)(2,1)S(1)} %slice.9.near_ref, bf16[192,2048]{1,0:T(8,128)(2,1)S(1)} %collective-permute-done.20.far_ref, ...), custom_call_target="tpu_custom_call" | custom-call | flops 1 | bytes 1 | tf_op jit(solution)/shard_map/pallas_call | solution.py:605
  62.7 3.6 %collective-permute-done.19.other_ref = bf16[256,512]{1,0:T(8,128)(2,1)S(1)} collective-permute-done((bf16[256,512]{1,0:T(8,128)(2,1)S(1)}, bf16[256,512]{1,0:T(8,128)(2,1)S(1)}, u32[]{:S(2)}, u32[]{:S(2)}) %collective-permute-start.19) | collective-permute-done | bytes 262176 | tf_op jit(solution)/shard_map/ppermute | solution.py:586
  67.2 5.3 %all-to-all-start = ((bf16[8,32,640]{2,1,0:T(8,128)(2,1)}), bf16[8,32,640]{2,1,0:T(8,128)(2,1)S(1)}, u32[]{:S(2)}, u32[]{:S(2)}) async-start(bf16[8,32,640]{2,1,0:T(8,128)(2,1)} %shard_map.158), calls=%async_computation | async-start | bytes 655360 | tf_op jit(solution)/shard_map/all_to_all | solution.py:540
  74.1 4.2 %collective-permute-done.21.refs_0_ = bf16[192,512]{1,0:T(8,128)(2,1)S(1)} collective-permute-done((bf16[192,512]{1,0:T(8,128)(2,1)S(1)}, bf16[192,512]{1,0:T(8,128)(2,1)S(1)}, u32[]{:S(2)}, u32[]{:S(2)}) %collective-permute-start.21) | collective-permute-done | bytes 196640 | tf_op jit(solution)/shard_map/ppermute | solution.py:586
  78.2 3.0 %all-to-all-done.refs_1_.partial_ref = bf16[8,32,640]{2,1,0:T(8,128)(2,1)S(1)} async-done(((bf16[8,32,640]{2,1,0:T(8,128)(2,1)}), bf16[8,32,640]{2,1,0:T(8,128)(2,1)S(1)}, u32[]{:S(2)}, u32[]{:S(2)}) %all-to-all-start) | async-done | bytes 327712 | tf_op jit(solution)/shard_map/all_to_all | solution.py:540
  82.4 3.4 %all-to-all-start.1 = ((bf16[8,32,512]{2,1,0:T(8,128)(2,1)}), bf16[8,32,512]{2,1,0:T(8,128)(2,1)S(1)}, u32[]{:S(2)}, u32[]{:S(2)}) async-start(bf16[8,32,512]{2,1,0:T(8,128)(2,1)} %bitcast.9), calls=%async_computation.1 | async-start | bytes 524288 | tf_op jit(solution)/shard_map/all_to_all | solution.py:540
  87.8 6.2 %all-to-all-done.1 = bf16[8,32,512]{2,1,0:T(8,128)(2,1)S(1)} async-done(((bf16[8,32,512]{2,1,0:T(8,128)(2,1)}), bf16[8,32,512]{2,1,0:T(8,128)(2,1)S(1)}, u32[]{:S(2)}, u32[]{:S(2)}) %all-to-all-start.1) | async-done | bytes 262176 | tf_op jit(solution)/shard_map/all_to_all | solution.py:540
  (65 shorter events, 27.5 us)
Async XLA Ops:
  0.6 9.0 %collective-permute-start.1 = (bf16[256,4096]{1,0:T(8,128)(2,1)}, bf16[256,4096]{1,0:T(8,128)(2,1)S(1)}, u32[]{:S(2)}, u32[]{:S(2)}) collective-permute-start(bf16[256,4096]{1,0:T(8,128)(2,1)} %near_hbm.3), channel_id=1, source_target_pairs={{0,1},{1,0},{2,3},{3,2},{4,5},{5,4},{6,7},{7,6},{8,9},{9,8},{10,11... | collective-permute-start | bytes 6291464 | tf_op jit(solution)/shard_map/ppermute | solution.py:536
  1.1 8.4 %collective-permute-start.2 = (bf16[256,4096]{1,0:T(8,128)(2,1)}, bf16[256,4096]{1,0:T(8,128)(2,1)}, u32[]{:S(2)}, u32[]{:S(2)}) collective-permute-start(bf16[256,4096]{1,0:T(8,128)(2,1)} %near_hbm.2), channel_id=1, source_target_pairs={{0,1},{1,0},{2,3},{3,2},{4,5},{5,4},{6,7},{7,6},{8,9},{9,8},{10,11... | collective-permute-start | bytes 6291464 | tf_op jit(solution)/shard_map/ppermute | solution.py:536
  4.6 43.5 %collective-permute-start = (bf16[448,2048]{1,0:T(8,128)(2,1)}, bf16[448,2048]{1,0:T(8,128)(2,1)S(1)}, u32[]{:S(2)}, u32[]{:S(2)}) collective-permute-start(bf16[448,2048]{1,0:T(8,128)(2,1)} %get-tuple-element.60), channel_id=1, source_target_pairs={{0,16},{16,0},{1,17},{17,1},{2,18},{18,2},{3,19},{19,3},{4,20},{20... | collective-permute-start | bytes 5505032 | tf_op jit(solution)/shard_map/ppermute | solution.py:586
  7.6 9.8 %collective-permute-start.5 = (bf16[272,512]{1,0:T(8,128)(2,1)}, bf16[272,512]{1,0:T(8,128)(2,1)S(1)}, u32[]{:S(2)}, u32[]{:S(2)}) collective-permute-start(bf16[272,512]{1,0:T(8,128)(2,1)} %get-tuple-element.63.refs_0_), channel_id=1, source_target_pairs={{0,4},{4,8},{8,12},{12,14},{14,10},{10,6},{6,2},{2,0},{1,5},{5,9},... | collective-permute-start | bytes 835592 | tf_op jit(solution)/shard_map/ppermute | solution.py:580
  9.1 9.8 %collective-permute-start.6 = (bf16[272,512]{1,0:T(8,128)(2,1)}, bf16[272,512]{1,0:T(8,128)(2,1)S(1)}, u32[]{:S(2)}, u32[]{:S(2)}) collective-permute-start(bf16[272,512]{1,0:T(8,128)(2,1)} %get-tuple-element.63.refs_0_), channel_id=1, source_target_pairs={{4,0},{8,4},{12,8},{14,12},{10,14},{6,10},{2,6},{0,2},{5,1},{9,5},... | collective-permute-start | bytes 835592 | tf_op jit(solution)/shard_map/ppermute | solution.py:583
  9.6 13.3 %collective-permute-start.3 = (bf16[256,512]{1,0:T(8,128)(2,1)}, bf16[256,512]{1,0:T(8,128)(2,1)S(1)}, u32[]{:S(2)}, u32[]{:S(2)}) collective-permute-start(bf16[256,512]{1,0:T(8,128)(2,1)} %get-tuple-element.62.refs_1_), channel_id=1, source_target_pairs={{0,4},{4,8},{8,12},{12,14},{14,10},{10,6},{6,2},{2,0},{1,5},{5,9},... | collective-permute-start | bytes 786440 | tf_op jit(solution)/shard_map/ppermute | solution.py:580
  11.2 13.3 %collective-permute-start.4 = (bf16[256,512]{1,0:T(8,128)(2,1)}, bf16[256,512]{1,0:T(8,128)(2,1)S(1)}, u32[]{:S(2)}, u32[]{:S(2)}) collective-permute-start(bf16[256,512]{1,0:T(8,128)(2,1)} %get-tuple-element.62.refs_1_), channel_id=1, source_target_pairs={{4,0},{8,4},{12,8},{14,12},{10,14},{6,10},{2,6},{0,2},{5,1},{9,5},... | collective-permute-start | bytes 786440 | tf_op jit(solution)/shard_map/ppermute | solution.py:583
  18.9 11.6 %collective-permute-start.10 = (bf16[272,512]{1,0:T(8,128)(2,1)S(1)}, bf16[272,512]{1,0:T(8,128)(2,1)S(1)}, u32[]{:S(2)}, u32[]{:S(2)}) collective-permute-start(bf16[272,512]{1,0:T(8,128)(2,1)S(1)} %collective-permute-done.6.refs_4_.refs_2_), channel_id=1, source_target_pairs={{4,0},{8,4},{12,8},{14,12},{10,14},{6,10},{2,6},{0,2},{5,1},{9,5},... | collective-permute-start | bytes 835592 | tf_op jit(solution)/shard_map/ppermute | solution.py:583
  19.4 11.1 %collective-permute-start.9 = (bf16[272,512]{1,0:T(8,128)(2,1)S(1)}, bf16[272,512]{1,0:T(8,128)(2,1)S(1)}, u32[]{:S(2)}, u32[]{:S(2)}) collective-permute-start(bf16[272,512]{1,0:T(8,128)(2,1)S(1)} %collective-permute-done.5.refs_2_.refs_1_), channel_id=1, source_target_pairs={{0,4},{4,8},{8,12},{12,14},{14,10},{10,6},{6,2},{2,0},{1,5},{5,9},... | collective-permute-start | bytes 835592 | tf_op jit(solution)/shard_map/ppermute | solution.py:580
  24.6 10.1 %collective-permute-start.7 = (bf16[256,512]{1,0:T(8,128)(2,1)S(1)}, bf16[256,512]{1,0:T(8,128)(2,1)S(1)}, u32[]{:S(2)}, u32[]{:S(2)}) collective-permute-start(bf16[256,512]{1,0:T(8,128)(2,1)S(1)} %collective-permute-done.3.refs_3_), channel_id=1, source_target_pairs={{0,4},{4,8},{8,12},{12,14},{14,10},{10,6},{6,2},{2,0},{1,5},{5,9},... | collective-permute-start | bytes 786440 | tf_op jit(solution)/shard_map/ppermute | solution.py:580
  26.1 10.0 %collective-permute-start.8 = (bf16[256,512]{1,0:T(8,128)(2,1)S(1)}, bf16[256,512]{1,0:T(8,128)(2,1)S(1)}, u32[]{:S(2)}, u32[]{:S(2)}) collective-permute-start(bf16[256,512]{1,0:T(8,128)(2,1)S(1)} %collective-permute-done.4.refs_5_), channel_id=1, source_target_pairs={{4,0},{8,4},{12,8},{14,12},{10,14},{6,10},{2,6},{0,2},{5,1},{9,5},... | collective-permute-start | bytes 786440 | tf_op jit(solution)/shard_map/ppermute | solution.py:583
  30.5 10.1 %collective-permute-start.13 = (bf16[272,512]{1,0:T(8,128)(2,1)S(1)}, bf16[272,512]{1,0:T(8,128)(2,1)S(1)}, u32[]{:S(2)}, u32[]{:S(2)}) collective-permute-start(bf16[272,512]{1,0:T(8,128)(2,1)S(1)} %collective-permute-done.9.refs_6_.refs_3_), channel_id=1, source_target_pairs={{0,4},{4,8},{8,12},{12,14},{14,10},{10,6},{6,2},{2,0},{1,5},{5,9},... | collective-permute-start | bytes 835592 | tf_op jit(solution)/shard_map/ppermute | solution.py:580
  32.1 10.0 %collective-permute-start.14 = (bf16[272,512]{1,0:T(8,128)(2,1)S(1)}, bf16[272,512]{1,0:T(8,128)(2,1)S(1)}, u32[]{:S(2)}, u32[]{:S(2)}) collective-permute-start(bf16[272,512]{1,0:T(8,128)(2,1)S(1)} %collective-permute-done.10.refs_8_.refs_4_), channel_id=1, source_target_pairs={{4,0},{8,4},{12,8},{14,12},{10,14},{6,10},{2,6},{0,2},{5,1},{9,5},... | collective-permute-start | bytes 835592 | tf_op jit(solution)/shard_map/ppermute | solution.py:583
  36.1 10.1 %collective-permute-start.11 = (bf16[256,512]{1,0:T(8,128)(2,1)S(1)}, bf16[256,512]{1,0:T(8,128)(2,1)S(1)}, u32[]{:S(2)}, u32[]{:S(2)}) collective-permute-start(bf16[256,512]{1,0:T(8,128)(2,1)S(1)} %collective-permute-done.7.refs_7_), channel_id=1, source_target_pairs={{0,4},{4,8},{8,12},{12,14},{14,10},{10,6},{6,2},{2,0},{1,5},{5,9},... | collective-permute-start | bytes 786440 | tf_op jit(solution)/shard_map/ppermute | solution.py:580
  37.7 8.5 %collective-permute-start.12 = (bf16[256,512]{1,0:T(8,128)(2,1)S(1)}, bf16[256,512]{1,0:T(8,128)(2,1)S(1)}, u32[]{:S(2)}, u32[]{:S(2)}) collective-permute-start(bf16[256,512]{1,0:T(8,128)(2,1)S(1)} %collective-permute-done.8.refs_9_), channel_id=1, source_target_pairs={{4,0},{8,4},{12,8},{14,12},{10,14},{6,10},{2,6},{0,2},{5,1},{9,5},... | collective-permute-start | bytes 786440 | tf_op jit(solution)/shard_map/ppermute | solution.py:583
  42.1 8.8 %collective-permute-start.15 = (bf16[272,512]{1,0:T(8,128)(2,1)S(1)}, bf16[272,512]{1,0:T(8,128)(2,1)S(1)}, u32[]{:S(2)}, u32[]{:S(2)}) collective-permute-start(bf16[272,512]{1,0:T(8,128)(2,1)S(1)} %collective-permute-done.13.refs_1_.refs_10_.refs_5_), channel_id=1, source_target_pairs={{0,4},{4,8},{8,12},{12,14},{14,10},{10,6},{6,2},{2,0},{1,5},{5,9},... | collective-permute-start | bytes 835592 | tf_op jit(solution)/shard_map/ppermute | solution.py:580
  46.2 6.8 %collective-permute-start.16 = (bf16[256,512]{1,0:T(8,128)(2,1)S(1)}, bf16[256,512]{1,0:T(8,128)(2,1)S(1)}, u32[]{:S(2)}, u32[]{:S(2)}) collective-permute-start(bf16[256,512]{1,0:T(8,128)(2,1)S(1)} %collective-permute-done.12.refs_4_.refs_13_), channel_id=1, source_target_pairs={{4,0},{8,4},{12,8},{14,12},{10,14},{6,10},{2,6},{0,2},{5,1},{9,5},... | collective-permute-start | bytes 786440 | tf_op jit(solution)/shard_map/ppermute | solution.py:583
  53.0 4.2 %collective-permute-start.17 = (bf16[256,2048]{1,0:T(8,128)(2,1)S(1)}, bf16[256,2048]{1,0:T(8,128)(2,1)S(1)}, u32[]{:S(2)}, u32[]{:S(2)}) collective-permute-start(bf16[256,2048]{1,0:T(8,128)(2,1)S(1)} %slice.8.near_ref), channel_id=1, source_target_pairs={{0,1},{1,0},{2,3},{3,2},{4,5},{5,4},{6,7},{7,6},{8,9},{9,8},{10,11... | collective-permute-start | bytes 3145736 | tf_op jit(solution)/shard_map/ppermute | solution.py:536
  53.0 8.0 %collective-permute-start.20 = (bf16[192,2048]{1,0:T(8,128)(2,1)S(1)}, bf16[192,2048]{1,0:T(8,128)(2,1)S(1)}, u32[]{:S(2)}, u32[]{:S(2)}) collective-permute-start(bf16[192,2048]{1,0:T(8,128)(2,1)S(1)} %slice.9.near_ref), channel_id=1, source_target_pairs={{0,1},{1,0},{2,3},{3,2},{4,5},{5,4},{6,7},{7,6},{8,9},{9,8},{10,11... | collective-permute-start | bytes 2359304 | tf_op jit(solution)/shard_map/ppermute | solution.py:536
  53.5 3.7 %collective-permute-start.18 = (bf16[16,256]{1,0:T(8,128)(2,1)S(1)}, bf16[16,256]{1,0:T(8,128)(2,1)S(1)}, u32[]{:S(2)}, u32[]{:S(2)}) collective-permute-start(bf16[16,256]{1,0:T(8,128)(2,1)S(1)} %shard_map.153), channel_id=1, source_target_pairs={{0,16},{16,0},{1,17},{17,1},{2,18},{18,2},{3,19},{19,3},{4,20},{20... | collective-permute-start | bytes 24584 | tf_op jit(solution)/shard_map/ppermute | solution.py:586
  59.1 7.1 %collective-permute-start.19 = (bf16[256,512]{1,0:T(8,128)(2,1)S(1)}, bf16[256,512]{1,0:T(8,128)(2,1)S(1)}, u32[]{:S(2)}, u32[]{:S(2)}) collective-permute-start(bf16[256,512]{1,0:T(8,128)(2,1)S(1)} %shard_map.155), channel_id=1, source_target_pairs={{0,16},{16,0},{1,17},{17,1},{2,18},{18,2},{3,19},{19,3},{4,20},{20... | collective-permute-start | bytes 786440 | tf_op jit(solution)/shard_map/ppermute | solution.py:586
  67.2 14.0 %all-to-all-start = ((bf16[8,32,640]{2,1,0:T(8,128)(2,1)}), bf16[8,32,640]{2,1,0:T(8,128)(2,1)S(1)}, u32[]{:S(2)}, u32[]{:S(2)}) async-start(bf16[8,32,640]{2,1,0:T(8,128)(2,1)} %shard_map.158), calls=%async_computation | async-start | bytes 655360 | tf_op jit(solution)/shard_map/all_to_all | solution.py:540
  72.6 5.7 %collective-permute-start.21 = (bf16[192,512]{1,0:T(8,128)(2,1)S(1)}, bf16[192,512]{1,0:T(8,128)(2,1)S(1)}, u32[]{:S(2)}, u32[]{:S(2)}) collective-permute-start(bf16[192,512]{1,0:T(8,128)(2,1)S(1)} %shard_map.156), channel_id=1, source_target_pairs={{0,16},{16,0},{1,17},{17,1},{2,18},{18,2},{3,19},{19,3},{4,20},{20... | collective-permute-start | bytes 589832 | tf_op jit(solution)/shard_map/ppermute | solution.py:586
  82.4 11.6 %all-to-all-start.1 = ((bf16[8,32,512]{2,1,0:T(8,128)(2,1)}), bf16[8,32,512]{2,1,0:T(8,128)(2,1)S(1)}, u32[]{:S(2)}, u32[]{:S(2)}) async-start(bf16[8,32,512]{2,1,0:T(8,128)(2,1)} %bitcast.9), calls=%async_computation.1 | async-start | bytes 524288 | tf_op jit(solution)/shard_map/all_to_all | solution.py:540
  (13 other events, 161.5 us)

commit v6 on v5

--- a/solution.py
+++ b/solution.py
@@ -109,7 +109,7 @@
     image_hbm, text_hbm, out_a, out_b, out_slot, out_block, out_pick, target_ref, owner_ref, query_ref, sems
 ):
     piece_b = out_b.shape[0]
-    piece = out_a.shape[0] - GROUP - sections
+    piece = out_a.shape[0] - GROUP
     at = pl.multiple_of(group_ref[0] * (piece + piece_b), LANES)
     moves = [
         (target_hbm, target_ref),
@@ -143,12 +143,8 @@
     copies[1].wait()
     groups = query_ref.shape[1] // (GROUP * HD)
     told = [query_group(query_ref, h) for h in range(groups)]
-    told.append(jnp.zeros((GROUP, out_a.shape[1] - groups * HD), jnp.float32))
-    told = jnp.concatenate(told, axis=1)
-    positions = jnp.concatenate(
-        [positions, jnp.zeros((sections, out_a.shape[1] - LANES), jnp.float32)], axis=1
-    )
-    out_a[piece:] = jnp.concatenate([told, positions], axis=0).astype(jnp.bfloat16)
+    told += [positions, jnp.zeros((GROUP, out_a.shape[1] - groups * HD - LANES), jnp.float32)]
+    out_a[piece:] = jnp.concatenate(told, axis=1).astype(jnp.bfloat16)
     copies[2].wait()
     out_block[...] = block_slots(owner_ref[...], sections, capr, block_rows)
     for copy in copies[3:]:
@@ -232,7 +228,7 @@
             pltpu.SemaphoreType.DMA((2 + 2 * (rows // tile),)),
         ],
         compiler_params=pltpu.CompilerParams(vmem_limit_bytes=VMEM),
-        cost_estimate=cost(1, 1),
+        cost_estimate=cost(1.2e10, 1),
     )(group, half, near, far, gains)
 
 
@@ -379,8 +375,7 @@
     held, block_rows, _ = pool_ref.shape
     heads = out_ref.shape[1] // 2
     groups = heads // GROUP
-    part = told_refs[0].shape[0] - GROUP - sections
-    told = [ref[part:, :].astype(jnp.float32) for ref in told_refs]
+    told = [ref[ref.shape[0] - GROUP :, :].astype(jnp.float32) for ref in told_refs]
     owner, fill = owner_ref[...], fill_ref[...]
     masks = []
     for j in range(sections):
@@ -409,7 +404,8 @@
     own = iota((sections, LANES), 0) == sources[0]
     sent = jnp.concatenate(
         [
-            jnp.sum(jnp.where(own, t[GROUP:, :LANES], 0.0), axis=0, keepdims=True) for t in told
+            jnp.sum(jnp.where(own, t[:, groups * HD : groups * HD + LANES], 0.0), axis=0, keepdims=True)
+            for t in told
         ],
         axis=0,
     )
@@ -595,7 +591,7 @@
         return call(
             functools.partial(dots_kernel, first, count, len(added)),
             shapes, index, base, *parts, *inputs, *states,
-            smem=(0, 1), cost=cost(1, 1),
+            smem=(0, 1), cost=cost(1.2e10 if count == 5 else 1, 1),
             aliases={2 + len(parts) + len(inputs) + k: k for k in range(len(states))},
         )
 
@@ -616,7 +612,7 @@
     own_a, own_b, image_slot, block_slot, picked = pl.pallas_call(
         functools.partial(open_kernel, sections, cape, capr, pool.shape[1]),
         out_shape=(
-            jax.ShapeDtypeStruct((piece + GROUP + sections, width), jnp.bfloat16),
+            jax.ShapeDtypeStruct((piece + GROUP, width), jnp.bfloat16),
             jax.ShapeDtypeStruct((depth // 2 - piece, width), jnp.bfloat16),
             jax.ShapeDtypeStruct((1, rows), jnp.int32),
             jax.ShapeDtypeStruct((1, block_owner.shape[1] * pool.shape[1]), jnp.int32),
@@ -766,7 +762,7 @@
     block_rows = old_pool.shape[1]
     capr = (block_owner.shape[0] + sections - 1) // sections * block_rows
     ring = (
-        sections == 8
+        sections == GROUP
         and tensors == 2
         and lax.axis_size("groups") == 2
         and kv_weight.shape[0] == 1024

time: 95 us -> 93.7 us (0.986)
  waiting for transfers between devices: 42.5 us -> 39.4 us
  starting transfers between devices: 30 us -> 31.7 us
    ppermute x7, waiting for transfers between devices: 12.6 us -> 5.78 us  [up(): return lax.ppermute(x, 'section', ahead)]
    ppermute x7, waiting for transfers between devices: 11 us -> 13.1 us  [down(): return lax.ppermute(x, 'section', back)]
    ppermute x7, starting transfers between devices: 11.1 us -> 13 us  [up(): return lax.ppermute(x, 'section', ahead)]
    ppermute x4, waiting for transfers between devices: 9.66 us -> 11.2 us  [across(): return lax.ppermute(x, 'groups', [(0, 1), (1, 0)])]
    ppermute x4, starting transfers between devices: 4.95 us -> 6.24 us  [across(): return lax.ppermute(x, 'groups', [(0, 1), (1, 0)])]
    ppermute x7, starting transfers between devices: 4.12 us -> 2.89 us  [down(): return lax.ppermute(x, 'section', back)]
  transfers between devices with their start and end apart: 24 -> 24, of which waited for: 18 -> 17; matrix products, arithmetic and copies ran while one was open for 0% -> 0% of each run, Pallas kernels for 18% -> 18%
where the time goes in v6:
time: 93.7 us; the launch traced here: 93.4 us
  waiting for transfers between devices  39.4 us (42%)
  starting transfers between devices  31.7 us (34%)
  Pallas kernels  19.2 us (20%)
  between operations  2.13 us (2%)
    ppermute x7, waiting for transfers between devices, down(): return lax.ppermute(x, 'section', back)  13.1 us
    ppermute x7, starting transfers between devices, up(): return lax.ppermute(x, 'section', ahead)  13 us
    ppermute x4, waiting for transfers between devices, across(): return lax.ppermute(x, 'groups', [(0, 1), (1, 0)])  11.2 us
    all_to_all x2, waiting for transfers between devices, exchange(): return lax.all_to_all(x, 'section', split_axis=0, concat_axis=0, tiled=True)  9.34 us
    all_to_all x2, starting transfers between devices, exchange(): return lax.all_to_all(x, 'section', split_axis=0, concat_axis=0, tiled=True)  8.42 us
    pallas_call x7, Pallas kernels, call(): pl.pallas_call(kernel, out_shape=outs, in_specs=[pl.BlockSpec(memory_spac...  8.19 us
    ppermute x4, starting transfers between devices, across(): return lax.ppermute(x, 'groups', [(0, 1), (1, 0)])  6.24 us
    ppermute x7, waiting for transfers between devices, up(): return lax.ppermute(x, 'section', ahead)  5.78 us
  transfers between devices with their start and end apart: 24, of which 17 were waited for; matrix products, arithmetic and copies ran while one was open for 0% of the time, Pallas kernels for 18%

profile of v6, /device:TPU:0, one launch (start us, length us, event | category | flops | bytes accessed | tf_op | source)
XLA Modules:
  0.0 93.4 jit_solution(8977720828363738326)
XLA Ops:
  1.2 3.3 %shard_map.149 = (bf16[264,512]{1,0:T(8,128)(2,1)}, bf16[256,512]{1,0:T(8,128)(2,1)}, s32[1,256]{1,0:T(1,128)}, s32[1,256]{1,0:T(1,128)}, bf16[448,2048]{1,0:T(8,128)(2,1)}) custom-call(s32[1]{0:T(128)} %bitcast.group_ref, s32[1]{0:T(128)} %bitcast.1.base_ref, s32[1]{0:T(128)} %bitcast.2.half_ref, bf16[1024,512]{1,0:T(8,128)(2,1)} %weight_hbm.1, ...), custom_call_target="tpu_custom_call" | custom-call | tf_op jit(solution)/shard_map/pallas_call | solution.py:612
  4.5 3.1 %collective-permute-start.5 = (bf16[264,512]{1,0:T(8,128)(2,1)}, bf16[264,512]{1,0:T(8,128)(2,1)S(1)}, u32[]{:S(2)}, u32[]{:S(2)}) collective-permute-start(bf16[264,512]{1,0:T(8,128)(2,1)} %get-tuple-element.63.refs_0_), channel_id=1, source_target_pairs={{0,4},{4,8},{8,12},{12,14},{14,10},{10,6},{6,2},{2,0},{1,5},{5,9},... | collective-permute-start | bytes 811016 | tf_op jit(solution)/shard_map/ppermute | solution.py:576
  7.6 2.0 %collective-permute-start = (bf16[448,2048]{1,0:T(8,128)(2,1)}, bf16[448,2048]{1,0:T(8,128)(2,1)S(1)}, u32[]{:S(2)}, u32[]{:S(2)}) collective-permute-start(bf16[448,2048]{1,0:T(8,128)(2,1)} %get-tuple-element.60), channel_id=1, source_target_pairs={{0,16},{16,0},{1,17},{17,1},{2,18},{18,2},{3,19},{19,3},{4,20},{20... | collective-permute-start | bytes 5505032 | tf_op jit(solution)/shard_map/ppermute | solution.py:582
  9.6 1.6 %collective-permute-start.3 = (bf16[256,512]{1,0:T(8,128)(2,1)}, bf16[256,512]{1,0:T(8,128)(2,1)S(1)}, u32[]{:S(2)}, u32[]{:S(2)}) collective-permute-start(bf16[256,512]{1,0:T(8,128)(2,1)} %get-tuple-element.62.refs_1_), channel_id=1, source_target_pairs={{0,4},{4,8},{8,12},{12,14},{14,10},{10,6},{6,2},{2,0},{1,5},{5,9},... | collective-permute-start | bytes 786440 | tf_op jit(solution)/shard_map/ppermute | solution.py:576
  11.6 2.8 %shard_map.150 = (bf16[8,256,512]{2,1,0:T(8,128)(2,1)S(1)}, f32[1,256]{1,0:T(1,128)S(1)}) custom-call(s32[1]{0:T(128)} %bitcast.group_ref, s32[1]{0:T(128)} %bitcast.2.half_ref, bf16[256,4096]{1,0:T(8,128)(2,1)S(1)} %copy-done.1, bf16[256,4096]{1,0:T(8,128)(2,1)} %collective-permute-done.2.far_hbm, f32[1,8192]{1,0:T(1,128)S(1)} %bitcast.11), custom_call_target="tpu_custom_call" | custom-call | flops 12000000000 | bytes 1 | tf_op jit(solution)/shard_map/pallas_call | solution.py:215
  15.0 2.2 %collective-permute-done.6.refs_4_.refs_2_ = bf16[264,512]{1,0:T(8,128)(2,1)S(1)} collective-permute-done((bf16[264,512]{1,0:T(8,128)(2,1)}, bf16[264,512]{1,0:T(8,128)(2,1)S(1)}, u32[]{:S(2)}, u32[]{:S(2)}) %collective-permute-start.6) | collective-permute-done | bytes 270368 | tf_op jit(solution)/shard_map/ppermute | solution.py:579
  17.2 2.0 %collective-permute-start.9 = (bf16[264,512]{1,0:T(8,128)(2,1)S(1)}, bf16[264,512]{1,0:T(8,128)(2,1)S(1)}, u32[]{:S(2)}, u32[]{:S(2)}) collective-permute-start(bf16[264,512]{1,0:T(8,128)(2,1)S(1)} %collective-permute-done.5.refs_2_.refs_1_), channel_id=1, source_target_pairs={{0,4},{4,8},{8,12},{12,14},{14,10},{10,6},{6,2},{2,0},{1,5},{5,9},... | collective-permute-start | bytes 811016 | tf_op jit(solution)/shard_map/ppermute | solution.py:576
  20.6 2.2 %collective-permute-done.4.refs_5_ = bf16[256,512]{1,0:T(8,128)(2,1)S(1)} collective-permute-done((bf16[256,512]{1,0:T(8,128)(2,1)}, bf16[256,512]{1,0:T(8,128)(2,1)S(1)}, u32[]{:S(2)}, u32[]{:S(2)}) %collective-permute-start.4) | collective-permute-done | bytes 262176 | tf_op jit(solution)/shard_map/ppermute | solution.py:579
  26.2 2.4 %collective-permute-done.10.refs_8_.refs_4_ = bf16[264,512]{1,0:T(8,128)(2,1)S(1)} collective-permute-done((bf16[264,512]{1,0:T(8,128)(2,1)S(1)}, bf16[264,512]{1,0:T(8,128)(2,1)S(1)}, u32[]{:S(2)}, u32[]{:S(2)}) %collective-permute-start.10) | collective-permute-done | bytes 270368 | tf_op jit(solution)/shard_map/ppermute | solution.py:579
  30.6 1.7 %collective-permute-done.7.refs_7_ = bf16[256,512]{1,0:T(8,128)(2,1)S(1)} collective-permute-done((bf16[256,512]{1,0:T(8,128)(2,1)S(1)}, bf16[256,512]{1,0:T(8,128)(2,1)S(1)}, u32[]{:S(2)}, u32[]{:S(2)}) %collective-permute-start.7) | collective-permute-done | bytes 262176 | tf_op jit(solution)/shard_map/ppermute | solution.py:576
  32.3 1.9 %collective-permute-done.8.refs_9_ = bf16[256,512]{1,0:T(8,128)(2,1)S(1)} collective-permute-done((bf16[256,512]{1,0:T(8,128)(2,1)S(1)}, bf16[256,512]{1,0:T(8,128)(2,1)S(1)}, u32[]{:S(2)}, u32[]{:S(2)}) %collective-permute-start.8) | collective-permute-done | bytes 262176 | tf_op jit(solution)/shard_map/ppermute | solution.py:579
  36.3 1.9 %shard_map.152 = (f32[192,512]{1,0:T(8,128)S(1)}, f32[256,512]{1,0:T(8,128)S(1)}) custom-call(s32[256]{0:T(256)S(1)} %copy-done.7, s32[1]{0:T(128)} %bitcast.1.base_ref, bf16[264,512]{1,0:T(8,128)(2,1)S(1)} %copy-done, bf16[256,512]{1,0:T(8,128)(2,1)S(1)} %copy-done.3, bf16[264,512]{1,0:T(8,128)(2,1)S(1)} %collective-permute-done.5.refs_2_.refs_1_, ...), custom_call_target="tpu_custom_call" | custom-call | flops 12000000000 | bytes 1 | tf_op jit(solution)/shard_map/pallas_call | solution.py:28
  38.2 1.8 %collective-permute-done.14.refs_3_.refs_12_.refs_6_ = bf16[264,512]{1,0:T(8,128)(2,1)S(1)} collective-permute-done((bf16[264,512]{1,0:T(8,128)(2,1)S(1)}, bf16[264,512]{1,0:T(8,128)(2,1)S(1)}, u32[]{:S(2)}, u32[]{:S(2)}) %collective-permute-start.14) | collective-permute-done | bytes 270368 | tf_op jit(solution)/shard_map/ppermute | solution.py:579
  41.6 2.1 %collective-permute-done.11.refs_2_.refs_11_ = bf16[256,512]{1,0:T(8,128)(2,1)S(1)} collective-permute-done((bf16[256,512]{1,0:T(8,128)(2,1)S(1)}, bf16[256,512]{1,0:T(8,128)(2,1)S(1)}, u32[]{:S(2)}, u32[]{:S(2)}) %collective-permute-start.11) | collective-permute-done | bytes 262176 | tf_op jit(solution)/shard_map/ppermute | solution.py:576
  45.6 3.9 %collective-permute-done = bf16[448,2048]{1,0:T(8,128)(2,1)S(1)} collective-permute-done((bf16[448,2048]{1,0:T(8,128)(2,1)}, bf16[448,2048]{1,0:T(8,128)(2,1)S(1)}, u32[]{:S(2)}, u32[]{:S(2)}) %collective-permute-start) | collective-permute-done | bytes 1835040 | tf_op jit(solution)/shard_map/ppermute | solution.py:582
  49.7 1.8 %collective-permute-done.16.refs_6_.refs_15_ = bf16[256,512]{1,0:T(8,128)(2,1)S(1)} collective-permute-done((bf16[256,512]{1,0:T(8,128)(2,1)S(1)}, bf16[256,512]{1,0:T(8,128)(2,1)S(1)}, u32[]{:S(2)}, u32[]{:S(2)}) %collective-permute-start.16) | collective-permute-done | bytes 262176 | tf_op jit(solution)/shard_map/ppermute | solution.py:579
  55.8 1.9 %shard_map.155 = bf16[256,512]{1,0:T(8,128)(2,1)S(1)} custom-call(s32[1]{0:T(128)} %bitcast.group_ref, s32[1]{0:T(128)} %bitcast.2.half_ref, s32[256]{0:T(256)S(1)} %copy-done.7, s32[1]{0:T(128)} %bitcast.1.base_ref, bf16[256,2048]{1,0:T(8,128)(2,1)S(1)} %slice.8.near_ref, bf16[256,2048]{1,0:T(8,128)(2,1)S(1)} %collective-permute-done.17.far_ref, ...), custom_call_target="tpu_custom_call" | custom-call | flops 1 | bytes 1 | tf_op jit(solution)/shard_map/pallas_call | solution.py:601
  60.6 1.7 %shard_map.156 = bf16[192,512]{1,0:T(8,128)(2,1)S(1)} custom-call(s32[1]{0:T(128)} %bitcast.group_ref, s32[1]{0:T(128)} %bitcast.2.half_ref, s32[256]{0:T(256)S(1)} %copy-done.7, s32[1]{0:T(128)} %bitcast.1.base_ref, bf16[192,2048]{1,0:T(8,128)(2,1)S(1)} %slice.9.near_ref, bf16[192,2048]{1,0:T(8,128)(2,1)S(1)} %collective-permute-done.20.far_ref, ...), custom_call_target="tpu_custom_call" | custom-call | flops 1 | bytes 1 | tf_op jit(solution)/shard_map/pallas_call | solution.py:601
  62.3 2.9 %collective-permute-done.19.other_ref = bf16[256,512]{1,0:T(8,128)(2,1)S(1)} collective-permute-done((bf16[256,512]{1,0:T(8,128)(2,1)S(1)}, bf16[256,512]{1,0:T(8,128)(2,1)S(1)}, u32[]{:S(2)}, u32[]{:S(2)}) %collective-permute-start.19) | collective-permute-done | bytes 262176 | tf_op jit(solution)/shard_map/ppermute | solution.py:582
  66.1 4.8 %all-to-all-start = ((bf16[8,32,640]{2,1,0:T(8,128)(2,1)}), bf16[8,32,640]{2,1,0:T(8,128)(2,1)S(1)}, u32[]{:S(2)}, u32[]{:S(2)}) async-start(bf16[8,32,640]{2,1,0:T(8,128)(2,1)} %shard_map.158), calls=%async_computation | async-start | bytes 655360 | tf_op jit(solution)/shard_map/all_to_all | solution.py:536
  72.8 3.9 %collective-permute-done.21.refs_0_ = bf16[192,512]{1,0:T(8,128)(2,1)S(1)} collective-permute-done((bf16[192,512]{1,0:T(8,128)(2,1)S(1)}, bf16[192,512]{1,0:T(8,128)(2,1)S(1)}, u32[]{:S(2)}, u32[]{:S(2)}) %collective-permute-start.21) | collective-permute-done | bytes 196640 | tf_op jit(solution)/shard_map/ppermute | solution.py:582
  76.6 3.1 %all-to-all-done.refs_1_.partial_ref = bf16[8,32,640]{2,1,0:T(8,128)(2,1)S(1)} async-done(((bf16[8,32,640]{2,1,0:T(8,128)(2,1)}), bf16[8,32,640]{2,1,0:T(8,128)(2,1)S(1)}, u32[]{:S(2)}, u32[]{:S(2)}) %all-to-all-start) | async-done | bytes 327712 | tf_op jit(solution)/shard_map/all_to_all | solution.py:536
  80.9 3.6 %all-to-all-start.1 = ((bf16[8,32,512]{2,1,0:T(8,128)(2,1)}), bf16[8,32,512]{2,1,0:T(8,128)(2,1)S(1)}, u32[]{:S(2)}, u32[]{:S(2)}) async-start(bf16[8,32,512]{2,1,0:T(8,128)(2,1)} %bitcast.9), calls=%async_computation.1 | async-start | bytes 524288 | tf_op jit(solution)/shard_map/all_to_all | solution.py:536
  86.4 6.3 %all-to-all-done.1 = bf16[8,32,512]{2,1,0:T(8,128)(2,1)S(1)} async-done(((bf16[8,32,512]{2,1,0:T(8,128)(2,1)}), bf16[8,32,512]{2,1,0:T(8,128)(2,1)S(1)}, u32[]{:S(2)}, u32[]{:S(2)}) %all-to-all-start.1) | async-done | bytes 262176 | tf_op jit(solution)/shard_map/all_to_all | solution.py:536
  (65 shorter events, 26.5 us)
Async XLA Ops:
  0.6 8.9 %collective-permute-start.1 = (bf16[256,4096]{1,0:T(8,128)(2,1)}, bf16[256,4096]{1,0:T(8,128)(2,1)S(1)}, u32[]{:S(2)}, u32[]{:S(2)}) collective-permute-start(bf16[256,4096]{1,0:T(8,128)(2,1)} %near_hbm.3), channel_id=1, source_target_pairs={{0,1},{1,0},{2,3},{3,2},{4,5},{5,4},{6,7},{7,6},{8,9},{9,8},{10,11... | collective-permute-start | bytes 6291464 | tf_op jit(solution)/shard_map/ppermute | solution.py:532
  1.1 8.4 %collective-permute-start.2 = (bf16[256,4096]{1,0:T(8,128)(2,1)}, bf16[256,4096]{1,0:T(8,128)(2,1)}, u32[]{:S(2)}, u32[]{:S(2)}) collective-permute-start(bf16[256,4096]{1,0:T(8,128)(2,1)} %near_hbm.2), channel_id=1, source_target_pairs={{0,1},{1,0},{2,3},{3,2},{4,5},{5,4},{6,7},{7,6},{8,9},{9,8},{10,11... | collective-permute-start | bytes 6291464 | tf_op jit(solution)/shard_map/ppermute | solution.py:532
  4.5 10.5 %collective-permute-start.5 = (bf16[264,512]{1,0:T(8,128)(2,1)}, bf16[264,512]{1,0:T(8,128)(2,1)S(1)}, u32[]{:S(2)}, u32[]{:S(2)}) collective-permute-start(bf16[264,512]{1,0:T(8,128)(2,1)} %get-tuple-element.63.refs_0_), channel_id=1, source_target_pairs={{0,4},{4,8},{8,12},{12,14},{14,10},{10,6},{6,2},{2,0},{1,5},{5,9},... | collective-permute-start | bytes 811016 | tf_op jit(solution)/shard_map/ppermute | solution.py:576
  7.6 9.6 %collective-permute-start.6 = (bf16[264,512]{1,0:T(8,128)(2,1)}, bf16[264,512]{1,0:T(8,128)(2,1)S(1)}, u32[]{:S(2)}, u32[]{:S(2)}) collective-permute-start(bf16[264,512]{1,0:T(8,128)(2,1)} %get-tuple-element.63.refs_0_), channel_id=1, source_target_pairs={{4,0},{8,4},{12,8},{14,12},{10,14},{6,10},{2,6},{0,2},{5,1},{9,5},... | collective-permute-start | bytes 811016 | tf_op jit(solution)/shard_map/ppermute | solution.py:579
  7.6 41.9 %collective-permute-start = (bf16[448,2048]{1,0:T(8,128)(2,1)}, bf16[448,2048]{1,0:T(8,128)(2,1)S(1)}, u32[]{:S(2)}, u32[]{:S(2)}) collective-permute-start(bf16[448,2048]{1,0:T(8,128)(2,1)} %get-tuple-element.60), channel_id=1, source_target_pairs={{0,16},{16,0},{1,17},{17,1},{2,18},{18,2},{3,19},{19,3},{4,20},{20... | collective-permute-start | bytes 5505032 | tf_op jit(solution)/shard_map/ppermute | solution.py:582
  9.6 11.0 %collective-permute-start.3 = (bf16[256,512]{1,0:T(8,128)(2,1)}, bf16[256,512]{1,0:T(8,128)(2,1)S(1)}, u32[]{:S(2)}, u32[]{:S(2)}) collective-permute-start(bf16[256,512]{1,0:T(8,128)(2,1)} %get-tuple-element.62.refs_1_), channel_id=1, source_target_pairs={{0,4},{4,8},{8,12},{12,14},{14,10},{10,6},{6,2},{2,0},{1,5},{5,9},... | collective-permute-start | bytes 786440 | tf_op jit(solution)/shard_map/ppermute | solution.py:576
  11.2 11.6 %collective-permute-start.4 = (bf16[256,512]{1,0:T(8,128)(2,1)}, bf16[256,512]{1,0:T(8,128)(2,1)S(1)}, u32[]{:S(2)}, u32[]{:S(2)}) collective-permute-start(bf16[256,512]{1,0:T(8,128)(2,1)} %get-tuple-element.62.refs_1_), channel_id=1, source_target_pairs={{4,0},{8,4},{12,8},{14,12},{10,14},{6,10},{2,6},{0,2},{5,1},{9,5},... | collective-permute-start | bytes 786440 | tf_op jit(solution)/shard_map/ppermute | solution.py:579
  17.2 11.4 %collective-permute-start.10 = (bf16[264,512]{1,0:T(8,128)(2,1)S(1)}, bf16[264,512]{1,0:T(8,128)(2,1)S(1)}, u32[]{:S(2)}, u32[]{:S(2)}) collective-permute-start(bf16[264,512]{1,0:T(8,128)(2,1)S(1)} %collective-permute-done.6.refs_4_.refs_2_), channel_id=1, source_target_pairs={{4,0},{8,4},{12,8},{14,12},{10,14},{6,10},{2,6},{0,2},{5,1},{9,5},... | collective-permute-start | bytes 811016 | tf_op jit(solution)/shard_map/ppermute | solution.py:579
  17.2 11.4 %collective-permute-start.9 = (bf16[264,512]{1,0:T(8,128)(2,1)S(1)}, bf16[264,512]{1,0:T(8,128)(2,1)S(1)}, u32[]{:S(2)}, u32[]{:S(2)}) collective-permute-start(bf16[264,512]{1,0:T(8,128)(2,1)S(1)} %collective-permute-done.5.refs_2_.refs_1_), channel_id=1, source_target_pairs={{0,4},{4,8},{8,12},{12,14},{14,10},{10,6},{6,2},{2,0},{1,5},{5,9},... | collective-permute-start | bytes 811016 | tf_op jit(solution)/shard_map/ppermute | solution.py:576
  22.8 9.5 %collective-permute-start.7 = (bf16[256,512]{1,0:T(8,128)(2,1)S(1)}, bf16[256,512]{1,0:T(8,128)(2,1)S(1)}, u32[]{:S(2)}, u32[]{:S(2)}) collective-permute-start(bf16[256,512]{1,0:T(8,128)(2,1)S(1)} %collective-permute-done.3.refs_3_), channel_id=1, source_target_pairs={{0,4},{4,8},{8,12},{12,14},{14,10},{10,6},{6,2},{2,0},{1,5},{5,9},... | collective-permute-start | bytes 786440 | tf_op jit(solution)/shard_map/ppermute | solution.py:576
  24.4 9.8 %collective-permute-start.8 = (bf16[256,512]{1,0:T(8,128)(2,1)S(1)}, bf16[256,512]{1,0:T(8,128)(2,1)S(1)}, u32[]{:S(2)}, u32[]{:S(2)}) collective-permute-start(bf16[256,512]{1,0:T(8,128)(2,1)S(1)} %collective-permute-done.4.refs_5_), channel_id=1, source_target_pairs={{4,0},{8,4},{12,8},{14,12},{10,14},{6,10},{2,6},{0,2},{5,1},{9,5},... | collective-permute-start | bytes 786440 | tf_op jit(solution)/shard_map/ppermute | solution.py:579
  28.6 9.6 %collective-permute-start.13 = (bf16[264,512]{1,0:T(8,128)(2,1)S(1)}, bf16[264,512]{1,0:T(8,128)(2,1)S(1)}, u32[]{:S(2)}, u32[]{:S(2)}) collective-permute-start(bf16[264,512]{1,0:T(8,128)(2,1)S(1)} %collective-permute-done.9.refs_6_.refs_3_), channel_id=1, source_target_pairs={{0,4},{4,8},{8,12},{12,14},{14,10},{10,6},{6,2},{2,0},{1,5},{5,9},... | collective-permute-start | bytes 811016 | tf_op jit(solution)/shard_map/ppermute | solution.py:576
  30.2 9.8 %collective-permute-start.14 = (bf16[264,512]{1,0:T(8,128)(2,1)S(1)}, bf16[264,512]{1,0:T(8,128)(2,1)S(1)}, u32[]{:S(2)}, u32[]{:S(2)}) collective-permute-start(bf16[264,512]{1,0:T(8,128)(2,1)S(1)} %collective-permute-done.10.refs_8_.refs_4_), channel_id=1, source_target_pairs={{4,0},{8,4},{12,8},{14,12},{10,14},{6,10},{2,6},{0,2},{5,1},{9,5},... | collective-permute-start | bytes 811016 | tf_op jit(solution)/shard_map/ppermute | solution.py:579
  34.2 9.5 %collective-permute-start.11 = (bf16[256,512]{1,0:T(8,128)(2,1)S(1)}, bf16[256,512]{1,0:T(8,128)(2,1)S(1)}, u32[]{:S(2)}, u32[]{:S(2)}) collective-permute-start(bf16[256,512]{1,0:T(8,128)(2,1)S(1)} %collective-permute-done.7.refs_7_), channel_id=1, source_target_pairs={{0,4},{4,8},{8,12},{12,14},{14,10},{10,6},{6,2},{2,0},{1,5},{5,9},... | collective-permute-start | bytes 786440 | tf_op jit(solution)/shard_map/ppermute | solution.py:576
  35.8 8.6 %collective-permute-start.12 = (bf16[256,512]{1,0:T(8,128)(2,1)S(1)}, bf16[256,512]{1,0:T(8,128)(2,1)S(1)}, u32[]{:S(2)}, u32[]{:S(2)}) collective-permute-start(bf16[256,512]{1,0:T(8,128)(2,1)S(1)} %collective-permute-done.8.refs_9_), channel_id=1, source_target_pairs={{4,0},{8,4},{12,8},{14,12},{10,14},{6,10},{2,6},{0,2},{5,1},{9,5},... | collective-permute-start | bytes 786440 | tf_op jit(solution)/shard_map/ppermute | solution.py:579
  40.0 9.7 %collective-permute-start.15 = (bf16[264,512]{1,0:T(8,128)(2,1)S(1)}, bf16[264,512]{1,0:T(8,128)(2,1)S(1)}, u32[]{:S(2)}, u32[]{:S(2)}) collective-permute-start(bf16[264,512]{1,0:T(8,128)(2,1)S(1)} %collective-permute-done.13.refs_1_.refs_10_.refs_5_), channel_id=1, source_target_pairs={{0,4},{4,8},{8,12},{12,14},{14,10},{10,6},{6,2},{2,0},{1,5},{5,9},... | collective-permute-start | bytes 811016 | tf_op jit(solution)/shard_map/ppermute | solution.py:576
  44.4 7.1 %collective-permute-start.16 = (bf16[256,512]{1,0:T(8,128)(2,1)S(1)}, bf16[256,512]{1,0:T(8,128)(2,1)S(1)}, u32[]{:S(2)}, u32[]{:S(2)}) collective-permute-start(bf16[256,512]{1,0:T(8,128)(2,1)S(1)} %collective-permute-done.12.refs_4_.refs_13_), channel_id=1, source_target_pairs={{4,0},{8,4},{12,8},{14,12},{10,14},{6,10},{2,6},{0,2},{5,1},{9,5},... | collective-permute-start | bytes 786440 | tf_op jit(solution)/shard_map/ppermute | solution.py:579
  51.6 4.2 %collective-permute-start.17 = (bf16[256,2048]{1,0:T(8,128)(2,1)S(1)}, bf16[256,2048]{1,0:T(8,128)(2,1)S(1)}, u32[]{:S(2)}, u32[]{:S(2)}) collective-permute-start(bf16[256,2048]{1,0:T(8,128)(2,1)S(1)} %slice.8.near_ref), channel_id=1, source_target_pairs={{0,1},{1,0},{2,3},{3,2},{4,5},{5,4},{6,7},{7,6},{8,9},{9,8},{10,11... | collective-permute-start | bytes 3145736 | tf_op jit(solution)/shard_map/ppermute | solution.py:532
  51.6 9.0 %collective-permute-start.20 = (bf16[192,2048]{1,0:T(8,128)(2,1)S(1)}, bf16[192,2048]{1,0:T(8,128)(2,1)S(1)}, u32[]{:S(2)}, u32[]{:S(2)}) collective-permute-start(bf16[192,2048]{1,0:T(8,128)(2,1)S(1)} %slice.9.near_ref), channel_id=1, source_target_pairs={{0,1},{1,0},{2,3},{3,2},{4,5},{5,4},{6,7},{7,6},{8,9},{9,8},{10,11... | collective-permute-start | bytes 2359304 | tf_op jit(solution)/shard_map/ppermute | solution.py:532
  52.1 3.7 %collective-permute-start.18 = (bf16[16,256]{1,0:T(8,128)(2,1)S(1)}, bf16[16,256]{1,0:T(8,128)(2,1)S(1)}, u32[]{:S(2)}, u32[]{:S(2)}) collective-permute-start(bf16[16,256]{1,0:T(8,128)(2,1)S(1)} %shard_map.153), channel_id=1, source_target_pairs={{0,16},{16,0},{1,17},{17,1},{2,18},{18,2},{3,19},{19,3},{4,20},{20... | collective-permute-start | bytes 24584 | tf_op jit(solution)/shard_map/ppermute | solution.py:582
  57.7 7.5 %collective-permute-start.19 = (bf16[256,512]{1,0:T(8,128)(2,1)S(1)}, bf16[256,512]{1,0:T(8,128)(2,1)S(1)}, u32[]{:S(2)}, u32[]{:S(2)}) collective-permute-start(bf16[256,512]{1,0:T(8,128)(2,1)S(1)} %shard_map.155), channel_id=1, source_target_pairs={{0,16},{16,0},{1,17},{17,1},{2,18},{18,2},{3,19},{19,3},{4,20},{20... | collective-permute-start | bytes 786440 | tf_op jit(solution)/shard_map/ppermute | solution.py:582
  66.1 13.6 %all-to-all-start = ((bf16[8,32,640]{2,1,0:T(8,128)(2,1)}), bf16[8,32,640]{2,1,0:T(8,128)(2,1)S(1)}, u32[]{:S(2)}, u32[]{:S(2)}) async-start(bf16[8,32,640]{2,1,0:T(8,128)(2,1)} %shard_map.158), calls=%async_computation | async-start | bytes 655360 | tf_op jit(solution)/shard_map/all_to_all | solution.py:536
  70.9 5.7 %collective-permute-start.21 = (bf16[192,512]{1,0:T(8,128)(2,1)S(1)}, bf16[192,512]{1,0:T(8,128)(2,1)S(1)}, u32[]{:S(2)}, u32[]{:S(2)}) collective-permute-start(bf16[192,512]{1,0:T(8,128)(2,1)S(1)} %shard_map.156), channel_id=1, source_target_pairs={{0,16},{16,0},{1,17},{17,1},{2,18},{18,2},{3,19},{19,3},{4,20},{20... | collective-permute-start | bytes 589832 | tf_op jit(solution)/shard_map/ppermute | solution.py:582
  80.9 11.8 %all-to-all-start.1 = ((bf16[8,32,512]{2,1,0:T(8,128)(2,1)}), bf16[8,32,512]{2,1,0:T(8,128)(2,1)S(1)}, u32[]{:S(2)}, u32[]{:S(2)}) async-start(bf16[8,32,512]{2,1,0:T(8,128)(2,1)} %bitcast.9), calls=%async_computation.1 | async-start | bytes 524288 | tf_op jit(solution)/shard_map/all_to_all | solution.py:536
  (13 other events, 162.8 us)

commit v7 on v5

--- a/solution.py
+++ b/solution.py
@@ -232,12 +232,12 @@
             pltpu.SemaphoreType.DMA((2 + 2 * (rows // tile),)),
         ],
         compiler_params=pltpu.CompilerParams(vmem_limit_bytes=VMEM),
-        cost_estimate=cost(1, 1),
+        cost_estimate=cost(1.2e10, 1),
     )(group, half, near, far, gains)
 
 
 def other_kernel(
-    first_term, group_ref, half_ref, index_ref, base_ref, near_ref, far_ref, factor_ref, gains_ref, *refs
+    first_term, first, group_ref, half_ref, index_ref, base_ref, near_ref, far_ref, factor_ref, gains_ref, *refs
 ):
     *weights, out_ref = refs
     slices, rows = len(weights) // 2, out_ref.shape[0]
@@ -246,7 +246,7 @@
     factor = terms[first_term : first_term + 1]
     for k in range(1, 3):
         factor = factor + terms[first_term + k : first_term + k + 1]
-    factor = jnp.sum(jnp.where(diagonal(rows), factor[:, :rows], 0.0), axis=1, keepdims=True)
+    factor = jnp.sum(jnp.where(diagonal(rows), factor[:, first : first + rows], 0.0), axis=1, keepdims=True)
     total = 0.0
     for k in range(slices):
         block = index_ref[base_ref[0] + k]
@@ -254,7 +254,8 @@
         side = half_ref[0] + far - 2 * far * half_ref[0]
         lane = (2 * (side * half + block - far * half) + group_ref[0]) * width
         at = pl.ds(pl.multiple_of((block - far * half) * width, LANES), width)
-        value = jnp.where(far > 0, far_ref[:, at], near_ref[:, at]).astype(jnp.float32) * factor
+        at = pl.ds(first, rows), at
+        value = jnp.where(far > 0, far_ref[at], near_ref[at]).astype(jnp.float32) * factor
         value = value * gains_ref[:, pl.ds(pl.multiple_of(lane, LANES), width)]
         value = value.astype(jnp.bfloat16)
         at = 0
@@ -462,10 +463,11 @@
         out[...] = total.astype(out.dtype)
 
 
-def last_image_kernel(image_ref, other_ref, place_ref, partial_ref, send_out):
+def last_image_kernel(image_ref, other_ref, more_ref, place_ref, partial_ref, send_out):
     sections, cape, _ = send_out.shape
     width = image_ref.shape[1]
-    image = image_ref[...] + other_ref[...].astype(jnp.float32)
+    other = [ref[...].astype(jnp.float32) for ref in (other_ref, more_ref)]
+    image = image_ref[...] + jnp.concatenate(other, axis=0)
     send = jnp.dot(place_ref[...], image.astype(jnp.bfloat16), preferred_element_type=jnp.float32)
     send_out[:, :, :width] = send.astype(jnp.bfloat16).reshape(sections, cape, width)
     send_out[:, :, width:] = partial_ref[...]
@@ -595,15 +597,14 @@
         return call(
             functools.partial(dots_kernel, first, count, len(added)),
             shapes, index, base, *parts, *inputs, *states,
-            smem=(0, 1), cost=cost(1, 1),
+            smem=(0, 1), cost=cost(1.2e10 if count == 5 else 1, 1),
             aliases={2 + len(parts) + len(inputs) + k: k for k in range(len(states))},
         )
 
-    def other_rows(first_term, near, far):
-        rows = near.shape[0]
+    def other_rows(first_term, near, far, first, rows):
         parts = [p for pair in slices for p in pair]
         return pl.pallas_call(
-            functools.partial(other_kernel, first_term),
+            functools.partial(other_kernel, first_term, first),
             out_shape=jax.ShapeDtypeStruct((rows, width), jnp.bfloat16),
             in_specs=[pl.BlockSpec(memory_space=pltpu.SMEM)] * 4
             + [pl.BlockSpec(memory_space=pltpu.VMEM)] * (4 + len(parts)),
@@ -683,16 +684,18 @@
     done = 2 * last - 1
     sums = dots(done, sections - done, (normed_text, normed_image), state, jnp.float32, bias)
     (image_far, factors), sums = after((image_far, factors), sums)
-    image_back = across(other_rows(0, other_image, image_far))
-    text_back = other_rows(3, other_text, beside(other_text))
-    (image_back,), (text_back, partial, place) = after(
-        (image_back,), (text_back, partial, place)
+    image_back = [
+        across(other_rows(0, other_image, image_far, at, rows // 2)) for at in (0, rows // 2)
+    ]
+    text_back = other_rows(3, other_text, beside(other_text), 0, text_rows)
+    image_back, (text_back, partial, place) = after(
+        image_back, (text_back, partial, place)
     )
     text_back = across(text_back)
     send = call(
         last_image_kernel,
         jax.ShapeDtypeStruct((sections, cape, width + HD), jnp.bfloat16),
-        sums[1], image_back, place, partial,
+        sums[1], *image_back, place, partial,
     )
     arrived = exchange(send)
     return (sums[0], text_back), arrived, position, block_slot, arrived

time: 95 us -> 94.2 us (level)
  waiting for transfers between devices: 42.5 us -> 38.4 us
  starting transfers between devices: 30 us -> 32.4 us
    ppermute x7, waiting for transfers between devices: 12.6 us -> 6.05 us  [up(): return lax.ppermute(x, 'section', ahead)]
    ppermute x7, waiting for transfers between devices: 11 us -> 13.9 us  [down(): return lax.ppermute(x, 'section', back)]
    ppermute x4 -> x5, starting transfers between devices: 4.95 us -> 6.95 us  [across(): return lax.ppermute(x, 'groups', [(0, 1), (1, 0)])]
    ppermute x7, starting transfers between devices: 11.1 us -> 13 us  [up(): return lax.ppermute(x, 'section', ahead)]
    ppermute x7, starting transfers between devices: 4.12 us -> 2.89 us  [down(): return lax.ppermute(x, 'section', back)]
    pallas_call x2 -> x3, Pallas kernels: 3.51 us -> 4.4 us  [other_rows(): pl.pallas_call(functools.partial(other_kernel, first_term, first), out_sh...]
    ppermute x4 -> x5, waiting for transfers between devices: 9.66 us -> 9.14 us  [across(): return lax.ppermute(x, 'groups', [(0, 1), (1, 0)])]
  transfers between devices with their start and end apart: 24 -> 25, of which waited for: 18 -> 18; matrix products, arithmetic and copies ran while one was open for 0% -> 0% of each run, Pallas kernels for 18% -> 19%
where the time goes in v7:
time: 94.2 us; the launch traced here: 93.9 us
  waiting for transfers between devices  38.4 us (41%)
  starting transfers between devices  32.4 us (34%)
  Pallas kernels  20 us (21%)
  between operations  2.15 us (2%)
    ppermute x7, waiting for transfers between devices, down(): return lax.ppermute(x, 'section', back)  13.9 us
    ppermute x7, starting transfers between devices, up(): return lax.ppermute(x, 'section', ahead)  13 us
    all_to_all x2, waiting for transfers between devices, exchange(): return lax.all_to_all(x, 'section', split_axis=0, concat_axis=0, tiled=True)  9.32 us
    ppermute x5, waiting for transfers between devices, across(): return lax.ppermute(x, 'groups', [(0, 1), (1, 0)])  9.14 us
    all_to_all x2, starting transfers between devices, exchange(): return lax.all_to_all(x, 'section', split_axis=0, concat_axis=0, tiled=True)  8.41 us
    pallas_call x7, Pallas kernels, call(): pl.pallas_call(kernel, out_shape=outs, in_specs=[pl.BlockSpec(memory_spac...  8.19 us
    ppermute x5, starting transfers between devices, across(): return lax.ppermute(x, 'groups', [(0, 1), (1, 0)])  6.95 us
    ppermute x7, waiting for transfers between devices, up(): return lax.ppermute(x, 'section', ahead)  6.05 us
  transfers between devices with their start and end apart: 25, of which 18 were waited for; matrix products, arithmetic and copies ran while one was open for 0% of the time, Pallas kernels for 19%

profile of v7, /device:TPU:0, one launch (start us, length us, event | category | flops | bytes accessed | tf_op | source)
XLA Modules:
  0.0 93.9 jit_solution(1750671336200590830)
XLA Ops:
  1.2 3.3 %shard_map.149 = (bf16[272,512]{1,0:T(8,128)(2,1)}, bf16[256,512]{1,0:T(8,128)(2,1)}, s32[1,256]{1,0:T(1,128)}, s32[1,256]{1,0:T(1,128)}, bf16[448,2048]{1,0:T(8,128)(2,1)}) custom-call(s32[1]{0:T(128)} %bitcast.group_ref, s32[1]{0:T(128)} %bitcast.1.base_ref, s32[1]{0:T(128)} %bitcast.2.half_ref, bf16[1024,512]{1,0:T(8,128)(2,1)} %weight_hbm.1, ...), custom_call_target="tpu_custom_call" | custom-call | tf_op jit(solution)/shard_map/pallas_call | solution.py:617
  4.5 3.1 %collective-permute-start.5 = (bf16[272,512]{1,0:T(8,128)(2,1)}, bf16[272,512]{1,0:T(8,128)(2,1)S(1)}, u32[]{:S(2)}, u32[]{:S(2)}) collective-permute-start(bf16[272,512]{1,0:T(8,128)(2,1)} %get-tuple-element.64.refs_0_), channel_id=1, source_target_pairs={{0,4},{4,8},{8,12},{12,14},{14,10},{10,6},{6,2},{2,0},{1,5},{5,9},... | collective-permute-start | bytes 835592 | tf_op jit(solution)/shard_map/ppermute | solution.py:582
  7.6 2.0 %collective-permute-start = (bf16[448,2048]{1,0:T(8,128)(2,1)}, bf16[448,2048]{1,0:T(8,128)(2,1)S(1)}, u32[]{:S(2)}, u32[]{:S(2)}) collective-permute-start(bf16[448,2048]{1,0:T(8,128)(2,1)} %get-tuple-element.61), channel_id=1, source_target_pairs={{0,16},{16,0},{1,17},{17,1},{2,18},{18,2},{3,19},{19,3},{4,20},{20... | collective-permute-start | bytes 5505032 | tf_op jit(solution)/shard_map/ppermute | solution.py:588
  9.6 1.6 %collective-permute-start.3 = (bf16[256,512]{1,0:T(8,128)(2,1)}, bf16[256,512]{1,0:T(8,128)(2,1)S(1)}, u32[]{:S(2)}, u32[]{:S(2)}) collective-permute-start(bf16[256,512]{1,0:T(8,128)(2,1)} %get-tuple-element.63.refs_1_), channel_id=1, source_target_pairs={{0,4},{4,8},{8,12},{12,14},{14,10},{10,6},{6,2},{2,0},{1,5},{5,9},... | collective-permute-start | bytes 786440 | tf_op jit(solution)/shard_map/ppermute | solution.py:582
  11.6 2.8 %shard_map.150 = (bf16[8,256,512]{2,1,0:T(8,128)(2,1)S(1)}, f32[1,256]{1,0:T(1,128)S(1)}) custom-call(s32[1]{0:T(128)} %bitcast.group_ref, s32[1]{0:T(128)} %bitcast.2.half_ref, bf16[256,4096]{1,0:T(8,128)(2,1)S(1)} %copy-done.2, bf16[256,4096]{1,0:T(8,128)(2,1)} %collective-permute-done.2.far_hbm, f32[1,8192]{1,0:T(1,128)S(1)} %bitcast.11), custom_call_target="tpu_custom_call" | custom-call | flops 12000000000 | bytes 1 | tf_op jit(solution)/shard_map/pallas_call | solution.py:219
  15.2 2.2 %collective-permute-done.6.refs_4_.refs_2_ = bf16[272,512]{1,0:T(8,128)(2,1)S(1)} collective-permute-done((bf16[272,512]{1,0:T(8,128)(2,1)}, bf16[272,512]{1,0:T(8,128)(2,1)S(1)}, u32[]{:S(2)}, u32[]{:S(2)}) %collective-permute-start.6) | collective-permute-done | bytes 278560 | tf_op jit(solution)/shard_map/ppermute | solution.py:585
  17.4 2.0 %collective-permute-start.9 = (bf16[272,512]{1,0:T(8,128)(2,1)S(1)}, bf16[272,512]{1,0:T(8,128)(2,1)S(1)}, u32[]{:S(2)}, u32[]{:S(2)}) collective-permute-start(bf16[272,512]{1,0:T(8,128)(2,1)S(1)} %collective-permute-done.5.refs_2_.refs_1_), channel_id=1, source_target_pairs={{0,4},{4,8},{8,12},{12,14},{14,10},{10,6},{6,2},{2,0},{1,5},{5,9},... | collective-permute-start | bytes 835592 | tf_op jit(solution)/shard_map/ppermute | solution.py:582
  20.8 2.2 %collective-permute-done.4.refs_5_ = bf16[256,512]{1,0:T(8,128)(2,1)S(1)} collective-permute-done((bf16[256,512]{1,0:T(8,128)(2,1)}, bf16[256,512]{1,0:T(8,128)(2,1)S(1)}, u32[]{:S(2)}, u32[]{:S(2)}) %collective-permute-start.4) | collective-permute-done | bytes 262176 | tf_op jit(solution)/shard_map/ppermute | solution.py:585
  26.4 2.6 %collective-permute-done.10.refs_8_.refs_4_ = bf16[272,512]{1,0:T(8,128)(2,1)S(1)} collective-permute-done((bf16[272,512]{1,0:T(8,128)(2,1)S(1)}, bf16[272,512]{1,0:T(8,128)(2,1)S(1)}, u32[]{:S(2)}, u32[]{:S(2)}) %collective-permute-start.10) | collective-permute-done | bytes 278560 | tf_op jit(solution)/shard_map/ppermute | solution.py:585
  29.0 1.6 %collective-permute-start.13 = (bf16[272,512]{1,0:T(8,128)(2,1)S(1)}, bf16[272,512]{1,0:T(8,128)(2,1)S(1)}, u32[]{:S(2)}, u32[]{:S(2)}) collective-permute-start(bf16[272,512]{1,0:T(8,128)(2,1)S(1)} %collective-permute-done.9.refs_6_.refs_3_), channel_id=1, source_target_pairs={{0,4},{4,8},{8,12},{12,14},{14,10},{10,6},{6,2},{2,0},{1,5},{5,9},... | collective-permute-start | bytes 835592 | tf_op jit(solution)/shard_map/ppermute | solution.py:582
  31.0 1.7 %collective-permute-done.7.refs_7_ = bf16[256,512]{1,0:T(8,128)(2,1)S(1)} collective-permute-done((bf16[256,512]{1,0:T(8,128)(2,1)S(1)}, bf16[256,512]{1,0:T(8,128)(2,1)S(1)}, u32[]{:S(2)}, u32[]{:S(2)}) %collective-permute-start.7) | collective-permute-done | bytes 262176 | tf_op jit(solution)/shard_map/ppermute | solution.py:582
  32.6 1.9 %collective-permute-done.8.refs_9_ = bf16[256,512]{1,0:T(8,128)(2,1)S(1)} collective-permute-done((bf16[256,512]{1,0:T(8,128)(2,1)S(1)}, bf16[256,512]{1,0:T(8,128)(2,1)S(1)}, u32[]{:S(2)}, u32[]{:S(2)}) %collective-permute-start.8) | collective-permute-done | bytes 262176 | tf_op jit(solution)/shard_map/ppermute | solution.py:585
  36.6 1.9 %shard_map.152 = (f32[192,512]{1,0:T(8,128)S(1)}, f32[256,512]{1,0:T(8,128)S(1)}) custom-call(s32[256]{0:T(256)S(1)} %copy-done.7, s32[1]{0:T(128)} %bitcast.1.base_ref, bf16[272,512]{1,0:T(8,128)(2,1)S(1)} %copy-done, bf16[256,512]{1,0:T(8,128)(2,1)S(1)} %copy-done.1, bf16[272,512]{1,0:T(8,128)(2,1)S(1)} %collective-permute-done.5.refs_2_.refs_1_, ...), custom_call_target="tpu_custom_call" | custom-call | flops 12000000000 | bytes 1 | tf_op jit(solution)/shard_map/pallas_call | solution.py:28
  38.6 1.9 %collective-permute-done.14.refs_3_.refs_12_.refs_6_ = bf16[272,512]{1,0:T(8,128)(2,1)S(1)} collective-permute-done((bf16[272,512]{1,0:T(8,128)(2,1)S(1)}, bf16[272,512]{1,0:T(8,128)(2,1)S(1)}, u32[]{:S(2)}, u32[]{:S(2)}) %collective-permute-start.14) | collective-permute-done | bytes 278560 | tf_op jit(solution)/shard_map/ppermute | solution.py:585
  42.1 2.1 %collective-permute-done.11.refs_2_.refs_11_ = bf16[256,512]{1,0:T(8,128)(2,1)S(1)} collective-permute-done((bf16[256,512]{1,0:T(8,128)(2,1)S(1)}, bf16[256,512]{1,0:T(8,128)(2,1)S(1)}, u32[]{:S(2)}, u32[]{:S(2)}) %collective-permute-start.11) | collective-permute-done | bytes 262176 | tf_op jit(solution)/shard_map/ppermute | solution.py:582
  46.1 3.4 %collective-permute-done = bf16[448,2048]{1,0:T(8,128)(2,1)S(1)} collective-permute-done((bf16[448,2048]{1,0:T(8,128)(2,1)}, bf16[448,2048]{1,0:T(8,128)(2,1)S(1)}, u32[]{:S(2)}, u32[]{:S(2)}) %collective-permute-start) | collective-permute-done | bytes 1835040 | tf_op jit(solution)/shard_map/ppermute | solution.py:588
  49.7 2.4 %collective-permute-done.16.refs_6_.refs_15_ = bf16[256,512]{1,0:T(8,128)(2,1)S(1)} collective-permute-done((bf16[256,512]{1,0:T(8,128)(2,1)S(1)}, bf16[256,512]{1,0:T(8,128)(2,1)S(1)}, u32[]{:S(2)}, u32[]{:S(2)}) %collective-permute-start.16) | collective-permute-done | bytes 262176 | tf_op jit(solution)/shard_map/ppermute | solution.py:585
  57.7 1.6 %collective-permute-start.20 = (bf16[128,512]{1,0:T(8,128)(2,1)S(1)}, bf16[128,512]{1,0:T(8,128)(2,1)S(1)}, u32[]{:S(2)}, u32[]{:S(2)}) collective-permute-start(bf16[128,512]{1,0:T(8,128)(2,1)S(1)} %shard_map.156), channel_id=1, source_target_pairs={{0,16},{16,0},{1,17},{17,1},{2,18},{18,2},{3,19},{19,3},{4,20},{20... | collective-permute-start | bytes 393224 | tf_op jit(solution)/shard_map/ppermute | solution.py:588
  62.6 1.7 %shard_map.157 = bf16[192,512]{1,0:T(8,128)(2,1)S(1)} custom-call(s32[1]{0:T(128)} %bitcast.group_ref, s32[1]{0:T(128)} %bitcast.2.half_ref, s32[256]{0:T(256)S(1)} %copy-done.7, s32[1]{0:T(128)} %bitcast.1.base_ref, bf16[192,2048]{1,0:T(8,128)(2,1)S(1)} %slice.9.near_ref, bf16[192,2048]{1,0:T(8,128)(2,1)S(1)} %collective-permute-done.21.far_ref, ...), custom_call_target="tpu_custom_call" | custom-call | flops 1 | bytes 1 | tf_op jit(solution)/shard_map/pallas_call | solution.py:606
  66.7 4.8 %all-to-all-start = ((bf16[8,32,640]{2,1,0:T(8,128)(2,1)}), bf16[8,32,640]{2,1,0:T(8,128)(2,1)S(1)}, u32[]{:S(2)}, u32[]{:S(2)}) async-start(bf16[8,32,640]{2,1,0:T(8,128)(2,1)} %shard_map.159), calls=%async_computation | async-start | bytes 655360 | tf_op jit(solution)/shard_map/all_to_all | solution.py:542
  73.4 3.7 %collective-permute-done.22.refs_0_ = bf16[192,512]{1,0:T(8,128)(2,1)S(1)} collective-permute-done((bf16[192,512]{1,0:T(8,128)(2,1)S(1)}, bf16[192,512]{1,0:T(8,128)(2,1)S(1)}, u32[]{:S(2)}, u32[]{:S(2)}) %collective-permute-start.22) | collective-permute-done | bytes 196640 | tf_op jit(solution)/shard_map/ppermute | solution.py:588
  77.1 3.1 %all-to-all-done.refs_1_.partial_ref = bf16[8,32,640]{2,1,0:T(8,128)(2,1)S(1)} async-done(((bf16[8,32,640]{2,1,0:T(8,128)(2,1)}), bf16[8,32,640]{2,1,0:T(8,128)(2,1)S(1)}, u32[]{:S(2)}, u32[]{:S(2)}) %all-to-all-start) | async-done | bytes 327712 | tf_op jit(solution)/shard_map/all_to_all | solution.py:542
  81.3 3.6 %all-to-all-start.1 = ((bf16[8,32,512]{2,1,0:T(8,128)(2,1)}), bf16[8,32,512]{2,1,0:T(8,128)(2,1)S(1)}, u32[]{:S(2)}, u32[]{:S(2)}) async-start(bf16[8,32,512]{2,1,0:T(8,128)(2,1)} %bitcast.9), calls=%async_computation.1 | async-start | bytes 524288 | tf_op jit(solution)/shard_map/all_to_all | solution.py:542
  86.9 6.3 %all-to-all-done.1 = bf16[8,32,512]{2,1,0:T(8,128)(2,1)S(1)} async-done(((bf16[8,32,512]{2,1,0:T(8,128)(2,1)}), bf16[8,32,512]{2,1,0:T(8,128)(2,1)S(1)}, u32[]{:S(2)}, u32[]{:S(2)}) %all-to-all-start.1) | async-done | bytes 262176 | tf_op jit(solution)/shard_map/all_to_all | solution.py:542
  (68 shorter events, 28.5 us)
Async XLA Ops:
  0.6 8.9 %collective-permute-start.1 = (bf16[256,4096]{1,0:T(8,128)(2,1)}, bf16[256,4096]{1,0:T(8,128)(2,1)S(1)}, u32[]{:S(2)}, u32[]{:S(2)}) collective-permute-start(bf16[256,4096]{1,0:T(8,128)(2,1)} %near_hbm.3), channel_id=1, source_target_pairs={{0,1},{1,0},{2,3},{3,2},{4,5},{5,4},{6,7},{7,6},{8,9},{9,8},{10,11... | collective-permute-start | bytes 6291464 | tf_op jit(solution)/shard_map/ppermute | solution.py:538
  1.1 8.4 %collective-permute-start.2 = (bf16[256,4096]{1,0:T(8,128)(2,1)}, bf16[256,4096]{1,0:T(8,128)(2,1)}, u32[]{:S(2)}, u32[]{:S(2)}) collective-permute-start(bf16[256,4096]{1,0:T(8,128)(2,1)} %near_hbm.2), channel_id=1, source_target_pairs={{0,1},{1,0},{2,3},{3,2},{4,5},{5,4},{6,7},{7,6},{8,9},{9,8},{10,11... | collective-permute-start | bytes 6291464 | tf_op jit(solution)/shard_map/ppermute | solution.py:538
  4.5 10.6 %collective-permute-start.5 = (bf16[272,512]{1,0:T(8,128)(2,1)}, bf16[272,512]{1,0:T(8,128)(2,1)S(1)}, u32[]{:S(2)}, u32[]{:S(2)}) collective-permute-start(bf16[272,512]{1,0:T(8,128)(2,1)} %get-tuple-element.64.refs_0_), channel_id=1, source_target_pairs={{0,4},{4,8},{8,12},{12,14},{14,10},{10,6},{6,2},{2,0},{1,5},{5,9},... | collective-permute-start | bytes 835592 | tf_op jit(solution)/shard_map/ppermute | solution.py:582
  7.6 9.8 %collective-permute-start.6 = (bf16[272,512]{1,0:T(8,128)(2,1)}, bf16[272,512]{1,0:T(8,128)(2,1)S(1)}, u32[]{:S(2)}, u32[]{:S(2)}) collective-permute-start(bf16[272,512]{1,0:T(8,128)(2,1)} %get-tuple-element.64.refs_0_), channel_id=1, source_target_pairs={{4,0},{8,4},{12,8},{14,12},{10,14},{6,10},{2,6},{0,2},{5,1},{9,5},... | collective-permute-start | bytes 835592 | tf_op jit(solution)/shard_map/ppermute | solution.py:585
  7.6 41.9 %collective-permute-start = (bf16[448,2048]{1,0:T(8,128)(2,1)}, bf16[448,2048]{1,0:T(8,128)(2,1)S(1)}, u32[]{:S(2)}, u32[]{:S(2)}) collective-permute-start(bf16[448,2048]{1,0:T(8,128)(2,1)} %get-tuple-element.61), channel_id=1, source_target_pairs={{0,16},{16,0},{1,17},{17,1},{2,18},{18,2},{3,19},{19,3},{4,20},{20... | collective-permute-start | bytes 5505032 | tf_op jit(solution)/shard_map/ppermute | solution.py:588
  9.6 11.2 %collective-permute-start.3 = (bf16[256,512]{1,0:T(8,128)(2,1)}, bf16[256,512]{1,0:T(8,128)(2,1)S(1)}, u32[]{:S(2)}, u32[]{:S(2)}) collective-permute-start(bf16[256,512]{1,0:T(8,128)(2,1)} %get-tuple-element.63.refs_1_), channel_id=1, source_target_pairs={{0,4},{4,8},{8,12},{12,14},{14,10},{10,6},{6,2},{2,0},{1,5},{5,9},... | collective-permute-start | bytes 786440 | tf_op jit(solution)/shard_map/ppermute | solution.py:582
  11.2 11.8 %collective-permute-start.4 = (bf16[256,512]{1,0:T(8,128)(2,1)}, bf16[256,512]{1,0:T(8,128)(2,1)S(1)}, u32[]{:S(2)}, u32[]{:S(2)}) collective-permute-start(bf16[256,512]{1,0:T(8,128)(2,1)} %get-tuple-element.63.refs_1_), channel_id=1, source_target_pairs={{4,0},{8,4},{12,8},{14,12},{10,14},{6,10},{2,6},{0,2},{5,1},{9,5},... | collective-permute-start | bytes 786440 | tf_op jit(solution)/shard_map/ppermute | solution.py:585
  17.4 11.6 %collective-permute-start.10 = (bf16[272,512]{1,0:T(8,128)(2,1)S(1)}, bf16[272,512]{1,0:T(8,128)(2,1)S(1)}, u32[]{:S(2)}, u32[]{:S(2)}) collective-permute-start(bf16[272,512]{1,0:T(8,128)(2,1)S(1)} %collective-permute-done.6.refs_4_.refs_2_), channel_id=1, source_target_pairs={{4,0},{8,4},{12,8},{14,12},{10,14},{6,10},{2,6},{0,2},{5,1},{9,5},... | collective-permute-start | bytes 835592 | tf_op jit(solution)/shard_map/ppermute | solution.py:585
  17.4 11.6 %collective-permute-start.9 = (bf16[272,512]{1,0:T(8,128)(2,1)S(1)}, bf16[272,512]{1,0:T(8,128)(2,1)S(1)}, u32[]{:S(2)}, u32[]{:S(2)}) collective-permute-start(bf16[272,512]{1,0:T(8,128)(2,1)S(1)} %collective-permute-done.5.refs_2_.refs_1_), channel_id=1, source_target_pairs={{0,4},{4,8},{8,12},{12,14},{14,10},{10,6},{6,2},{2,0},{1,5},{5,9},... | collective-permute-start | bytes 835592 | tf_op jit(solution)/shard_map/ppermute | solution.py:582
  23.0 9.7 %collective-permute-start.7 = (bf16[256,512]{1,0:T(8,128)(2,1)S(1)}, bf16[256,512]{1,0:T(8,128)(2,1)S(1)}, u32[]{:S(2)}, u32[]{:S(2)}) collective-permute-start(bf16[256,512]{1,0:T(8,128)(2,1)S(1)} %collective-permute-done.3.refs_3_), channel_id=1, source_target_pairs={{0,4},{4,8},{8,12},{12,14},{14,10},{10,6},{6,2},{2,0},{1,5},{5,9},... | collective-permute-start | bytes 786440 | tf_op jit(solution)/shard_map/ppermute | solution.py:582
  24.6 10.0 %collective-permute-start.8 = (bf16[256,512]{1,0:T(8,128)(2,1)S(1)}, bf16[256,512]{1,0:T(8,128)(2,1)S(1)}, u32[]{:S(2)}, u32[]{:S(2)}) collective-permute-start(bf16[256,512]{1,0:T(8,128)(2,1)S(1)} %collective-permute-done.4.refs_5_), channel_id=1, source_target_pairs={{4,0},{8,4},{12,8},{14,12},{10,14},{6,10},{2,6},{0,2},{5,1},{9,5},... | collective-permute-start | bytes 786440 | tf_op jit(solution)/shard_map/ppermute | solution.py:585
  29.0 9.7 %collective-permute-start.13 = (bf16[272,512]{1,0:T(8,128)(2,1)S(1)}, bf16[272,512]{1,0:T(8,128)(2,1)S(1)}, u32[]{:S(2)}, u32[]{:S(2)}) collective-permute-start(bf16[272,512]{1,0:T(8,128)(2,1)S(1)} %collective-permute-done.9.refs_6_.refs_3_), channel_id=1, source_target_pairs={{0,4},{4,8},{8,12},{12,14},{14,10},{10,6},{6,2},{2,0},{1,5},{5,9},... | collective-permute-start | bytes 835592 | tf_op jit(solution)/shard_map/ppermute | solution.py:582
  30.5 10.0 %collective-permute-start.14 = (bf16[272,512]{1,0:T(8,128)(2,1)S(1)}, bf16[272,512]{1,0:T(8,128)(2,1)S(1)}, u32[]{:S(2)}, u32[]{:S(2)}) collective-permute-start(bf16[272,512]{1,0:T(8,128)(2,1)S(1)} %collective-permute-done.10.refs_8_.refs_4_), channel_id=1, source_target_pairs={{4,0},{8,4},{12,8},{14,12},{10,14},{6,10},{2,6},{0,2},{5,1},{9,5},... | collective-permute-start | bytes 835592 | tf_op jit(solution)/shard_map/ppermute | solution.py:585
  34.6 9.7 %collective-permute-start.11 = (bf16[256,512]{1,0:T(8,128)(2,1)S(1)}, bf16[256,512]{1,0:T(8,128)(2,1)S(1)}, u32[]{:S(2)}, u32[]{:S(2)}) collective-permute-start(bf16[256,512]{1,0:T(8,128)(2,1)S(1)} %collective-permute-done.7.refs_7_), channel_id=1, source_target_pairs={{0,4},{4,8},{8,12},{12,14},{14,10},{10,6},{6,2},{2,0},{1,5},{5,9},... | collective-permute-start | bytes 786440 | tf_op jit(solution)/shard_map/ppermute | solution.py:582
  36.1 8.8 %collective-permute-start.12 = (bf16[256,512]{1,0:T(8,128)(2,1)S(1)}, bf16[256,512]{1,0:T(8,128)(2,1)S(1)}, u32[]{:S(2)}, u32[]{:S(2)}) collective-permute-start(bf16[256,512]{1,0:T(8,128)(2,1)S(1)} %collective-permute-done.8.refs_9_), channel_id=1, source_target_pairs={{4,0},{8,4},{12,8},{14,12},{10,14},{6,10},{2,6},{0,2},{5,1},{9,5},... | collective-permute-start | bytes 786440 | tf_op jit(solution)/shard_map/ppermute | solution.py:585
  40.5 9.1 %collective-permute-start.15 = (bf16[272,512]{1,0:T(8,128)(2,1)S(1)}, bf16[272,512]{1,0:T(8,128)(2,1)S(1)}, u32[]{:S(2)}, u32[]{:S(2)}) collective-permute-start(bf16[272,512]{1,0:T(8,128)(2,1)S(1)} %collective-permute-done.13.refs_1_.refs_10_.refs_5_), channel_id=1, source_target_pairs={{0,4},{4,8},{8,12},{12,14},{14,10},{10,6},{6,2},{2,0},{1,5},{5,9},... | collective-permute-start | bytes 835592 | tf_op jit(solution)/shard_map/ppermute | solution.py:582
  45.0 7.1 %collective-permute-start.16 = (bf16[256,512]{1,0:T(8,128)(2,1)S(1)}, bf16[256,512]{1,0:T(8,128)(2,1)S(1)}, u32[]{:S(2)}, u32[]{:S(2)}) collective-permute-start(bf16[256,512]{1,0:T(8,128)(2,1)S(1)} %collective-permute-done.12.refs_4_.refs_13_), channel_id=1, source_target_pairs={{4,0},{8,4},{12,8},{14,12},{10,14},{6,10},{2,6},{0,2},{5,1},{9,5},... | collective-permute-start | bytes 786440 | tf_op jit(solution)/shard_map/ppermute | solution.py:585
  52.1 4.2 %collective-permute-start.17 = (bf16[256,2048]{1,0:T(8,128)(2,1)S(1)}, bf16[256,2048]{1,0:T(8,128)(2,1)S(1)}, u32[]{:S(2)}, u32[]{:S(2)}) collective-permute-start(bf16[256,2048]{1,0:T(8,128)(2,1)S(1)} %slice.8.near_ref), channel_id=1, source_target_pairs={{0,1},{1,0},{2,3},{3,2},{4,5},{5,4},{6,7},{7,6},{8,9},{9,8},{10,11... | collective-permute-start | bytes 3145736 | tf_op jit(solution)/shard_map/ppermute | solution.py:538
  52.1 10.4 %collective-permute-start.21 = (bf16[192,2048]{1,0:T(8,128)(2,1)S(1)}, bf16[192,2048]{1,0:T(8,128)(2,1)S(1)}, u32[]{:S(2)}, u32[]{:S(2)}) collective-permute-start(bf16[192,2048]{1,0:T(8,128)(2,1)S(1)} %slice.9.near_ref), channel_id=1, source_target_pairs={{0,1},{1,0},{2,3},{3,2},{4,5},{5,4},{6,7},{7,6},{8,9},{9,8},{10,11... | collective-permute-start | bytes 2359304 | tf_op jit(solution)/shard_map/ppermute | solution.py:538
  57.7 6.5 %collective-permute-start.20 = (bf16[128,512]{1,0:T(8,128)(2,1)S(1)}, bf16[128,512]{1,0:T(8,128)(2,1)S(1)}, u32[]{:S(2)}, u32[]{:S(2)}) collective-permute-start(bf16[128,512]{1,0:T(8,128)(2,1)S(1)} %shard_map.156), channel_id=1, source_target_pairs={{0,16},{16,0},{1,17},{17,1},{2,18},{18,2},{3,19},{19,3},{4,20},{20... | collective-permute-start | bytes 393224 | tf_op jit(solution)/shard_map/ppermute | solution.py:588
  60.7 5.0 %collective-permute-start.19 = (bf16[128,512]{1,0:T(8,128)(2,1)S(1)}, bf16[128,512]{1,0:T(8,128)(2,1)S(1)}, u32[]{:S(2)}, u32[]{:S(2)}) collective-permute-start(bf16[128,512]{1,0:T(8,128)(2,1)S(1)} %shard_map.155), channel_id=1, source_target_pairs={{0,16},{16,0},{1,17},{17,1},{2,18},{18,2},{3,19},{19,3},{4,20},{20... | collective-permute-start | bytes 393224 | tf_op jit(solution)/shard_map/ppermute | solution.py:588
  66.7 13.5 %all-to-all-start = ((bf16[8,32,640]{2,1,0:T(8,128)(2,1)}), bf16[8,32,640]{2,1,0:T(8,128)(2,1)S(1)}, u32[]{:S(2)}, u32[]{:S(2)}) async-start(bf16[8,32,640]{2,1,0:T(8,128)(2,1)} %shard_map.159), calls=%async_computation | async-start | bytes 655360 | tf_op jit(solution)/shard_map/all_to_all | solution.py:542
  71.5 5.7 %collective-permute-start.22 = (bf16[192,512]{1,0:T(8,128)(2,1)S(1)}, bf16[192,512]{1,0:T(8,128)(2,1)S(1)}, u32[]{:S(2)}, u32[]{:S(2)}) collective-permute-start(bf16[192,512]{1,0:T(8,128)(2,1)S(1)} %shard_map.157), channel_id=1, source_target_pairs={{0,16},{16,0},{1,17},{17,1},{2,18},{18,2},{3,19},{19,3},{4,20},{20... | collective-permute-start | bytes 589832 | tf_op jit(solution)/shard_map/ppermute | solution.py:588
  81.3 11.8 %all-to-all-start.1 = ((bf16[8,32,512]{2,1,0:T(8,128)(2,1)}), bf16[8,32,512]{2,1,0:T(8,128)(2,1)S(1)}, u32[]{:S(2)}, u32[]{:S(2)}) async-start(bf16[8,32,512]{2,1,0:T(8,128)(2,1)} %bitcast.9), calls=%async_computation.1 | async-start | bytes 524288 | tf_op jit(solution)/shard_map/all_to_all | solution.py:542
  (14 other events, 164.5 us)
